TPU v7x, 32 devices: a whole 2x2x4 slice. The times are simulated.
32 devices in a mesh: win: 2 (over core), slab: 16 (over z, y, x).
Axes of the slice: x: 2, y: 2, z: 4, core: 2. Of those that a mesh axis runs over, the one named last changes fastest.
Arguments:
- states: float32 [2, 6, 32, 64, 256], P('win', None, 'slab'), may hold values from -6 to 6
- load_shape: bfloat16 [3, 32, 64, 256], P(None, 'slab'), may hold values from -6 to 6
- zone_ids: int32 [32, 64, 256], P('slab'), may hold values from 0 to 7
- zone_shear: float32 [8], replicated, may hold values from 0.3 to 1.2
- zone_lame: float32 [8], replicated, may hold values from 0.3 to 1.5
- amp_table: float32 [16], replicated, may hold values from 0.5 to 2
- cycle_index: int32 [16], replicated, may hold values from 0 to 15, each once
Outputs:
- new_ends: float32 [2, 6, 32, 64, 256], P('win', None, 'slab')
Inputs may be any that keep to these rules, and one draw needn't show every extreme that they name: cycle_index holds each of 0 to 15 once.
All inputs are finite; a program needn't handle non-finite values.
Results may differ from a plain program's by a relative error of at most 0.0003.
Values sent between devices are 32-bit elements; how exact they have to be, the bound alone decides.
No kernel may reach another device: no remote copies, remote signals or barrier semaphores. Data moves between devices by JAX's collectives and lax.ppermute only.
A program may use at most 64 MiB of HBM per device.

v0:
```python
import jax
import jax.numpy as jnp
from jax import lax
from jax.sharding import PartitionSpec as P

FINE = 4
COARSE = 2


DT_FINE = 0.18
DT_COARSE = 0.36
FACE_WEIGHT = 14.0 / 30.0
EDGE_WEIGHT = 3.0 / 30.0
CORNER_WEIGHT = 1.0 / 30.0


def padded_2(block, sides, width):
    for axis, dim in sides:
        count = lax.axis_size(axis)
        forward = [(i, i + 1) for i in range(count - 1)]
        backward = [(target, source) for source, target in forward]
        low = lax.ppermute(
            lax.slice_in_dim(block, block.shape[dim] - width, None, axis=dim), axis, forward
        )
        high = lax.ppermute(lax.slice_in_dim(block, 0, width, axis=dim), axis, backward)
        block = jnp.concatenate([low, block, high], axis=dim)
    return block


def passed_along(block, axis, distance):
    devices = range(lax.axis_size(axis))
    route = [(i - distance, i) for i in devices if i - distance in devices]
    return lax.ppermute(block, axis, route)


def combine(first_vec, second_vec, first_sign, second_sign):
    return tuple((first_sign * first_vec[i] + second_sign * second_vec[i] for i in range(3)))


def acceleration(padded, stiff_shear, stiff_bulk, loading):
    layers = padded.shape[1] - 2
    stripes = padded.shape[2] - 2
    columns = padded.shape[3] - 2

    def shifted_by(offset):
        return padded[
            :,
            1 + offset[0] : 1 + offset[0] + layers,
            1 + offset[1] : 1 + offset[1] + stripes,
            1 + offset[2] : 1 + offset[2] + columns,
        ]

    centre = shifted_by((0, 0, 0))
    laplace = jnp.zeros_like(centre)
    for step_z in (-1, 0, 1):
        for step_y in (-1, 0, 1):
            for step_x in (-1, 0, 1):
                reach = abs(step_z) + abs(step_y) + abs(step_x)
                if reach > 0:
                    weight = (FACE_WEIGHT, EDGE_WEIGHT, CORNER_WEIGHT)[reach - 1]
                    laplace = laplace + weight * (shifted_by((step_z, step_y, step_x)) - centre)
    axis_units = ((0, 0, 1), (0, 1, 0), (1, 0, 0))
    coupled = []
    for component in range(3):
        own_unit = axis_units[component]
        along = (
            shifted_by(own_unit)[component]
            + shifted_by(combine(own_unit, own_unit, -1, 0))[component]
            - 2.0 * centre[component]
        )
        for other in range(3):
            if other != component:
                other_unit = axis_units[other]
                both_up = shifted_by(combine(own_unit, other_unit, 1, 1))[other]
                up_down = shifted_by(combine(own_unit, other_unit, 1, -1))[other]
                down_up = shifted_by(combine(own_unit, other_unit, -1, 1))[other]
                both_down = shifted_by(combine(own_unit, other_unit, -1, -1))[other]
                along = along + 0.25 * (both_up - up_down - down_up + both_down)
        coupled.append(along)
    coupling = jnp.stack(coupled)
    return stiff_shear * laplace + stiff_bulk * coupling + loading


def slab_rim(displaced):
    rimmed = padded_2(displaced, (("slab", 1),), 1)
    return jnp.pad(rimmed, ((0, 0), (0, 0), (1, 1), (1, 1)))


def propagate(status, step_count, time_step, stiff_shear, stiff_bulk, loading, padder):

    def advance(turn_index, current):
        displaced = current[:3]
        velocity = current[3:]
        velocity = velocity + time_step * acceleration(
            padder(displaced), stiff_shear, stiff_bulk, loading
        )
        displaced = displaced + time_step * velocity
        return jnp.concatenate([displaced, velocity], axis=0)

    return lax.fori_loop(0, step_count, advance, status)


def table_pick(table, position):
    return jnp.sum(
        jnp.where(
            jnp.arange(table.shape[0], dtype=jnp.int32) == position, table, jnp.zeros_like(table)
        )
    )


def shards(states, load_shape, zone_ids, zone_shear, zone_lame, amp_table, cycle_index):
    windows = lax.axis_size("win")
    window_index = lax.axis_index("win")
    zone_range = jnp.arange(zone_shear.shape[0], dtype=jnp.int32)
    matches = zone_ids[None] == zone_range[:, None, None, None]
    stiff_shear = jnp.sum(jnp.where(matches, zone_shear[:, None, None, None], 0.0), axis=0)
    lame_first = jnp.sum(jnp.where(matches, zone_lame[:, None, None, None], 0.0), axis=0)
    stiff_bulk = lame_first + stiff_shear
    load_field = load_shape.astype(jnp.float32)
    own_start = states[0]
    loading = table_pick(amp_table, table_pick(cycle_index, window_index)) * load_field
    fine_end = propagate(own_start, FINE, DT_FINE, stiff_shear, stiff_bulk, loading, slab_rim)
    coarse_old = propagate(own_start, COARSE, DT_COARSE, stiff_shear, stiff_bulk, loading, slab_rim)
    correction = fine_end - coarse_old

    def link(turn_index, current):
        advanced = (
            propagate(current, COARSE, DT_COARSE, stiff_shear, stiff_bulk, loading, slab_rim)
            + correction
        )
        received = passed_along(advanced, "win", 1)
        return jnp.where(window_index == 0, own_start, received)

    current = lax.fori_loop(0, windows - 1, link, own_start)
    new_end = (
        propagate(current, COARSE, DT_COARSE, stiff_shear, stiff_bulk, loading, slab_rim)
        + correction
    )
    return new_end[None]


def solution(mesh):
    placed = (
        P("win", None, "slab", None, None),
        P(None, "slab", None, None),
        P("slab", None, None),
        P(),
        P(),
        P(),
        P(),
    )
    return jax.shard_map(
        shards,
        mesh=mesh,
        in_specs=placed,
        out_specs=P("win", None, "slab", None, None),
        check_vma=False,
    )
```

profile of v0, /device:TPU:13, one launch (start us, length us, event | category | flops | bytes accessed | tf_op | source)
XLA Modules:
  0.0 145.7 jit_solution(8642579020506731573)
XLA Ops:
  0.0 1.2 copy.9
  2.1 1.2 fusion.238
  4.2 33.2 %while.47 = (s32[]{:T(128)}, f32[6,2,64,256]{3,2,1,0:T(8,128)S(1)}, f32[2,64,256]{2,1,0:T(8,128)S(1)}, f32[2,64,256]{2,1,0:T(8,128)S(1)}, f32[3,2,64,256]{3,2,1,0:T(8,128)S(1)}, /*index=5*/s32[]{:T(128)}) while((s32[]{:T(128)}, f32[6,2,64,256]{3,2,1,0:T(8,128)S(1)}, f32[2,64,256]{2,1,0:T(8,128)S(1)}, f32[2,64,256]{2,1,0:T(8,128)S(1)}, ...), condition=%wide.region_5.6_spmd, body=%wide.region_4.5_spmd.sunk | while | flops 13354194 | bytes 24410452 | solution.py:100
  4.2 3.1 %collective-permute-start = (f32[3,1,64,256]{3,2,1,0:T(8,128)S(1)}, f32[3,1,64,256]{3,2,1,0:T(8,128)S(1)}, u32[]{:S(2)}, u32[]{:S(2)}) collective-permute-start(f32[3,1,64,256]{3,2,1,0:T(8,128)S(1)} %get-tuple-element.378), channel_id=1, source_target_pairs={{1,0},{2,1},{3,2},{4,3},{5,4},{6,5},{7,6},{8,7},{9,8},{10,9},{11,1... | collective-permute-start | bytes 589832 | tf_op jit(solution)/shard_map/while/body/eval_jaxpr/while/body/eval_jaxpr/ppermute | solution.py:25
  7.3 2.2 %collective-permute-start.1 = (f32[3,1,64,256]{3,2,1,0:T(8,128)S(1)}, f32[3,1,64,256]{3,2,1,0:T(8,128)S(1)}, u32[]{:S(2)}, u32[]{:S(2)}) collective-permute-start(f32[3,1,64,256]{3,2,1,0:T(8,128)S(1)} %get-tuple-element.379), channel_id=1, source_target_pairs={{0,1},{1,2},{2,3},{3,4},{4,5},{5,6},{6,7},{7,8},{8,9},{9,10},{10,1... | collective-permute-start | bytes 589832 | tf_op jit(solution)/shard_map/while/body/eval_jaxpr/while/body/eval_jaxpr/ppermute | solution.py:22
  9.6 2.3 %collective-permute-done = f32[3,1,64,256]{3,2,1,0:T(8,128)S(1)} collective-permute-done((f32[3,1,64,256]{3,2,1,0:T(8,128)S(1)}, f32[3,1,64,256]{3,2,1,0:T(8,128)S(1)}, u32[]{:S(2)}, u32[]{:S(2)}) %collective-permute-start) | collective-permute-done | bytes 196640 | tf_op jit(solution)/shard_map/while/body/eval_jaxpr/while/body/eval_jaxpr/ppermute | solution.py:25
  11.9 4.0 %collective-permute-done.1 = f32[3,1,64,256]{3,2,1,0:T(8,128)S(1)} collective-permute-done((f32[3,1,64,256]{3,2,1,0:T(8,128)S(1)}, f32[3,1,64,256]{3,2,1,0:T(8,128)S(1)}, u32[]{:S(2)}, u32[]{:S(2)}) %collective-permute-start.1) | collective-permute-done | bytes 196640 | tf_op jit(solution)/shard_map/while/body/eval_jaxpr/while/body/eval_jaxpr/ppermute | solution.py:22
  17.2 2.0 %multiply_add_fusion.6 = (f32[3,2,64,256]{3,2,1,0:T(8,128)S(1)}, f32[3,2,64,256]{3,2,1,0:T(8,128)S(1)}) fusion(f32[6,2,64,256]{3,2,1,0:T(8,128)S(1)} %get-tuple-element.407, f32[3,2,64,256]{3,2,1,0:T(8,128)S(1)} %get-tuple-element.416, f32[1,2,64,256]{3,2,1,0:T(8,128)S(1)} %fusion.259, f32[1,2,64,256]{3,2,1,0:T(8,128)S(1)} %fusion.260, ...), kind=kLoop, calls=%fused_computation.99.clone.1 | loop fusion | flops 8749056 | bytes 12845056 | tf_op jit(solution)/shard_map/while/body/eval_jaxpr/while/body/eval_jaxpr/add | solution.py:97
  19.4 6.2 %collective-permute-start = (f32[3,1,64,256]{3,2,1,0:T(8,128)S(1)}, f32[3,1,64,256]{3,2,1,0:T(8,128)S(1)}, u32[]{:S(2)}, u32[]{:S(2)}) collective-permute-start(f32[3,1,64,256]{3,2,1,0:T(8,128)S(1)} %get-tuple-element.378), channel_id=1, source_target_pairs={{1,0},{2,1},{3,2},{4,3},{5,4},{6,5},{7,6},{8,7},{9,8},{10,9},{11,1... | collective-permute-start | bytes 589832 | tf_op jit(solution)/shard_map/while/body/eval_jaxpr/while/body/eval_jaxpr/ppermute | solution.py:25
  25.5 1.9 %collective-permute-start.1 = (f32[3,1,64,256]{3,2,1,0:T(8,128)S(1)}, f32[3,1,64,256]{3,2,1,0:T(8,128)S(1)}, u32[]{:S(2)}, u32[]{:S(2)}) collective-permute-start(f32[3,1,64,256]{3,2,1,0:T(8,128)S(1)} %get-tuple-element.379), channel_id=1, source_target_pairs={{0,1},{1,2},{2,3},{3,4},{4,5},{5,6},{6,7},{7,8},{8,9},{9,10},{10,1... | collective-permute-start | bytes 589832 | tf_op jit(solution)/shard_map/while/body/eval_jaxpr/while/body/eval_jaxpr/ppermute | solution.py:22
  27.5 1.8 %collective-permute-done = f32[3,1,64,256]{3,2,1,0:T(8,128)S(1)} collective-permute-done((f32[3,1,64,256]{3,2,1,0:T(8,128)S(1)}, f32[3,1,64,256]{3,2,1,0:T(8,128)S(1)}, u32[]{:S(2)}, u32[]{:S(2)}) %collective-permute-start) | collective-permute-done | bytes 196640 | tf_op jit(solution)/shard_map/while/body/eval_jaxpr/while/body/eval_jaxpr/ppermute | solution.py:25
  29.3 4.7 %collective-permute-done.1 = f32[3,1,64,256]{3,2,1,0:T(8,128)S(1)} collective-permute-done((f32[3,1,64,256]{3,2,1,0:T(8,128)S(1)}, f32[3,1,64,256]{3,2,1,0:T(8,128)S(1)}, u32[]{:S(2)}, u32[]{:S(2)}) %collective-permute-start.1) | collective-permute-done | bytes 196640 | tf_op jit(solution)/shard_map/while/body/eval_jaxpr/while/body/eval_jaxpr/ppermute | solution.py:22
  35.3 2.0 %multiply_add_fusion.6 = (f32[3,2,64,256]{3,2,1,0:T(8,128)S(1)}, f32[3,2,64,256]{3,2,1,0:T(8,128)S(1)}) fusion(f32[6,2,64,256]{3,2,1,0:T(8,128)S(1)} %get-tuple-element.407, f32[3,2,64,256]{3,2,1,0:T(8,128)S(1)} %get-tuple-element.416, f32[1,2,64,256]{3,2,1,0:T(8,128)S(1)} %fusion.259, f32[1,2,64,256]{3,2,1,0:T(8,128)S(1)} %fusion.260, ...), kind=kLoop, calls=%fused_computation.99.clone.1 | loop fusion | flops 8749056 | bytes 12845056 | tf_op jit(solution)/shard_map/while/body/eval_jaxpr/while/body/eval_jaxpr/add | solution.py:97
  37.4 67.3 %while.48 = (s32[]{:T(128)}, f32[6,2,64,256]{3,2,1,0:T(8,128)S(1)}, f32[2,64,256]{2,1,0:T(8,128)S(1)}, f32[2,64,256]{2,1,0:T(8,128)S(1)}, f32[3,2,64,256]{3,2,1,0:T(8,128)S(1)}, /*index=5*/s32[]{:T(128)}) while((s32[]{:T(128)}, f32[6,2,64,256]{3,2,1,0:T(8,128)S(1)}, f32[2,64,256]{2,1,0:T(8,128)S(1)}, f32[2,64,256]{2,1,0:T(8,128)S(1)}, ...), condition=%wide.region_7.8_spmd, body=%wide.region_6.7_spmd.sunk | while | flops 13354194 | bytes 24410452 | solution.py:100
  37.4 3.4 %collective-permute-start.2 = (f32[3,1,64,256]{3,2,1,0:T(8,128)S(1)}, f32[3,1,64,256]{3,2,1,0:T(8,128)S(1)}, u32[]{:S(2)}, u32[]{:S(2)}) collective-permute-start(f32[3,1,64,256]{3,2,1,0:T(8,128)S(1)} %get-tuple-element.387), channel_id=1, source_target_pairs={{1,0},{2,1},{3,2},{4,3},{5,4},{6,5},{7,6},{8,7},{9,8},{10,9},{11,1... | collective-permute-start | bytes 589832 | tf_op jit(solution)/shard_map/while/body/eval_jaxpr/ppermute | solution.py:25
  40.8 2.2 %collective-permute-start.3 = (f32[3,1,64,256]{3,2,1,0:T(8,128)S(1)}, f32[3,1,64,256]{3,2,1,0:T(8,128)S(1)}, u32[]{:S(2)}, u32[]{:S(2)}) collective-permute-start(f32[3,1,64,256]{3,2,1,0:T(8,128)S(1)} %get-tuple-element.388), channel_id=1, source_target_pairs={{0,1},{1,2},{2,3},{3,4},{4,5},{5,6},{6,7},{7,8},{8,9},{9,10},{10,1... | collective-permute-start | bytes 589832 | tf_op jit(solution)/shard_map/while/body/eval_jaxpr/ppermute | solution.py:22
  43.0 1.6 %collective-permute-done.2 = f32[3,1,64,256]{3,2,1,0:T(8,128)S(1)} collective-permute-done((f32[3,1,64,256]{3,2,1,0:T(8,128)S(1)}, f32[3,1,64,256]{3,2,1,0:T(8,128)S(1)}, u32[]{:S(2)}, u32[]{:S(2)}) %collective-permute-start.2) | collective-permute-done | bytes 196640 | tf_op jit(solution)/shard_map/while/body/eval_jaxpr/ppermute | solution.py:25
  44.6 4.7 %collective-permute-done.3 = f32[3,1,64,256]{3,2,1,0:T(8,128)S(1)} collective-permute-done((f32[3,1,64,256]{3,2,1,0:T(8,128)S(1)}, f32[3,1,64,256]{3,2,1,0:T(8,128)S(1)}, u32[]{:S(2)}, u32[]{:S(2)}) %collective-permute-start.3) | collective-permute-done | bytes 196640 | tf_op jit(solution)/shard_map/while/body/eval_jaxpr/ppermute | solution.py:22
  50.5 2.0 %multiply_add_fusion.7 = (f32[3,2,64,256]{3,2,1,0:T(8,128)S(1)}, f32[3,2,64,256]{3,2,1,0:T(8,128)S(1)}) fusion(f32[6,2,64,256]{3,2,1,0:T(8,128)S(1)} %get-tuple-element.425, f32[3,2,64,256]{3,2,1,0:T(8,128)S(1)} %get-tuple-element.434, f32[1,2,64,256]{3,2,1,0:T(8,128)S(1)} %fusion.263, f32[1,2,64,256]{3,2,1,0:T(8,128)S(1)} %fusion.264, ...), kind=kLoop, calls=%fused_computation.237.clone.1 | loop fusion | flops 8749056 | bytes 12845056 | tf_op jit(solution)/shard_map/while/body/eval_jaxpr/add | solution.py:97
  52.7 6.5 %collective-permute-start.2 = (f32[3,1,64,256]{3,2,1,0:T(8,128)S(1)}, f32[3,1,64,256]{3,2,1,0:T(8,128)S(1)}, u32[]{:S(2)}, u32[]{:S(2)}) collective-permute-start(f32[3,1,64,256]{3,2,1,0:T(8,128)S(1)} %get-tuple-element.387), channel_id=1, source_target_pairs={{1,0},{2,1},{3,2},{4,3},{5,4},{6,5},{7,6},{8,7},{9,8},{10,9},{11,1... | collective-permute-start | bytes 589832 | tf_op jit(solution)/shard_map/while/body/eval_jaxpr/ppermute | solution.py:25
  59.2 1.9 %collective-permute-start.3 = (f32[3,1,64,256]{3,2,1,0:T(8,128)S(1)}, f32[3,1,64,256]{3,2,1,0:T(8,128)S(1)}, u32[]{:S(2)}, u32[]{:S(2)}) collective-permute-start(f32[3,1,64,256]{3,2,1,0:T(8,128)S(1)} %get-tuple-element.388), channel_id=1, source_target_pairs={{0,1},{1,2},{2,3},{3,4},{4,5},{5,6},{6,7},{7,8},{8,9},{9,10},{10,1... | collective-permute-start | bytes 589832 | tf_op jit(solution)/shard_map/while/body/eval_jaxpr/ppermute | solution.py:22
  61.2 1.8 %collective-permute-done.2 = f32[3,1,64,256]{3,2,1,0:T(8,128)S(1)} collective-permute-done((f32[3,1,64,256]{3,2,1,0:T(8,128)S(1)}, f32[3,1,64,256]{3,2,1,0:T(8,128)S(1)}, u32[]{:S(2)}, u32[]{:S(2)}) %collective-permute-start.2) | collective-permute-done | bytes 196640 | tf_op jit(solution)/shard_map/while/body/eval_jaxpr/ppermute | solution.py:25
  63.0 4.7 %collective-permute-done.3 = f32[3,1,64,256]{3,2,1,0:T(8,128)S(1)} collective-permute-done((f32[3,1,64,256]{3,2,1,0:T(8,128)S(1)}, f32[3,1,64,256]{3,2,1,0:T(8,128)S(1)}, u32[]{:S(2)}, u32[]{:S(2)}) %collective-permute-start.3) | collective-permute-done | bytes 196640 | tf_op jit(solution)/shard_map/while/body/eval_jaxpr/ppermute | solution.py:22
  69.0 2.0 %multiply_add_fusion.7 = (f32[3,2,64,256]{3,2,1,0:T(8,128)S(1)}, f32[3,2,64,256]{3,2,1,0:T(8,128)S(1)}) fusion(f32[6,2,64,256]{3,2,1,0:T(8,128)S(1)} %get-tuple-element.425, f32[3,2,64,256]{3,2,1,0:T(8,128)S(1)} %get-tuple-element.434, f32[1,2,64,256]{3,2,1,0:T(8,128)S(1)} %fusion.263, f32[1,2,64,256]{3,2,1,0:T(8,128)S(1)} %fusion.264, ...), kind=kLoop, calls=%fused_computation.237.clone.1 | loop fusion | flops 8749056 | bytes 12845056 | tf_op jit(solution)/shard_map/while/body/eval_jaxpr/add | solution.py:97
  71.1 3.4 %collective-permute-start.2 = (f32[3,1,64,256]{3,2,1,0:T(8,128)S(1)}, f32[3,1,64,256]{3,2,1,0:T(8,128)S(1)}, u32[]{:S(2)}, u32[]{:S(2)}) collective-permute-start(f32[3,1,64,256]{3,2,1,0:T(8,128)S(1)} %get-tuple-element.387), channel_id=1, source_target_pairs={{1,0},{2,1},{3,2},{4,3},{5,4},{6,5},{7,6},{8,7},{9,8},{10,9},{11,1... | collective-permute-start | bytes 589832 | tf_op jit(solution)/shard_map/while/body/eval_jaxpr/ppermute | solution.py:25
  74.5 2.2 %collective-permute-start.3 = (f32[3,1,64,256]{3,2,1,0:T(8,128)S(1)}, f32[3,1,64,256]{3,2,1,0:T(8,128)S(1)}, u32[]{:S(2)}, u32[]{:S(2)}) collective-permute-start(f32[3,1,64,256]{3,2,1,0:T(8,128)S(1)} %get-tuple-element.388), channel_id=1, source_target_pairs={{0,1},{1,2},{2,3},{3,4},{4,5},{5,6},{6,7},{7,8},{8,9},{9,10},{10,1... | collective-permute-start | bytes 589832 | tf_op jit(solution)/shard_map/while/body/eval_jaxpr/ppermute | solution.py:22
  76.7 1.6 %collective-permute-done.2 = f32[3,1,64,256]{3,2,1,0:T(8,128)S(1)} collective-permute-done((f32[3,1,64,256]{3,2,1,0:T(8,128)S(1)}, f32[3,1,64,256]{3,2,1,0:T(8,128)S(1)}, u32[]{:S(2)}, u32[]{:S(2)}) %collective-permute-start.2) | collective-permute-done | bytes 196640 | tf_op jit(solution)/shard_map/while/body/eval_jaxpr/ppermute | solution.py:25
  78.2 4.7 %collective-permute-done.3 = f32[3,1,64,256]{3,2,1,0:T(8,128)S(1)} collective-permute-done((f32[3,1,64,256]{3,2,1,0:T(8,128)S(1)}, f32[3,1,64,256]{3,2,1,0:T(8,128)S(1)}, u32[]{:S(2)}, u32[]{:S(2)}) %collective-permute-start.3) | collective-permute-done | bytes 196640 | tf_op jit(solution)/shard_map/while/body/eval_jaxpr/ppermute | solution.py:22
  84.2 2.0 %multiply_add_fusion.7 = (f32[3,2,64,256]{3,2,1,0:T(8,128)S(1)}, f32[3,2,64,256]{3,2,1,0:T(8,128)S(1)}) fusion(f32[6,2,64,256]{3,2,1,0:T(8,128)S(1)} %get-tuple-element.425, f32[3,2,64,256]{3,2,1,0:T(8,128)S(1)} %get-tuple-element.434, f32[1,2,64,256]{3,2,1,0:T(8,128)S(1)} %fusion.263, f32[1,2,64,256]{3,2,1,0:T(8,128)S(1)} %fusion.264, ...), kind=kLoop, calls=%fused_computation.237.clone.1 | loop fusion | flops 8749056 | bytes 12845056 | tf_op jit(solution)/shard_map/while/body/eval_jaxpr/add | solution.py:97
  86.3 6.5 %collective-permute-start.2 = (f32[3,1,64,256]{3,2,1,0:T(8,128)S(1)}, f32[3,1,64,256]{3,2,1,0:T(8,128)S(1)}, u32[]{:S(2)}, u32[]{:S(2)}) collective-permute-start(f32[3,1,64,256]{3,2,1,0:T(8,128)S(1)} %get-tuple-element.387), channel_id=1, source_target_pairs={{1,0},{2,1},{3,2},{4,3},{5,4},{6,5},{7,6},{8,7},{9,8},{10,9},{11,1... | collective-permute-start | bytes 589832 | tf_op jit(solution)/shard_map/while/body/eval_jaxpr/ppermute | solution.py:25
  92.9 1.9 %collective-permute-start.3 = (f32[3,1,64,256]{3,2,1,0:T(8,128)S(1)}, f32[3,1,64,256]{3,2,1,0:T(8,128)S(1)}, u32[]{:S(2)}, u32[]{:S(2)}) collective-permute-start(f32[3,1,64,256]{3,2,1,0:T(8,128)S(1)} %get-tuple-element.388), channel_id=1, source_target_pairs={{0,1},{1,2},{2,3},{3,4},{4,5},{5,6},{6,7},{7,8},{8,9},{9,10},{10,1... | collective-permute-start | bytes 589832 | tf_op jit(solution)/shard_map/while/body/eval_jaxpr/ppermute | solution.py:22
  94.8 1.8 %collective-permute-done.2 = f32[3,1,64,256]{3,2,1,0:T(8,128)S(1)} collective-permute-done((f32[3,1,64,256]{3,2,1,0:T(8,128)S(1)}, f32[3,1,64,256]{3,2,1,0:T(8,128)S(1)}, u32[]{:S(2)}, u32[]{:S(2)}) %collective-permute-start.2) | collective-permute-done | bytes 196640 | tf_op jit(solution)/shard_map/while/body/eval_jaxpr/ppermute | solution.py:25
  96.6 4.7 %collective-permute-done.3 = f32[3,1,64,256]{3,2,1,0:T(8,128)S(1)} collective-permute-done((f32[3,1,64,256]{3,2,1,0:T(8,128)S(1)}, f32[3,1,64,256]{3,2,1,0:T(8,128)S(1)}, u32[]{:S(2)}, u32[]{:S(2)}) %collective-permute-start.3) | collective-permute-done | bytes 196640 | tf_op jit(solution)/shard_map/while/body/eval_jaxpr/ppermute | solution.py:22
  102.6 2.0 %multiply_add_fusion.7 = (f32[3,2,64,256]{3,2,1,0:T(8,128)S(1)}, f32[3,2,64,256]{3,2,1,0:T(8,128)S(1)}) fusion(f32[6,2,64,256]{3,2,1,0:T(8,128)S(1)} %get-tuple-element.425, f32[3,2,64,256]{3,2,1,0:T(8,128)S(1)} %get-tuple-element.434, f32[1,2,64,256]{3,2,1,0:T(8,128)S(1)} %fusion.263, f32[1,2,64,256]{3,2,1,0:T(8,128)S(1)} %fusion.264, ...), kind=kLoop, calls=%fused_computation.237.clone.1 | loop fusion | flops 8749056 | bytes 12845056 | tf_op jit(solution)/shard_map/while/body/eval_jaxpr/add | solution.py:97
  104.7 1.3 fusion.242
  106.0 1.3 collective-permute-start.6
  107.3 3.6 %collective-permute-done.6 = f32[6,2,64,256]{3,2,1,0:T(8,128)S(1)} collective-permute-done((f32[6,2,64,256]{3,2,1,0:T(8,128)}, f32[6,2,64,256]{3,2,1,0:T(8,128)S(1)}, u32[]{:S(2)}, u32[]{:S(2)}) %collective-permute-start.6) | collective-permute-done | bytes 786464 | tf_op jit(solution)/shard_map/while/body/eval_jaxpr/ppermute | solution.py:33
  111.1 33.6 %while.49 = (s32[]{:T(128)}, f32[6,2,64,256]{3,2,1,0:T(8,128)S(1)}, f32[2,64,256]{2,1,0:T(8,128)S(1)}, f32[2,64,256]{2,1,0:T(8,128)S(1)}, f32[3,2,64,256]{3,2,1,0:T(8,128)S(1)}, /*index=5*/s32[]{:T(128)}) while((s32[]{:T(128)}, f32[6,2,64,256]{3,2,1,0:T(8,128)S(1)}, f32[2,64,256]{2,1,0:T(8,128)S(1)}, f32[2,64,256]{2,1,0:T(8,128)S(1)}, ...), condition=%wide.region_9.10_spmd, body=%wide.region_8.9_spmd.sunk | while | flops 13354194 | bytes 24410452 | solution.py:100
  111.1 3.0 %collective-permute-start.4 = (f32[3,1,64,256]{3,2,1,0:T(8,128)S(1)}, f32[3,1,64,256]{3,2,1,0:T(8,128)S(1)}, u32[]{:S(2)}, u32[]{:S(2)}) collective-permute-start(f32[3,1,64,256]{3,2,1,0:T(8,128)S(1)} %get-tuple-element.396), channel_id=1, source_target_pairs={{1,0},{2,1},{3,2},{4,3},{5,4},{6,5},{7,6},{8,7},{9,8},{10,9},{11,1... | collective-permute-start | bytes 589832 | tf_op jit(solution)/shard_map/while/body/eval_jaxpr/ppermute | solution.py:25
  114.1 2.5 %collective-permute-start.5 = (f32[3,1,64,256]{3,2,1,0:T(8,128)S(1)}, f32[3,1,64,256]{3,2,1,0:T(8,128)S(1)}, u32[]{:S(2)}, u32[]{:S(2)}) collective-permute-start(f32[3,1,64,256]{3,2,1,0:T(8,128)S(1)} %get-tuple-element.397), channel_id=1, source_target_pairs={{0,1},{1,2},{2,3},{3,4},{4,5},{5,6},{6,7},{7,8},{8,9},{9,10},{10,1... | collective-permute-start | bytes 589832 | tf_op jit(solution)/shard_map/while/body/eval_jaxpr/ppermute | solution.py:22
  116.6 2.9 %collective-permute-done.4 = f32[3,1,64,256]{3,2,1,0:T(8,128)S(1)} collective-permute-done((f32[3,1,64,256]{3,2,1,0:T(8,128)S(1)}, f32[3,1,64,256]{3,2,1,0:T(8,128)S(1)}, u32[]{:S(2)}, u32[]{:S(2)}) %collective-permute-start.4) | collective-permute-done | bytes 196640 | tf_op jit(solution)/shard_map/while/body/eval_jaxpr/ppermute | solution.py:25
  119.5 3.4 %collective-permute-done.5 = f32[3,1,64,256]{3,2,1,0:T(8,128)S(1)} collective-permute-done((f32[3,1,64,256]{3,2,1,0:T(8,128)S(1)}, f32[3,1,64,256]{3,2,1,0:T(8,128)S(1)}, u32[]{:S(2)}, u32[]{:S(2)}) %collective-permute-start.5) | collective-permute-done | bytes 196640 | tf_op jit(solution)/shard_map/while/body/eval_jaxpr/ppermute | solution.py:22
  124.2 2.0 %multiply_add_fusion.8 = (f32[3,2,64,256]{3,2,1,0:T(8,128)S(1)}, f32[3,2,64,256]{3,2,1,0:T(8,128)S(1)}) fusion(f32[6,2,64,256]{3,2,1,0:T(8,128)S(1)} %get-tuple-element.443, f32[3,2,64,256]{3,2,1,0:T(8,128)S(1)} %get-tuple-element.452, f32[1,2,64,256]{3,2,1,0:T(8,128)S(1)} %fusion.267, f32[1,2,64,256]{3,2,1,0:T(8,128)S(1)} %fusion.268, ...), kind=kLoop, calls=%fused_computation.375.clone.1 | loop fusion | flops 8749056 | bytes 12845056 | tf_op jit(solution)/shard_map/while/body/eval_jaxpr/add | solution.py:97
  126.3 6.4 %collective-permute-start.4 = (f32[3,1,64,256]{3,2,1,0:T(8,128)S(1)}, f32[3,1,64,256]{3,2,1,0:T(8,128)S(1)}, u32[]{:S(2)}, u32[]{:S(2)}) collective-permute-start(f32[3,1,64,256]{3,2,1,0:T(8,128)S(1)} %get-tuple-element.396), channel_id=1, source_target_pairs={{1,0},{2,1},{3,2},{4,3},{5,4},{6,5},{7,6},{8,7},{9,8},{10,9},{11,1... | collective-permute-start | bytes 589832 | tf_op jit(solution)/shard_map/while/body/eval_jaxpr/ppermute | solution.py:25
  132.8 1.9 %collective-permute-start.5 = (f32[3,1,64,256]{3,2,1,0:T(8,128)S(1)}, f32[3,1,64,256]{3,2,1,0:T(8,128)S(1)}, u32[]{:S(2)}, u32[]{:S(2)}) collective-permute-start(f32[3,1,64,256]{3,2,1,0:T(8,128)S(1)} %get-tuple-element.397), channel_id=1, source_target_pairs={{0,1},{1,2},{2,3},{3,4},{4,5},{5,6},{6,7},{7,8},{8,9},{9,10},{10,1... | collective-permute-start | bytes 589832 | tf_op jit(solution)/shard_map/while/body/eval_jaxpr/ppermute | solution.py:22
  134.7 1.8 %collective-permute-done.4 = f32[3,1,64,256]{3,2,1,0:T(8,128)S(1)} collective-permute-done((f32[3,1,64,256]{3,2,1,0:T(8,128)S(1)}, f32[3,1,64,256]{3,2,1,0:T(8,128)S(1)}, u32[]{:S(2)}, u32[]{:S(2)}) %collective-permute-start.4) | collective-permute-done | bytes 196640 | tf_op jit(solution)/shard_map/while/body/eval_jaxpr/ppermute | solution.py:25
  136.6 4.7 %collective-permute-done.5 = f32[3,1,64,256]{3,2,1,0:T(8,128)S(1)} collective-permute-done((f32[3,1,64,256]{3,2,1,0:T(8,128)S(1)}, f32[3,1,64,256]{3,2,1,0:T(8,128)S(1)}, u32[]{:S(2)}, u32[]{:S(2)}) %collective-permute-start.5) | collective-permute-done | bytes 196640 | tf_op jit(solution)/shard_map/while/body/eval_jaxpr/ppermute | solution.py:22
  142.5 2.0 %multiply_add_fusion.8 = (f32[3,2,64,256]{3,2,1,0:T(8,128)S(1)}, f32[3,2,64,256]{3,2,1,0:T(8,128)S(1)}) fusion(f32[6,2,64,256]{3,2,1,0:T(8,128)S(1)} %get-tuple-element.443, f32[3,2,64,256]{3,2,1,0:T(8,128)S(1)} %get-tuple-element.452, f32[1,2,64,256]{3,2,1,0:T(8,128)S(1)} %fusion.267, f32[1,2,64,256]{3,2,1,0:T(8,128)S(1)} %fusion.268, ...), kind=kLoop, calls=%fused_computation.375.clone.1 | loop fusion | flops 8749056 | bytes 12845056 | tf_op jit(solution)/shard_map/while/body/eval_jaxpr/add | solution.py:97
  (81 shorter events, 14.0 us)
Async XLA Ops:
  0.0 1.4 copy-start
  0.0 1.4 copy-start.7
  0.0 2.1 %copy-start.8 = (f32[16]{0:T(128)S(1)}, f32[16]{0:T(128)}, u32[]{:S(2)}) copy-start(f32[16]{0:T(128)} %param.18) | copy-start | bytes 196
  0.0 3.3 %copy-start.4 = (s32[2,64,256]{2,1,0:T(8,128)S(1)}, s32[2,64,256]{2,1,0:T(8,128)}, u32[]{:S(2)}) copy-start(s32[2,64,256]{2,1,0:T(8,128)} %param.15) | copy-start | bytes 393220
  0.0 3.3 %copy-start.5 = (f32[8]{0:T(128)S(1)}, f32[8]{0:T(128)}, u32[]{:S(2)}) copy-start(f32[8]{0:T(128)} %param.17) | copy-start | bytes 100
  0.0 3.3 %copy-start.6 = (f32[8]{0:T(128)S(1)}, f32[8]{0:T(128)}, u32[]{:S(2)}) copy-start(f32[8]{0:T(128)} %param.16) | copy-start | bytes 100
  1.4 2.2 %copy-start.3 = (bf16[3,2,64,256]{3,2,1,0:T(8,128)(2,1)S(1)}, bf16[3,2,64,256]{3,2,1,0:T(8,128)(2,1)}, u32[]{:S(2)}) copy-start(bf16[3,2,64,256]{3,2,1,0:T(8,128)(2,1)} %param.14) | copy-start | bytes 589828
  4.2 7.7 %collective-permute-start = (f32[3,1,64,256]{3,2,1,0:T(8,128)S(1)}, f32[3,1,64,256]{3,2,1,0:T(8,128)S(1)}, u32[]{:S(2)}, u32[]{:S(2)}) collective-permute-start(f32[3,1,64,256]{3,2,1,0:T(8,128)S(1)} %get-tuple-element.378), channel_id=1, source_target_pairs={{1,0},{2,1},{3,2},{4,3},{5,4},{6,5},{7,6},{8,7},{9,8},{10,9},{11,1... | collective-permute-start | bytes 589832 | tf_op jit(solution)/shard_map/while/body/eval_jaxpr/while/body/eval_jaxpr/ppermute | solution.py:25
  7.3 8.6 %collective-permute-start.1 = (f32[3,1,64,256]{3,2,1,0:T(8,128)S(1)}, f32[3,1,64,256]{3,2,1,0:T(8,128)S(1)}, u32[]{:S(2)}, u32[]{:S(2)}) collective-permute-start(f32[3,1,64,256]{3,2,1,0:T(8,128)S(1)} %get-tuple-element.379), channel_id=1, source_target_pairs={{0,1},{1,2},{2,3},{3,4},{4,5},{5,6},{6,7},{7,8},{8,9},{9,10},{10,1... | collective-permute-start | bytes 589832 | tf_op jit(solution)/shard_map/while/body/eval_jaxpr/while/body/eval_jaxpr/ppermute | solution.py:22
  19.4 9.9 %collective-permute-start = (f32[3,1,64,256]{3,2,1,0:T(8,128)S(1)}, f32[3,1,64,256]{3,2,1,0:T(8,128)S(1)}, u32[]{:S(2)}, u32[]{:S(2)}) collective-permute-start(f32[3,1,64,256]{3,2,1,0:T(8,128)S(1)} %get-tuple-element.378), channel_id=1, source_target_pairs={{1,0},{2,1},{3,2},{4,3},{5,4},{6,5},{7,6},{8,7},{9,8},{10,9},{11,1... | collective-permute-start | bytes 589832 | tf_op jit(solution)/shard_map/while/body/eval_jaxpr/while/body/eval_jaxpr/ppermute | solution.py:25
  25.5 8.4 %collective-permute-start.1 = (f32[3,1,64,256]{3,2,1,0:T(8,128)S(1)}, f32[3,1,64,256]{3,2,1,0:T(8,128)S(1)}, u32[]{:S(2)}, u32[]{:S(2)}) collective-permute-start(f32[3,1,64,256]{3,2,1,0:T(8,128)S(1)} %get-tuple-element.379), channel_id=1, source_target_pairs={{0,1},{1,2},{2,3},{3,4},{4,5},{5,6},{6,7},{7,8},{8,9},{9,10},{10,1... | collective-permute-start | bytes 589832 | tf_op jit(solution)/shard_map/while/body/eval_jaxpr/while/body/eval_jaxpr/ppermute | solution.py:22
  37.4 7.2 %collective-permute-start.2 = (f32[3,1,64,256]{3,2,1,0:T(8,128)S(1)}, f32[3,1,64,256]{3,2,1,0:T(8,128)S(1)}, u32[]{:S(2)}, u32[]{:S(2)}) collective-permute-start(f32[3,1,64,256]{3,2,1,0:T(8,128)S(1)} %get-tuple-element.387), channel_id=1, source_target_pairs={{1,0},{2,1},{3,2},{4,3},{5,4},{6,5},{7,6},{8,7},{9,8},{10,9},{11,1... | collective-permute-start | bytes 589832 | tf_op jit(solution)/shard_map/while/body/eval_jaxpr/ppermute | solution.py:25
  40.8 8.4 %collective-permute-start.3 = (f32[3,1,64,256]{3,2,1,0:T(8,128)S(1)}, f32[3,1,64,256]{3,2,1,0:T(8,128)S(1)}, u32[]{:S(2)}, u32[]{:S(2)}) collective-permute-start(f32[3,1,64,256]{3,2,1,0:T(8,128)S(1)} %get-tuple-element.388), channel_id=1, source_target_pairs={{0,1},{1,2},{2,3},{3,4},{4,5},{5,6},{6,7},{7,8},{8,9},{9,10},{10,1... | collective-permute-start | bytes 589832 | tf_op jit(solution)/shard_map/while/body/eval_jaxpr/ppermute | solution.py:22
  52.7 10.3 %collective-permute-start.2 = (f32[3,1,64,256]{3,2,1,0:T(8,128)S(1)}, f32[3,1,64,256]{3,2,1,0:T(8,128)S(1)}, u32[]{:S(2)}, u32[]{:S(2)}) collective-permute-start(f32[3,1,64,256]{3,2,1,0:T(8,128)S(1)} %get-tuple-element.387), channel_id=1, source_target_pairs={{1,0},{2,1},{3,2},{4,3},{5,4},{6,5},{7,6},{8,7},{9,8},{10,9},{11,1... | collective-permute-start | bytes 589832 | tf_op jit(solution)/shard_map/while/body/eval_jaxpr/ppermute | solution.py:25
  59.2 8.4 %collective-permute-start.3 = (f32[3,1,64,256]{3,2,1,0:T(8,128)S(1)}, f32[3,1,64,256]{3,2,1,0:T(8,128)S(1)}, u32[]{:S(2)}, u32[]{:S(2)}) collective-permute-start(f32[3,1,64,256]{3,2,1,0:T(8,128)S(1)} %get-tuple-element.388), channel_id=1, source_target_pairs={{0,1},{1,2},{2,3},{3,4},{4,5},{5,6},{6,7},{7,8},{8,9},{9,10},{10,1... | collective-permute-start | bytes 589832 | tf_op jit(solution)/shard_map/while/body/eval_jaxpr/ppermute | solution.py:22
  71.1 7.2 %collective-permute-start.2 = (f32[3,1,64,256]{3,2,1,0:T(8,128)S(1)}, f32[3,1,64,256]{3,2,1,0:T(8,128)S(1)}, u32[]{:S(2)}, u32[]{:S(2)}) collective-permute-start(f32[3,1,64,256]{3,2,1,0:T(8,128)S(1)} %get-tuple-element.387), channel_id=1, source_target_pairs={{1,0},{2,1},{3,2},{4,3},{5,4},{6,5},{7,6},{8,7},{9,8},{10,9},{11,1... | collective-permute-start | bytes 589832 | tf_op jit(solution)/shard_map/while/body/eval_jaxpr/ppermute | solution.py:25
  74.5 8.4 %collective-permute-start.3 = (f32[3,1,64,256]{3,2,1,0:T(8,128)S(1)}, f32[3,1,64,256]{3,2,1,0:T(8,128)S(1)}, u32[]{:S(2)}, u32[]{:S(2)}) collective-permute-start(f32[3,1,64,256]{3,2,1,0:T(8,128)S(1)} %get-tuple-element.388), channel_id=1, source_target_pairs={{0,1},{1,2},{2,3},{3,4},{4,5},{5,6},{6,7},{7,8},{8,9},{9,10},{10,1... | collective-permute-start | bytes 589832 | tf_op jit(solution)/shard_map/while/body/eval_jaxpr/ppermute | solution.py:22
  86.3 10.3 %collective-permute-start.2 = (f32[3,1,64,256]{3,2,1,0:T(8,128)S(1)}, f32[3,1,64,256]{3,2,1,0:T(8,128)S(1)}, u32[]{:S(2)}, u32[]{:S(2)}) collective-permute-start(f32[3,1,64,256]{3,2,1,0:T(8,128)S(1)} %get-tuple-element.387), channel_id=1, source_target_pairs={{1,0},{2,1},{3,2},{4,3},{5,4},{6,5},{7,6},{8,7},{9,8},{10,9},{11,1... | collective-permute-start | bytes 589832 | tf_op jit(solution)/shard_map/while/body/eval_jaxpr/ppermute | solution.py:25
  92.9 8.4 %collective-permute-start.3 = (f32[3,1,64,256]{3,2,1,0:T(8,128)S(1)}, f32[3,1,64,256]{3,2,1,0:T(8,128)S(1)}, u32[]{:S(2)}, u32[]{:S(2)}) collective-permute-start(f32[3,1,64,256]{3,2,1,0:T(8,128)S(1)} %get-tuple-element.388), channel_id=1, source_target_pairs={{0,1},{1,2},{2,3},{3,4},{4,5},{5,6},{6,7},{7,8},{8,9},{9,10},{10,1... | collective-permute-start | bytes 589832 | tf_op jit(solution)/shard_map/while/body/eval_jaxpr/ppermute | solution.py:22
  104.7 6.2 %copy-start.1 = (f32[1,6,2,64,256]{4,3,2,1,0:T(8,128)S(1)}, f32[1,6,2,64,256]{4,3,2,1,0:T(8,128)}, u32[]{:S(2)}) copy-start(f32[1,6,2,64,256]{4,3,2,1,0:T(8,128)} %param.13) | copy-start | bytes 2359300
  106.0 4.9 %collective-permute-start.6 = (f32[6,2,64,256]{3,2,1,0:T(8,128)}, f32[6,2,64,256]{3,2,1,0:T(8,128)S(1)}, u32[]{:S(2)}, u32[]{:S(2)}) collective-permute-start(f32[6,2,64,256]{3,2,1,0:T(8,128)} %get-tuple-element.275), channel_id=1, source_target_pairs={{0,16},{1,17},{2,18},{3,19},{4,20},{5,21},{6,22},{7,23},{8,24},{9,... | collective-permute-start | bytes 2359304 | tf_op jit(solution)/shard_map/while/body/eval_jaxpr/ppermute | solution.py:33
  111.1 33.6 %copy-start.2 = (f32[6,2,64,256]{3,2,1,0:T(8,128)S(1)}, f32[6,2,64,256]{3,2,1,0:T(8,128)}, u32[]{:S(2)}) copy-start(f32[6,2,64,256]{3,2,1,0:T(8,128)} %get-tuple-element.276) | copy-start | bytes 2359300
  111.1 8.4 %collective-permute-start.4 = (f32[3,1,64,256]{3,2,1,0:T(8,128)S(1)}, f32[3,1,64,256]{3,2,1,0:T(8,128)S(1)}, u32[]{:S(2)}, u32[]{:S(2)}) collective-permute-start(f32[3,1,64,256]{3,2,1,0:T(8,128)S(1)} %get-tuple-element.396), channel_id=1, source_target_pairs={{1,0},{2,1},{3,2},{4,3},{5,4},{6,5},{7,6},{8,7},{9,8},{10,9},{11,1... | collective-permute-start | bytes 589832 | tf_op jit(solution)/shard_map/while/body/eval_jaxpr/ppermute | solution.py:25
  114.1 8.8 %collective-permute-start.5 = (f32[3,1,64,256]{3,2,1,0:T(8,128)S(1)}, f32[3,1,64,256]{3,2,1,0:T(8,128)S(1)}, u32[]{:S(2)}, u32[]{:S(2)}) collective-permute-start(f32[3,1,64,256]{3,2,1,0:T(8,128)S(1)} %get-tuple-element.397), channel_id=1, source_target_pairs={{0,1},{1,2},{2,3},{3,4},{4,5},{5,6},{6,7},{7,8},{8,9},{9,10},{10,1... | collective-permute-start | bytes 589832 | tf_op jit(solution)/shard_map/while/body/eval_jaxpr/ppermute | solution.py:22
  126.3 10.2 %collective-permute-start.4 = (f32[3,1,64,256]{3,2,1,0:T(8,128)S(1)}, f32[3,1,64,256]{3,2,1,0:T(8,128)S(1)}, u32[]{:S(2)}, u32[]{:S(2)}) collective-permute-start(f32[3,1,64,256]{3,2,1,0:T(8,128)S(1)} %get-tuple-element.396), channel_id=1, source_target_pairs={{1,0},{2,1},{3,2},{4,3},{5,4},{6,5},{7,6},{8,7},{9,8},{10,9},{11,1... | collective-permute-start | bytes 589832 | tf_op jit(solution)/shard_map/while/body/eval_jaxpr/ppermute | solution.py:25
  132.8 8.5 %collective-permute-start.5 = (f32[3,1,64,256]{3,2,1,0:T(8,128)S(1)}, f32[3,1,64,256]{3,2,1,0:T(8,128)S(1)}, u32[]{:S(2)}, u32[]{:S(2)}) collective-permute-start(f32[3,1,64,256]{3,2,1,0:T(8,128)S(1)} %get-tuple-element.397), channel_id=1, source_target_pairs={{0,1},{1,2},{2,3},{3,4},{4,5},{5,6},{6,7},{7,8},{8,9},{9,10},{10,1... | collective-permute-start | bytes 589832 | tf_op jit(solution)/shard_map/while/body/eval_jaxpr/ppermute | solution.py:22
where the time goes:
time: 147 us; the launch traced here: 146 us
  starting transfers between devices  56.4 us (38%)
  waiting for transfers between devices  54.7 us (37%)
  other arithmetic  31.9 us (22%)
  local copies, waits for them, and re-layouts  1.86 us (1%)
    ppermute x8, starting transfers between devices, padded_2(): lax.ppermute(lax.slice_in_dim(block, 0, width, axis=dim), axis, backward)  38.4 us
    ppermute x8, waiting for transfers between devices, padded_2(): lax.ppermute(lax.slice_in_dim(block, block.shape[dim] - width, None, axis...  35.5 us
    ppermute x8, starting transfers between devices, padded_2(): lax.ppermute(lax.slice_in_dim(block, block.shape[dim] - width, None, axis...  16.7 us
    add x8, other arithmetic, advance(): displaced = displaced + time_step * velocity  16 us
    ppermute x8, waiting for transfers between devices, padded_2(): lax.ppermute(lax.slice_in_dim(block, 0, width, axis=dim), axis, backward)  15.6 us
    add x24, other arithmetic, acceleration(): along = along + 0.25 * (both_up - up_down - down_up + both_down)  6.93 us
    ppermute x1, waiting for transfers between devices, passed_along(): return lax.ppermute(block, axis, route)  3.62 us
    concatenate x8, other arithmetic, padded_2(): block = jnp.concatenate([low, block, high], axis=dim)  3.38 us
  transfers between devices with their start and end apart: 17, of which 17 were waited for; matrix products, arithmetic and copies ran while one was open for 0% of the time, Pallas kernels for 0%

commit v1 on v0

--- a/solution.py
+++ b/solution.py
@@ -120,22 +120,20 @@
     own_start = states[0]
     loading = table_pick(amp_table, table_pick(cycle_index, window_index)) * load_field
     fine_end = propagate(own_start, FINE, DT_FINE, stiff_shear, stiff_bulk, loading, slab_rim)
-    coarse_old = propagate(own_start, COARSE, DT_COARSE, stiff_shear, stiff_bulk, loading, slab_rim)
-    correction = fine_end - coarse_old
+    first = window_index == 0
+    silent = jnp.zeros_like(loading)
+
+    def coarse(status):
+        return propagate(status, COARSE, DT_COARSE, stiff_shear, stiff_bulk, silent, slab_rim)
+
+    advanced = coarse(jnp.where(first, fine_end, own_start))
+    correction = fine_end - jnp.where(first, jnp.zeros_like(advanced), advanced)
 
     def link(turn_index, current):
-        advanced = (
-            propagate(current, COARSE, DT_COARSE, stiff_shear, stiff_bulk, loading, slab_rim)
-            + correction
-        )
-        received = passed_along(advanced, "win", 1)
-        return jnp.where(window_index == 0, own_start, received)
+        return coarse(correction + passed_along(current, "win", 1))
 
-    current = lax.fori_loop(0, windows - 1, link, own_start)
-    new_end = (
-        propagate(current, COARSE, DT_COARSE, stiff_shear, stiff_bulk, loading, slab_rim)
-        + correction
-    )
+    advanced = lax.fori_loop(0, windows - 2, link, advanced)
+    new_end = correction + passed_along(advanced, "win", 1)
     return new_end[None]
 
 

time: 147 us -> 112 us (0.76)
  starting transfers between devices: 56.4 us -> 42.8 us
  waiting for transfers between devices: 54.7 us -> 41.7 us
  other arithmetic: 31.9 us -> 24.8 us
    ppermute x8 -> x6, starting transfers between devices: 38.4 us -> 29.2 us  [padded_2(): lax.ppermute(lax.slice_in_dim(block, 0, width, axis=dim), axis, backward)]
    ppermute x8 -> x6, waiting for transfers between devices: 35.5 us -> 27.4 us  [padded_2(): lax.ppermute(lax.slice_in_dim(block, block.shape[dim] - width, None, axis...]
    ppermute x8 -> x6, waiting for transfers between devices: 15.6 us -> 10.8 us  [padded_2(): lax.ppermute(lax.slice_in_dim(block, 0, width, axis=dim), axis, backward)]
    ppermute x8 -> x6, starting transfers between devices: 16.7 us -> 12.4 us  [padded_2(): lax.ppermute(lax.slice_in_dim(block, block.shape[dim] - width, None, axis...]
    add x8 -> x6, other arithmetic: 16 us -> 12 us  [advance(): displaced = displaced + time_step * velocity]
    add x24 -> x18, other arithmetic: 6.93 us -> 5.19 us  [acceleration(): along = along + 0.25 * (both_up - up_down - down_up + both_down)]
    concatenate x8 -> x6, other arithmetic: 3.38 us -> 2.54 us  [padded_2(): block = jnp.concatenate([low, block, high], axis=dim)]
  transfers between devices with their start and end apart: 17 -> 13, of which waited for: 17 -> 13; matrix products, arithmetic and copies ran while one was open for 0% -> 0% of each run, Pallas kernels for 0% -> 0%
where the time goes in v1:
time: 112 us; the launch traced here: 111 us
  starting transfers between devices  42.8 us (38%)
  waiting for transfers between devices  41.7 us (37%)
  other arithmetic  24.8 us (22%)
  local copies, waits for them, and re-layouts  1.49 us (1%)
    ppermute x6, starting transfers between devices, padded_2(): lax.ppermute(lax.slice_in_dim(block, 0, width, axis=dim), axis, backward)  29.2 us
    ppermute x6, waiting for transfers between devices, padded_2(): lax.ppermute(lax.slice_in_dim(block, block.shape[dim] - width, None, axis...  27.4 us
    ppermute x6, starting transfers between devices, padded_2(): lax.ppermute(lax.slice_in_dim(block, block.shape[dim] - width, None, axis...  12.4 us
    add x6, other arithmetic, advance(): displaced = displaced + time_step * velocity  12 us
    ppermute x6, waiting for transfers between devices, padded_2(): lax.ppermute(lax.slice_in_dim(block, 0, width, axis=dim), axis, backward)  10.8 us
    add x18, other arithmetic, acceleration(): along = along + 0.25 * (both_up - up_down - down_up + both_down)  5.19 us
    ppermute x1, waiting for transfers between devices, passed_along(): return lax.ppermute(block, axis, route)  3.42 us
    reduce_sum x2, other arithmetic, table_pick(): jnp.sum(jnp.where(jnp.arange(table.shape[0], dtype=jnp.int32) == position...  2.59 us
  transfers between devices with their start and end apart: 13, of which 13 were waited for; matrix products, arithmetic and copies ran while one was open for 0% of the time, Pallas kernels for 0%

profile of v1, /device:TPU:13, one launch (start us, length us, event | category | flops | bytes accessed | tf_op | source)
XLA Modules:
  0.0 111.3 jit_solution(16247496443749583513)
XLA Ops:
  0.0 1.4 %fusion.157 = s32[]{:T(128)} fusion(s32[16]{0:T(128)} %param.17, s32[]{:T(128)S(6)} %axis_index.15), kind=kLoop, calls=%fused_computation.283 | loop fusion | flops 47 | bytes 72 | tf_op jit(solution)/shard_map/reduce_sum | solution.py:104
  1.4 1.1 %copy.9 = f32[6,2,64,256]{3,2,1,0:T(8,128)S(1)} copy(f32[6,2,64,256]{3,2,1,0:T(8,128)} %bitcast.4) | data formatting | bytes 1572864
  2.5 1.2 %fusion.158 = f32[]{:T(128)} fusion(f32[16]{0:T(128)S(1)} %copy-done.5, s32[]{:T(128)} %fusion.157), kind=kLoop, calls=%fused_computation.284 | loop fusion | flops 47 | bytes 72 | tf_op jit(solution)/shard_map/reduce_sum | solution.py:104
  4.1 0.7 convert_multiply_fusion
  4.8 67.0 %while.24 = (s32[]{:T(128)}, f32[6,2,64,256]{3,2,1,0:T(8,128)S(1)}, f32[2,64,256]{2,1,0:T(8,128)S(1)}, f32[2,64,256]{2,1,0:T(8,128)S(1)}, f32[3,2,64,256]{3,2,1,0:T(8,128)S(1)}, /*index=5*/s32[]{:T(128)}) while((s32[]{:T(128)}, f32[6,2,64,256]{3,2,1,0:T(8,128)S(1)}, f32[2,64,256]{2,1,0:T(8,128)S(1)}, f32[2,64,256]{2,1,0:T(8,128)S(1)}, ...), condition=%wide.region_5.6_spmd, body=%wide.region_4.5_spmd.sunk | while | flops 13354194 | bytes 24410452 | solution.py:100
  4.8 3.2 %collective-permute-start = (f32[3,1,64,256]{3,2,1,0:T(8,128)S(1)}, f32[3,1,64,256]{3,2,1,0:T(8,128)S(1)}, u32[]{:S(2)}, u32[]{:S(2)}) collective-permute-start(f32[3,1,64,256]{3,2,1,0:T(8,128)S(1)} %get-tuple-element.213), channel_id=1, source_target_pairs={{1,0},{2,1},{3,2},{4,3},{5,4},{6,5},{7,6},{8,7},{9,8},{10,9},{11,1... | collective-permute-start | bytes 589832 | tf_op jit(solution)/shard_map/while/body/eval_jaxpr/ppermute | solution.py:25
  8.0 2.2 %collective-permute-start.1 = (f32[3,1,64,256]{3,2,1,0:T(8,128)S(1)}, f32[3,1,64,256]{3,2,1,0:T(8,128)S(1)}, u32[]{:S(2)}, u32[]{:S(2)}) collective-permute-start(f32[3,1,64,256]{3,2,1,0:T(8,128)S(1)} %get-tuple-element.214), channel_id=1, source_target_pairs={{0,1},{1,2},{2,3},{3,4},{4,5},{5,6},{6,7},{7,8},{8,9},{9,10},{10,1... | collective-permute-start | bytes 589832 | tf_op jit(solution)/shard_map/while/body/eval_jaxpr/ppermute | solution.py:22
  10.3 2.3 %collective-permute-done = f32[3,1,64,256]{3,2,1,0:T(8,128)S(1)} collective-permute-done((f32[3,1,64,256]{3,2,1,0:T(8,128)S(1)}, f32[3,1,64,256]{3,2,1,0:T(8,128)S(1)}, u32[]{:S(2)}, u32[]{:S(2)}) %collective-permute-start) | collective-permute-done | bytes 196640 | tf_op jit(solution)/shard_map/while/body/eval_jaxpr/ppermute | solution.py:25
  12.6 4.0 %collective-permute-done.1 = f32[3,1,64,256]{3,2,1,0:T(8,128)S(1)} collective-permute-done((f32[3,1,64,256]{3,2,1,0:T(8,128)S(1)}, f32[3,1,64,256]{3,2,1,0:T(8,128)S(1)}, u32[]{:S(2)}, u32[]{:S(2)}) %collective-permute-start.1) | collective-permute-done | bytes 196640 | tf_op jit(solution)/shard_map/while/body/eval_jaxpr/ppermute | solution.py:22
  16.7 0.4 select_maximum_fusion.6
  17.3 0.3 fusion.173
  18.0 2.0 %multiply_add_fusion.4 = (f32[3,2,64,256]{3,2,1,0:T(8,128)S(1)}, f32[3,2,64,256]{3,2,1,0:T(8,128)S(1)}) fusion(f32[6,2,64,256]{3,2,1,0:T(8,128)S(1)} %get-tuple-element.232, f32[3,2,64,256]{3,2,1,0:T(8,128)S(1)} %get-tuple-element.241, f32[1,2,64,256]{3,2,1,0:T(8,128)S(1)} %fusion.172, f32[1,2,64,256]{3,2,1,0:T(8,128)S(1)} %fusion.173, ...), kind=kLoop, calls=%fused_computation.99.clone.1 | loop fusion | flops 8749056 | bytes 12845056 | tf_op jit(solution)/shard_map/while/body/eval_jaxpr/add | solution.py:97
  20.1 6.2 %collective-permute-start = (f32[3,1,64,256]{3,2,1,0:T(8,128)S(1)}, f32[3,1,64,256]{3,2,1,0:T(8,128)S(1)}, u32[]{:S(2)}, u32[]{:S(2)}) collective-permute-start(f32[3,1,64,256]{3,2,1,0:T(8,128)S(1)} %get-tuple-element.213), channel_id=1, source_target_pairs={{1,0},{2,1},{3,2},{4,3},{5,4},{6,5},{7,6},{8,7},{9,8},{10,9},{11,1... | collective-permute-start | bytes 589832 | tf_op jit(solution)/shard_map/while/body/eval_jaxpr/ppermute | solution.py:25
  26.3 1.9 %collective-permute-start.1 = (f32[3,1,64,256]{3,2,1,0:T(8,128)S(1)}, f32[3,1,64,256]{3,2,1,0:T(8,128)S(1)}, u32[]{:S(2)}, u32[]{:S(2)}) collective-permute-start(f32[3,1,64,256]{3,2,1,0:T(8,128)S(1)} %get-tuple-element.214), channel_id=1, source_target_pairs={{0,1},{1,2},{2,3},{3,4},{4,5},{5,6},{6,7},{7,8},{8,9},{9,10},{10,1... | collective-permute-start | bytes 589832 | tf_op jit(solution)/shard_map/while/body/eval_jaxpr/ppermute | solution.py:22
  28.2 1.8 %collective-permute-done = f32[3,1,64,256]{3,2,1,0:T(8,128)S(1)} collective-permute-done((f32[3,1,64,256]{3,2,1,0:T(8,128)S(1)}, f32[3,1,64,256]{3,2,1,0:T(8,128)S(1)}, u32[]{:S(2)}, u32[]{:S(2)}) %collective-permute-start) | collective-permute-done | bytes 196640 | tf_op jit(solution)/shard_map/while/body/eval_jaxpr/ppermute | solution.py:25
  30.0 4.7 %collective-permute-done.1 = f32[3,1,64,256]{3,2,1,0:T(8,128)S(1)} collective-permute-done((f32[3,1,64,256]{3,2,1,0:T(8,128)S(1)}, f32[3,1,64,256]{3,2,1,0:T(8,128)S(1)}, u32[]{:S(2)}, u32[]{:S(2)}) %collective-permute-start.1) | collective-permute-done | bytes 196640 | tf_op jit(solution)/shard_map/while/body/eval_jaxpr/ppermute | solution.py:22
  34.7 0.4 select_maximum_fusion.6
  35.4 0.3 fusion.173
  36.0 2.0 %multiply_add_fusion.4 = (f32[3,2,64,256]{3,2,1,0:T(8,128)S(1)}, f32[3,2,64,256]{3,2,1,0:T(8,128)S(1)}) fusion(f32[6,2,64,256]{3,2,1,0:T(8,128)S(1)} %get-tuple-element.232, f32[3,2,64,256]{3,2,1,0:T(8,128)S(1)} %get-tuple-element.241, f32[1,2,64,256]{3,2,1,0:T(8,128)S(1)} %fusion.172, f32[1,2,64,256]{3,2,1,0:T(8,128)S(1)} %fusion.173, ...), kind=kLoop, calls=%fused_computation.99.clone.1 | loop fusion | flops 8749056 | bytes 12845056 | tf_op jit(solution)/shard_map/while/body/eval_jaxpr/add | solution.py:97
  38.1 3.4 %collective-permute-start = (f32[3,1,64,256]{3,2,1,0:T(8,128)S(1)}, f32[3,1,64,256]{3,2,1,0:T(8,128)S(1)}, u32[]{:S(2)}, u32[]{:S(2)}) collective-permute-start(f32[3,1,64,256]{3,2,1,0:T(8,128)S(1)} %get-tuple-element.213), channel_id=1, source_target_pairs={{1,0},{2,1},{3,2},{4,3},{5,4},{6,5},{7,6},{8,7},{9,8},{10,9},{11,1... | collective-permute-start | bytes 589832 | tf_op jit(solution)/shard_map/while/body/eval_jaxpr/ppermute | solution.py:25
  41.5 2.2 %collective-permute-start.1 = (f32[3,1,64,256]{3,2,1,0:T(8,128)S(1)}, f32[3,1,64,256]{3,2,1,0:T(8,128)S(1)}, u32[]{:S(2)}, u32[]{:S(2)}) collective-permute-start(f32[3,1,64,256]{3,2,1,0:T(8,128)S(1)} %get-tuple-element.214), channel_id=1, source_target_pairs={{0,1},{1,2},{2,3},{3,4},{4,5},{5,6},{6,7},{7,8},{8,9},{9,10},{10,1... | collective-permute-start | bytes 589832 | tf_op jit(solution)/shard_map/while/body/eval_jaxpr/ppermute | solution.py:22
  43.7 1.6 %collective-permute-done = f32[3,1,64,256]{3,2,1,0:T(8,128)S(1)} collective-permute-done((f32[3,1,64,256]{3,2,1,0:T(8,128)S(1)}, f32[3,1,64,256]{3,2,1,0:T(8,128)S(1)}, u32[]{:S(2)}, u32[]{:S(2)}) %collective-permute-start) | collective-permute-done | bytes 196640 | tf_op jit(solution)/shard_map/while/body/eval_jaxpr/ppermute | solution.py:25
  45.3 4.7 %collective-permute-done.1 = f32[3,1,64,256]{3,2,1,0:T(8,128)S(1)} collective-permute-done((f32[3,1,64,256]{3,2,1,0:T(8,128)S(1)}, f32[3,1,64,256]{3,2,1,0:T(8,128)S(1)}, u32[]{:S(2)}, u32[]{:S(2)}) %collective-permute-start.1) | collective-permute-done | bytes 196640 | tf_op jit(solution)/shard_map/while/body/eval_jaxpr/ppermute | solution.py:22
  50.0 0.4 select_maximum_fusion.6
  51.3 2.0 %multiply_add_fusion.4 = (f32[3,2,64,256]{3,2,1,0:T(8,128)S(1)}, f32[3,2,64,256]{3,2,1,0:T(8,128)S(1)}) fusion(f32[6,2,64,256]{3,2,1,0:T(8,128)S(1)} %get-tuple-element.232, f32[3,2,64,256]{3,2,1,0:T(8,128)S(1)} %get-tuple-element.241, f32[1,2,64,256]{3,2,1,0:T(8,128)S(1)} %fusion.172, f32[1,2,64,256]{3,2,1,0:T(8,128)S(1)} %fusion.173, ...), kind=kLoop, calls=%fused_computation.99.clone.1 | loop fusion | flops 8749056 | bytes 12845056 | tf_op jit(solution)/shard_map/while/body/eval_jaxpr/add | solution.py:97
  53.4 6.5 %collective-permute-start = (f32[3,1,64,256]{3,2,1,0:T(8,128)S(1)}, f32[3,1,64,256]{3,2,1,0:T(8,128)S(1)}, u32[]{:S(2)}, u32[]{:S(2)}) collective-permute-start(f32[3,1,64,256]{3,2,1,0:T(8,128)S(1)} %get-tuple-element.213), channel_id=1, source_target_pairs={{1,0},{2,1},{3,2},{4,3},{5,4},{6,5},{7,6},{8,7},{9,8},{10,9},{11,1... | collective-permute-start | bytes 589832 | tf_op jit(solution)/shard_map/while/body/eval_jaxpr/ppermute | solution.py:25
  59.9 1.9 %collective-permute-start.1 = (f32[3,1,64,256]{3,2,1,0:T(8,128)S(1)}, f32[3,1,64,256]{3,2,1,0:T(8,128)S(1)}, u32[]{:S(2)}, u32[]{:S(2)}) collective-permute-start(f32[3,1,64,256]{3,2,1,0:T(8,128)S(1)} %get-tuple-element.214), channel_id=1, source_target_pairs={{0,1},{1,2},{2,3},{3,4},{4,5},{5,6},{6,7},{7,8},{8,9},{9,10},{10,1... | collective-permute-start | bytes 589832 | tf_op jit(solution)/shard_map/while/body/eval_jaxpr/ppermute | solution.py:22
  61.9 1.8 %collective-permute-done = f32[3,1,64,256]{3,2,1,0:T(8,128)S(1)} collective-permute-done((f32[3,1,64,256]{3,2,1,0:T(8,128)S(1)}, f32[3,1,64,256]{3,2,1,0:T(8,128)S(1)}, u32[]{:S(2)}, u32[]{:S(2)}) %collective-permute-start) | collective-permute-done | bytes 196640 | tf_op jit(solution)/shard_map/while/body/eval_jaxpr/ppermute | solution.py:25
  63.7 4.7 %collective-permute-done.1 = f32[3,1,64,256]{3,2,1,0:T(8,128)S(1)} collective-permute-done((f32[3,1,64,256]{3,2,1,0:T(8,128)S(1)}, f32[3,1,64,256]{3,2,1,0:T(8,128)S(1)}, u32[]{:S(2)}, u32[]{:S(2)}) %collective-permute-start.1) | collective-permute-done | bytes 196640 | tf_op jit(solution)/shard_map/while/body/eval_jaxpr/ppermute | solution.py:22
  68.4 0.4 select_maximum_fusion.6
  69.7 2.0 %multiply_add_fusion.4 = (f32[3,2,64,256]{3,2,1,0:T(8,128)S(1)}, f32[3,2,64,256]{3,2,1,0:T(8,128)S(1)}) fusion(f32[6,2,64,256]{3,2,1,0:T(8,128)S(1)} %get-tuple-element.232, f32[3,2,64,256]{3,2,1,0:T(8,128)S(1)} %get-tuple-element.241, f32[1,2,64,256]{3,2,1,0:T(8,128)S(1)} %fusion.172, f32[1,2,64,256]{3,2,1,0:T(8,128)S(1)} %fusion.173, ...), kind=kLoop, calls=%fused_computation.99.clone.1 | loop fusion | flops 8749056 | bytes 12845056 | tf_op jit(solution)/shard_map/while/body/eval_jaxpr/add | solution.py:97
  71.9 33.6 %while.25 = (s32[]{:T(128)}, f32[6,2,64,256]{3,2,1,0:T(8,128)S(1)}, f32[2,64,256]{2,1,0:T(8,128)S(1)}, f32[2,64,256]{2,1,0:T(8,128)S(1)}, s32[]{:T(128)}) while((s32[]{:T(128)}, f32[6,2,64,256]{3,2,1,0:T(8,128)S(1)}, f32[2,64,256]{2,1,0:T(8,128)S(1)}, f32[2,64,256]{2,1,0:T(8,128)S(1)}, s32[]{:T(128)}) %tuple.67), condition=%wide.region_7.8_spmd, body=%wide.region_6.7_spmd.sunk | while | flops 13255890 | bytes 24017228 | solution.py:100
  71.9 3.4 %collective-permute-start.2 = (f32[3,1,64,256]{3,2,1,0:T(8,128)S(1)}, f32[3,1,64,256]{3,2,1,0:T(8,128)S(1)}, u32[]{:S(2)}, u32[]{:S(2)}) collective-permute-start(f32[3,1,64,256]{3,2,1,0:T(8,128)S(1)} %get-tuple-element.221), channel_id=1, source_target_pairs={{1,0},{2,1},{3,2},{4,3},{5,4},{6,5},{7,6},{8,7},{9,8},{10,9},{11,1... | collective-permute-start | bytes 589832 | tf_op jit(solution)/shard_map/while/body/eval_jaxpr/ppermute | solution.py:25
  75.3 2.2 %collective-permute-start.3 = (f32[3,1,64,256]{3,2,1,0:T(8,128)S(1)}, f32[3,1,64,256]{3,2,1,0:T(8,128)S(1)}, u32[]{:S(2)}, u32[]{:S(2)}) collective-permute-start(f32[3,1,64,256]{3,2,1,0:T(8,128)S(1)} %get-tuple-element.222), channel_id=1, source_target_pairs={{0,1},{1,2},{2,3},{3,4},{4,5},{5,6},{6,7},{7,8},{8,9},{9,10},{10,1... | collective-permute-start | bytes 589832 | tf_op jit(solution)/shard_map/while/body/eval_jaxpr/ppermute | solution.py:22
  77.5 1.6 %collective-permute-done.2 = f32[3,1,64,256]{3,2,1,0:T(8,128)S(1)} collective-permute-done((f32[3,1,64,256]{3,2,1,0:T(8,128)S(1)}, f32[3,1,64,256]{3,2,1,0:T(8,128)S(1)}, u32[]{:S(2)}, u32[]{:S(2)}) %collective-permute-start.2) | collective-permute-done | bytes 196640 | tf_op jit(solution)/shard_map/while/body/eval_jaxpr/ppermute | solution.py:25
  79.1 4.7 %collective-permute-done.3 = f32[3,1,64,256]{3,2,1,0:T(8,128)S(1)} collective-permute-done((f32[3,1,64,256]{3,2,1,0:T(8,128)S(1)}, f32[3,1,64,256]{3,2,1,0:T(8,128)S(1)}, u32[]{:S(2)}, u32[]{:S(2)}) %collective-permute-start.3) | collective-permute-done | bytes 196640 | tf_op jit(solution)/shard_map/while/body/eval_jaxpr/ppermute | solution.py:22
  83.8 0.4 select_maximum_fusion.7
  85.1 2.0 %multiply_add_fusion.5 = (f32[3,2,64,256]{3,2,1,0:T(8,128)S(1)}, f32[3,2,64,256]{3,2,1,0:T(8,128)S(1)}) fusion(f32[6,2,64,256]{3,2,1,0:T(8,128)S(1)} %get-tuple-element.249, f32[1,2,64,256]{3,2,1,0:T(8,128)S(1)} %fusion.176, f32[1,2,64,256]{3,2,1,0:T(8,128)S(1)} %fusion.177, f32[1,2,64,256]{3,2,1,0:T(8,128)S(1)} %fusion.178, ...), kind=kLoop, calls=%fused_computation.236.clone.1 | loop fusion | flops 8650752 | bytes 12451840 | tf_op jit(solution)/shard_map/while/body/eval_jaxpr/add | solution.py:97
  87.2 6.5 %collective-permute-start.2 = (f32[3,1,64,256]{3,2,1,0:T(8,128)S(1)}, f32[3,1,64,256]{3,2,1,0:T(8,128)S(1)}, u32[]{:S(2)}, u32[]{:S(2)}) collective-permute-start(f32[3,1,64,256]{3,2,1,0:T(8,128)S(1)} %get-tuple-element.221), channel_id=1, source_target_pairs={{1,0},{2,1},{3,2},{4,3},{5,4},{6,5},{7,6},{8,7},{9,8},{10,9},{11,1... | collective-permute-start | bytes 589832 | tf_op jit(solution)/shard_map/while/body/eval_jaxpr/ppermute | solution.py:25
  93.7 1.9 %collective-permute-start.3 = (f32[3,1,64,256]{3,2,1,0:T(8,128)S(1)}, f32[3,1,64,256]{3,2,1,0:T(8,128)S(1)}, u32[]{:S(2)}, u32[]{:S(2)}) collective-permute-start(f32[3,1,64,256]{3,2,1,0:T(8,128)S(1)} %get-tuple-element.222), channel_id=1, source_target_pairs={{0,1},{1,2},{2,3},{3,4},{4,5},{5,6},{6,7},{7,8},{8,9},{9,10},{10,1... | collective-permute-start | bytes 589832 | tf_op jit(solution)/shard_map/while/body/eval_jaxpr/ppermute | solution.py:22
  95.7 1.8 %collective-permute-done.2 = f32[3,1,64,256]{3,2,1,0:T(8,128)S(1)} collective-permute-done((f32[3,1,64,256]{3,2,1,0:T(8,128)S(1)}, f32[3,1,64,256]{3,2,1,0:T(8,128)S(1)}, u32[]{:S(2)}, u32[]{:S(2)}) %collective-permute-start.2) | collective-permute-done | bytes 196640 | tf_op jit(solution)/shard_map/while/body/eval_jaxpr/ppermute | solution.py:25
  97.5 4.7 %collective-permute-done.3 = f32[3,1,64,256]{3,2,1,0:T(8,128)S(1)} collective-permute-done((f32[3,1,64,256]{3,2,1,0:T(8,128)S(1)}, f32[3,1,64,256]{3,2,1,0:T(8,128)S(1)}, u32[]{:S(2)}, u32[]{:S(2)}) %collective-permute-start.3) | collective-permute-done | bytes 196640 | tf_op jit(solution)/shard_map/while/body/eval_jaxpr/ppermute | solution.py:22
  102.2 0.4 select_maximum_fusion.7
  102.8 0.3 fusion.177
  103.5 2.0 %multiply_add_fusion.5 = (f32[3,2,64,256]{3,2,1,0:T(8,128)S(1)}, f32[3,2,64,256]{3,2,1,0:T(8,128)S(1)}) fusion(f32[6,2,64,256]{3,2,1,0:T(8,128)S(1)} %get-tuple-element.249, f32[1,2,64,256]{3,2,1,0:T(8,128)S(1)} %fusion.176, f32[1,2,64,256]{3,2,1,0:T(8,128)S(1)} %fusion.177, f32[1,2,64,256]{3,2,1,0:T(8,128)S(1)} %fusion.178, ...), kind=kLoop, calls=%fused_computation.236.clone.1 | loop fusion | flops 8650752 | bytes 12451840 | tf_op jit(solution)/shard_map/while/body/eval_jaxpr/add | solution.py:97
  105.5 1.3 %collective-permute-start.4 = (f32[6,2,64,256]{3,2,1,0:T(8,128)S(1)}, f32[6,2,64,256]{3,2,1,0:T(8,128)S(1)}, u32[]{:S(2)}, u32[]{:S(2)}) collective-permute-start(f32[6,2,64,256]{3,2,1,0:T(8,128)S(1)} %get-tuple-element.124), channel_id=1, source_target_pairs={{0,16},{1,17},{2,18},{3,19},{4,20},{5,21},{6,22},{7,23},{8,24},{9,... | collective-permute-start | bytes 2359304 | tf_op jit(solution)/shard_map/ppermute | solution.py:33
  106.8 3.4 %collective-permute-done.4 = f32[6,2,64,256]{3,2,1,0:T(8,128)S(1)} collective-permute-done((f32[6,2,64,256]{3,2,1,0:T(8,128)S(1)}, f32[6,2,64,256]{3,2,1,0:T(8,128)S(1)}, u32[]{:S(2)}, u32[]{:S(2)}) %collective-permute-start.4) | collective-permute-done | bytes 786464 | tf_op jit(solution)/shard_map/ppermute | solution.py:33
  110.3 1.1 add_bitcast_fusion
  (48 shorter events, 5.2 us)
Async XLA Ops:
  0.0 2.5 %copy-start.5 = (f32[16]{0:T(128)S(1)}, f32[16]{0:T(128)}, u32[]{:S(2)}) copy-start(f32[16]{0:T(128)} %param.16) | copy-start | bytes 196
  0.0 3.8 %copy-start.3 = (f32[8]{0:T(128)S(1)}, f32[8]{0:T(128)}, u32[]{:S(2)}) copy-start(f32[8]{0:T(128)} %param.15) | copy-start | bytes 100
  0.0 3.8 %copy-start.4 = (f32[8]{0:T(128)S(1)}, f32[8]{0:T(128)}, u32[]{:S(2)}) copy-start(f32[8]{0:T(128)} %param.14) | copy-start | bytes 100
  0.0 3.8 %copy-start.2 = (s32[2,64,256]{2,1,0:T(8,128)S(1)}, s32[2,64,256]{2,1,0:T(8,128)}, u32[]{:S(2)}) copy-start(s32[2,64,256]{2,1,0:T(8,128)} %param.13) | copy-start | bytes 393220
  0.0 4.0 %copy-start.1 = (bf16[3,2,64,256]{3,2,1,0:T(8,128)(2,1)S(1)}, bf16[3,2,64,256]{3,2,1,0:T(8,128)(2,1)}, u32[]{:S(2)}) copy-start(bf16[3,2,64,256]{3,2,1,0:T(8,128)(2,1)} %param.12) | copy-start | bytes 589828
  4.8 67.0 %copy-start = (f32[1,6,2,64,256]{4,3,2,1,0:T(8,128)S(1)}, f32[1,6,2,64,256]{4,3,2,1,0:T(8,128)}, u32[]{:S(2)}) copy-start(f32[1,6,2,64,256]{4,3,2,1,0:T(8,128)} %param.11) | copy-start | bytes 2359300
  4.8 7.8 %collective-permute-start = (f32[3,1,64,256]{3,2,1,0:T(8,128)S(1)}, f32[3,1,64,256]{3,2,1,0:T(8,128)S(1)}, u32[]{:S(2)}, u32[]{:S(2)}) collective-permute-start(f32[3,1,64,256]{3,2,1,0:T(8,128)S(1)} %get-tuple-element.213), channel_id=1, source_target_pairs={{1,0},{2,1},{3,2},{4,3},{5,4},{6,5},{7,6},{8,7},{9,8},{10,9},{11,1... | collective-permute-start | bytes 589832 | tf_op jit(solution)/shard_map/while/body/eval_jaxpr/ppermute | solution.py:25
  8.0 8.6 %collective-permute-start.1 = (f32[3,1,64,256]{3,2,1,0:T(8,128)S(1)}, f32[3,1,64,256]{3,2,1,0:T(8,128)S(1)}, u32[]{:S(2)}, u32[]{:S(2)}) collective-permute-start(f32[3,1,64,256]{3,2,1,0:T(8,128)S(1)} %get-tuple-element.214), channel_id=1, source_target_pairs={{0,1},{1,2},{2,3},{3,4},{4,5},{5,6},{6,7},{7,8},{8,9},{9,10},{10,1... | collective-permute-start | bytes 589832 | tf_op jit(solution)/shard_map/while/body/eval_jaxpr/ppermute | solution.py:22
  20.1 9.9 %collective-permute-start = (f32[3,1,64,256]{3,2,1,0:T(8,128)S(1)}, f32[3,1,64,256]{3,2,1,0:T(8,128)S(1)}, u32[]{:S(2)}, u32[]{:S(2)}) collective-permute-start(f32[3,1,64,256]{3,2,1,0:T(8,128)S(1)} %get-tuple-element.213), channel_id=1, source_target_pairs={{1,0},{2,1},{3,2},{4,3},{5,4},{6,5},{7,6},{8,7},{9,8},{10,9},{11,1... | collective-permute-start | bytes 589832 | tf_op jit(solution)/shard_map/while/body/eval_jaxpr/ppermute | solution.py:25
  26.3 8.4 %collective-permute-start.1 = (f32[3,1,64,256]{3,2,1,0:T(8,128)S(1)}, f32[3,1,64,256]{3,2,1,0:T(8,128)S(1)}, u32[]{:S(2)}, u32[]{:S(2)}) collective-permute-start(f32[3,1,64,256]{3,2,1,0:T(8,128)S(1)} %get-tuple-element.214), channel_id=1, source_target_pairs={{0,1},{1,2},{2,3},{3,4},{4,5},{5,6},{6,7},{7,8},{8,9},{9,10},{10,1... | collective-permute-start | bytes 589832 | tf_op jit(solution)/shard_map/while/body/eval_jaxpr/ppermute | solution.py:22
  38.1 7.2 %collective-permute-start = (f32[3,1,64,256]{3,2,1,0:T(8,128)S(1)}, f32[3,1,64,256]{3,2,1,0:T(8,128)S(1)}, u32[]{:S(2)}, u32[]{:S(2)}) collective-permute-start(f32[3,1,64,256]{3,2,1,0:T(8,128)S(1)} %get-tuple-element.213), channel_id=1, source_target_pairs={{1,0},{2,1},{3,2},{4,3},{5,4},{6,5},{7,6},{8,7},{9,8},{10,9},{11,1... | collective-permute-start | bytes 589832 | tf_op jit(solution)/shard_map/while/body/eval_jaxpr/ppermute | solution.py:25
  41.5 8.4 %collective-permute-start.1 = (f32[3,1,64,256]{3,2,1,0:T(8,128)S(1)}, f32[3,1,64,256]{3,2,1,0:T(8,128)S(1)}, u32[]{:S(2)}, u32[]{:S(2)}) collective-permute-start(f32[3,1,64,256]{3,2,1,0:T(8,128)S(1)} %get-tuple-element.214), channel_id=1, source_target_pairs={{0,1},{1,2},{2,3},{3,4},{4,5},{5,6},{6,7},{7,8},{8,9},{9,10},{10,1... | collective-permute-start | bytes 589832 | tf_op jit(solution)/shard_map/while/body/eval_jaxpr/ppermute | solution.py:22
  53.4 10.3 %collective-permute-start = (f32[3,1,64,256]{3,2,1,0:T(8,128)S(1)}, f32[3,1,64,256]{3,2,1,0:T(8,128)S(1)}, u32[]{:S(2)}, u32[]{:S(2)}) collective-permute-start(f32[3,1,64,256]{3,2,1,0:T(8,128)S(1)} %get-tuple-element.213), channel_id=1, source_target_pairs={{1,0},{2,1},{3,2},{4,3},{5,4},{6,5},{7,6},{8,7},{9,8},{10,9},{11,1... | collective-permute-start | bytes 589832 | tf_op jit(solution)/shard_map/while/body/eval_jaxpr/ppermute | solution.py:25
  59.9 8.4 %collective-permute-start.1 = (f32[3,1,64,256]{3,2,1,0:T(8,128)S(1)}, f32[3,1,64,256]{3,2,1,0:T(8,128)S(1)}, u32[]{:S(2)}, u32[]{:S(2)}) collective-permute-start(f32[3,1,64,256]{3,2,1,0:T(8,128)S(1)} %get-tuple-element.214), channel_id=1, source_target_pairs={{0,1},{1,2},{2,3},{3,4},{4,5},{5,6},{6,7},{7,8},{8,9},{9,10},{10,1... | collective-permute-start | bytes 589832 | tf_op jit(solution)/shard_map/while/body/eval_jaxpr/ppermute | solution.py:22
  71.9 7.2 %collective-permute-start.2 = (f32[3,1,64,256]{3,2,1,0:T(8,128)S(1)}, f32[3,1,64,256]{3,2,1,0:T(8,128)S(1)}, u32[]{:S(2)}, u32[]{:S(2)}) collective-permute-start(f32[3,1,64,256]{3,2,1,0:T(8,128)S(1)} %get-tuple-element.221), channel_id=1, source_target_pairs={{1,0},{2,1},{3,2},{4,3},{5,4},{6,5},{7,6},{8,7},{9,8},{10,9},{11,1... | collective-permute-start | bytes 589832 | tf_op jit(solution)/shard_map/while/body/eval_jaxpr/ppermute | solution.py:25
  75.3 8.4 %collective-permute-start.3 = (f32[3,1,64,256]{3,2,1,0:T(8,128)S(1)}, f32[3,1,64,256]{3,2,1,0:T(8,128)S(1)}, u32[]{:S(2)}, u32[]{:S(2)}) collective-permute-start(f32[3,1,64,256]{3,2,1,0:T(8,128)S(1)} %get-tuple-element.222), channel_id=1, source_target_pairs={{0,1},{1,2},{2,3},{3,4},{4,5},{5,6},{6,7},{7,8},{8,9},{9,10},{10,1... | collective-permute-start | bytes 589832 | tf_op jit(solution)/shard_map/while/body/eval_jaxpr/ppermute | solution.py:22
  87.2 10.3 %collective-permute-start.2 = (f32[3,1,64,256]{3,2,1,0:T(8,128)S(1)}, f32[3,1,64,256]{3,2,1,0:T(8,128)S(1)}, u32[]{:S(2)}, u32[]{:S(2)}) collective-permute-start(f32[3,1,64,256]{3,2,1,0:T(8,128)S(1)} %get-tuple-element.221), channel_id=1, source_target_pairs={{1,0},{2,1},{3,2},{4,3},{5,4},{6,5},{7,6},{8,7},{9,8},{10,9},{11,1... | collective-permute-start | bytes 589832 | tf_op jit(solution)/shard_map/while/body/eval_jaxpr/ppermute | solution.py:25
  93.7 8.4 %collective-permute-start.3 = (f32[3,1,64,256]{3,2,1,0:T(8,128)S(1)}, f32[3,1,64,256]{3,2,1,0:T(8,128)S(1)}, u32[]{:S(2)}, u32[]{:S(2)}) collective-permute-start(f32[3,1,64,256]{3,2,1,0:T(8,128)S(1)} %get-tuple-element.222), channel_id=1, source_target_pairs={{0,1},{1,2},{2,3},{3,4},{4,5},{5,6},{6,7},{7,8},{8,9},{9,10},{10,1... | collective-permute-start | bytes 589832 | tf_op jit(solution)/shard_map/while/body/eval_jaxpr/ppermute | solution.py:22
  105.5 4.7 %collective-permute-start.4 = (f32[6,2,64,256]{3,2,1,0:T(8,128)S(1)}, f32[6,2,64,256]{3,2,1,0:T(8,128)S(1)}, u32[]{:S(2)}, u32[]{:S(2)}) collective-permute-start(f32[6,2,64,256]{3,2,1,0:T(8,128)S(1)} %get-tuple-element.124), channel_id=1, source_target_pairs={{0,16},{1,17},{2,18},{3,19},{4,20},{5,21},{6,22},{7,23},{8,24},{9,... | collective-permute-start | bytes 2359304 | tf_op jit(solution)/shard_map/ppermute | solution.py:33

commit v2 on v1

--- a/solution.py
+++ b/solution.py
@@ -1,6 +1,10 @@
+import functools
+
 import jax
 import jax.numpy as jnp
 from jax import lax
+from jax.experimental import pallas as pl
+from jax.experimental.pallas import tpu as pltpu
 from jax.sharding import PartitionSpec as P
 
 FINE = 4
@@ -12,6 +16,20 @@
 FACE_WEIGHT = 14.0 / 30.0
 EDGE_WEIGHT = 3.0 / 30.0
 CORNER_WEIGHT = 1.0 / 30.0
+
+
+def passed_along(block, axis, distance):
+    devices = range(lax.axis_size(axis))
+    route = [(i - distance, i) for i in devices if i - distance in devices]
+    return lax.ppermute(block, axis, route)
+
+
+def table_pick(table, position):
+    return jnp.sum(
+        jnp.where(
+            jnp.arange(table.shape[0], dtype=jnp.int32) == position, table, jnp.zeros_like(table)
+        )
+    )
 
 
 def padded_2(block, sides, width):
@@ -25,12 +43,6 @@
         high = lax.ppermute(lax.slice_in_dim(block, 0, width, axis=dim), axis, backward)
         block = jnp.concatenate([low, block, high], axis=dim)
     return block
-
-
-def passed_along(block, axis, distance):
-    devices = range(lax.axis_size(axis))
-    route = [(i - distance, i) for i in devices if i - distance in devices]
-    return lax.ppermute(block, axis, route)
 
 
 def combine(first_vec, second_vec, first_sign, second_sign):
@@ -100,15 +112,7 @@
     return lax.fori_loop(0, step_count, advance, status)
 
 
-def table_pick(table, position):
-    return jnp.sum(
-        jnp.where(
-            jnp.arange(table.shape[0], dtype=jnp.int32) == position, table, jnp.zeros_like(table)
-        )
-    )
-
-
-def shards(states, load_shape, zone_ids, zone_shear, zone_lame, amp_table, cycle_index):
+def shards_single(states, load_shape, zone_ids, zone_shear, zone_lame, amp_table, cycle_index):
     windows = lax.axis_size("win")
     window_index = lax.axis_index("win")
     zone_range = jnp.arange(zone_shear.shape[0], dtype=jnp.int32)
@@ -137,6 +141,296 @@
     return new_end[None]
 
 
+class Inplane:
+    def __init__(self, u):
+        rows, columns = u[0].shape
+        row = lax.broadcasted_iota(jnp.int32, (rows, columns), 0)
+        column = lax.broadcasted_iota(jnp.int32, (rows, columns), 1)
+
+        def shifted(f, axis, up):
+            if up:
+                edge = (row == rows - 1, column == columns - 1)[axis]
+                return jnp.where(edge, 0.0, pltpu.roll(f, f.shape[axis] - 1, axis))
+            edge = (row == 0, column == 0)[axis]
+            return jnp.where(edge, 0.0, pltpu.roll(f, 1, axis))
+
+        self.u = u
+        self.shifted = shifted
+        plus = [shifted(f, 1, True) for f in u]
+        minus = [shifted(f, 1, False) for f in u]
+        self.sum_x = [a + b for a, b in zip(plus, minus)]
+        self.diff_x = [a - b for a, b in zip(plus, minus)]
+        self.up_y = [None, shifted(u[1], 0, True), shifted(u[2], 0, True)]
+        self.down_y = [None, shifted(u[1], 0, False), shifted(u[2], 0, False)]
+        self.even = []
+        for f, s in zip(u, self.sum_x):
+            across = s + 3.0 * f
+            square = shifted(across, 0, True) + shifted(across, 0, False) + 3.0 * across
+            self.even.append((square + 5.0 * f) * (1.0 / 30.0))
+        self.odd = [
+            0.25 * self.diff_x[2],
+            0.25 * (self.up_y[2] - self.down_y[2]),
+            0.25 * (self.diff_x[0] + (self.up_y[1] - self.down_y[1])),
+        ]
+
+    def own(self):
+        u, shifted = self.u, self.shifted
+        up_x, down_x = shifted(u[0], 0, True), shifted(u[0], 0, False)
+        sum_y = [up_x + down_x, self.up_y[1] + self.down_y[1], self.up_y[2] + self.down_y[2]]
+        shear = [
+            3.0 * e + (s + t) * (1.0 / 6.0) - (17.0 / 3.0) * f
+            for e, s, t, f in zip(self.even, self.sum_x, sum_y, u)
+        ]
+        cross = [
+            0.25 * (shifted(d, 0, True) - shifted(d, 0, False)) for d in self.diff_x[:2]
+        ]
+        bulk = [
+            self.sum_x[0] - 2.0 * u[0] + cross[1],
+            sum_y[1] - 2.0 * u[1] + cross[0],
+            -2.0 * u[2],
+        ]
+        return shear, bulk
+
+
+def towards(plane_sums, sign):
+    odd = [sign * f for f in plane_sums[3:6]]
+    return plane_sums[:3], [odd[0], odd[1], odd[2] + plane_sums[6]]
+
+
+def sums_of(inplane):
+    return (*inplane.even, *inplane.odd, inplane.u[2])
+
+
+def partial_step(planes, velocity, shear, bulk, load, step):
+    count = len(planes)
+    outgoing = [sums_of(p) for p in planes]
+    velocities, displaced = [], []
+    for z, plane in enumerate(planes):
+        even, other = plane.own()
+        for neighbour, sign in ((z - 1, -1.0), (z + 1, 1.0)):
+            if 0 <= neighbour < count:
+                e, o = towards(outgoing[neighbour], sign)
+                even = [a + b for a, b in zip(even, e)]
+                other = [a + b for a, b in zip(other, o)]
+        v = [
+            velocity(c, z) + step * (shear(z) * even[c] + bulk(z) * other[c] + load(c, z))
+            for c in range(3)
+        ]
+        velocities.append(v)
+        displaced.append([plane.u[c] + step * v[c] for c in range(3)])
+    return velocities, displaced, outgoing
+
+
+def prepare(planes, velocity, shear, bulk, load, step, part_ref, up_ref, down_ref, rim_ref):
+    count = len(planes)
+    velocities, displaced, outgoing = partial_step(planes, velocity, shear, bulk, load, step)
+    for z in range(count):
+        for c in range(3):
+            part_ref[c, z] = velocities[z][c]
+    for c in range(3):
+        down_ref[c] = planes[0].u[c]
+        down_ref[3 + c] = displaced[0][c]
+        up_ref[c] = planes[count - 1].u[c]
+        up_ref[3 + c] = displaced[count - 1][c]
+    for c in range(6):
+        rim_ref[0, c] = outgoing[0][c]
+        rim_ref[1, c] = outgoing[count - 1][c]
+
+
+def zone_values(zone, shear_table, lame_table, offset):
+    shear = jnp.zeros(zone.shape, jnp.float32)
+    bulk = jnp.zeros(zone.shape, jnp.float32)
+    for k in range(shear_table.shape[0]):
+        hit = zone == k + offset
+        shear = jnp.where(hit, shear_table[k], shear)
+        bulk = jnp.where(hit, shear_table[k] + lame_table[k], bulk)
+    return shear, bulk
+
+
+def open_kernel(
+    step, shear_table, lame_table, amp_ref, state, load_shape, zones,
+    moduli, loading, part, up, down, rim,
+):
+    count = zones.shape[0]
+    amplitude = amp_ref[0]
+    for z in range(count):
+        moduli[0, z], moduli[1, z] = zone_values(zones[z], shear_table, lame_table, 0)
+        for c in range(3):
+            loading[c, z] = amplitude * load_shape[c, z].astype(jnp.float32)
+    planes = [Inplane([state[c, z] for c in range(3)]) for z in range(count)]
+    prepare(
+        planes,
+        lambda c, z: state[3 + c, z],
+        lambda z: moduli[0, z],
+        lambda z: moduli[1, z],
+        lambda c, z: loading[c, z],
+        step, part, up, down, rim,
+    )
+    down[6] = (zones[0] + 1).astype(jnp.float32)
+    up[6] = (zones[count - 1] + 1).astype(jnp.float32)
+
+
+def two_steps(step, u0, part, rim, low, high, moduli, edges, load):
+    count = moduli.shape[1]
+    square = step * step
+    sides = ((low, 0, 0, -1.0), (high, 1, count - 1, 1.0))
+    velocities = [[part[c, z] for c in range(3)] for z in range(count)]
+    outer = []
+    for side, (got, edge, z, sign) in enumerate(sides):
+        there = Inplane([got[c] for c in range(3)])
+        even, odd = towards(sums_of(there), sign)
+        for c in range(3):
+            velocities[z][c] = velocities[z][c] + step * (
+                moduli[0, z] * even[c] + moduli[1, z] * odd[c]
+            )
+        here = tuple(rim[side, c] for c in range(6)) + (u0[2, z],)
+        even, odd = towards(here, -sign)
+        outer.append(
+            [
+                got[3 + c] + square * (edges[2 * side] * even[c] + edges[2 * side + 1] * odd[c])
+                for c in range(3)
+            ]
+        )
+    planes = [
+        Inplane([u0[c, z] + step * velocities[z][c] for c in range(3)]) for z in range(count)
+    ]
+    shear = lambda z: moduli[0, z]
+    bulk = lambda z: moduli[1, z]
+    ends, _, _ = partial_step(planes, lambda c, z: velocities[z][c], shear, bulk, load, step)
+    for side, (got, edge, z, sign) in enumerate(sides):
+        even, odd = towards(sums_of(Inplane(outer[side])), sign)
+        for c in range(3):
+            ends[z][c] = ends[z][c] + step * (shear(z) * even[c] + bulk(z) * odd[c])
+    displaced = [[planes[z].u[c] + step * ends[z][c] for c in range(3)] for z in range(count)]
+    return ends, displaced
+
+
+def edge_moduli(zone_low, zone_high, shear_table, lame_table):
+    return (
+        *zone_values(zone_low, shear_table, lame_table, 1.0),
+        *zone_values(zone_high, shear_table, lame_table, 1.0),
+    )
+
+
+def fine_kernel(
+    step, last, shear_table, lame_table, first_ref, start, state, moduli, loading, part, rim,
+    low, high, zone_low, zone_high, *outs,
+):
+    count = moduli.shape[1]
+    edges = edge_moduli(zone_low[...], zone_high[...], shear_table, lame_table)
+    ends, displaced = two_steps(
+        step, state, part, rim, low, high, moduli, edges, lambda c, z: loading[c, z]
+    )
+    new_state, next_part, up, down, next_rim = outs[:5]
+    for z in range(count):
+        for c in range(3):
+            new_state[c, z] = displaced[z][c]
+            new_state[3 + c, z] = ends[z][c]
+    if last:
+        entry = outs[5]
+        first = first_ref[0] == 1
+        for z in range(count):
+            for c in range(6):
+                entry[c, z] = jnp.where(first, new_state[c, z], start[c, z])
+        next_step, load = DT_COARSE, lambda c, z: 0.0
+    else:
+        entry = new_state
+        next_step, load = step, lambda c, z: loading[c, z]
+    planes = [Inplane([entry[c, z] for c in range(3)]) for z in range(count)]
+    prepare(
+        planes, lambda c, z: entry[3 + c, z], lambda z: moduli[0, z], lambda z: moduli[1, z],
+        load, next_step, next_part, up, down, next_rim,
+    )
+
+
+def coarse_open_kernel(state, moduli, part, up, down, rim):
+    count = moduli.shape[1]
+    planes = [Inplane([state[c, z] for c in range(3)]) for z in range(count)]
+    prepare(
+        planes, lambda c, z: state[3 + c, z], lambda z: moduli[0, z], lambda z: moduli[1, z],
+        lambda c, z: 0.0, DT_COARSE, part, up, down, rim,
+    )
+
+
+def coarse_kernel(
+    shear_table, lame_table, state, moduli, part, rim, low, high, zone_low, zone_high, new_state
+):
+    edges = edge_moduli(zone_low[...], zone_high[...], shear_table, lame_table)
+    ends, displaced = two_steps(
+        DT_COARSE, state, part, rim, low, high, moduli, edges, lambda c, z: 0.0
+    )
+    for z in range(moduli.shape[1]):
+        for c in range(3):
+            new_state[c, z] = displaced[z][c]
+            new_state[3 + c, z] = ends[z][c]
+
+
+def called(kernel, outs, scalars, *operands):
+    smem = pl.BlockSpec(memory_space=pltpu.SMEM)
+    vmem = pl.BlockSpec(memory_space=pltpu.VMEM)
+    return pl.pallas_call(
+        kernel,
+        out_shape=[jax.ShapeDtypeStruct(shape, jnp.float32) for shape in outs],
+        in_specs=[smem] * len(scalars) + [vmem] * len(operands),
+        out_specs=[vmem] * len(outs),
+        compiler_params=pltpu.CompilerParams(vmem_limit_bytes=48 * 1024 * 1024),
+    )(*scalars, *operands)
+
+
+def exchanged(up, down):
+    return passed_along(up, "slab", 1), passed_along(down, "slab", -1)
+
+
+def shards(states, load_shape, zone_ids, zone_shear, zone_lame, amp_table, cycle_index):
+    windows = lax.axis_size("win")
+    window_index = lax.axis_index("win")
+    first = window_index == 0
+    first_flag = first.astype(jnp.int32).reshape(1)
+    start = states[0]
+    count, rows, columns = zone_ids.shape
+    plane = (rows, columns)
+    field, state = (3, count, *plane), (6, count, *plane)
+    message, rims = (6, *plane), (2, 6, *plane)
+    amplitude = amp_table[cycle_index[window_index]].reshape(1)
+    tables = (zone_shear, zone_lame)
+
+    moduli, loading, part, up, down, rim = called(
+        functools.partial(open_kernel, DT_FINE),
+        [(2, count, *plane), field, field, (7, *plane), (7, *plane), rims],
+        (*tables, amplitude), start, load_shape, zone_ids,
+    )
+    low, high = exchanged(up, down)
+    zones = low[6], high[6]
+    current = start
+    entry = None
+    for turn in range(FINE // 2):
+        last = turn == FINE // 2 - 1
+        outs = [state, field, message, message, rims] + ([state] if last else [])
+        current, part, up, down, rim, *entry = called(
+            functools.partial(fine_kernel, DT_FINE, last), outs,
+            (*tables, first_flag), start, current, moduli, loading, part, rim, low, high, *zones,
+        )
+        low, high = exchanged(up, down)
+    fine_end = current
+
+    def coarse_end(status, part, rim, low, high):
+        return called(
+            coarse_kernel, [state], tables, status, moduli, part, rim, low, high, *zones
+        )[0]
+
+    advanced = coarse_end(entry[0], part, rim, low, high)
+    correction = fine_end - jnp.where(first, 0.0, advanced)
+    for _ in range(windows - 2):
+        status = correction + passed_along(advanced, "win", 1)
+        part, up, down, rim = called(
+            coarse_open_kernel, [field, message, message, rims], (), status, moduli
+        )
+        advanced = coarse_end(status, part, rim, *exchanged(up, down))
+    everyone = lax.ppermute(advanced, "win", [(i, (i + 1) % windows) for i in range(windows)])
+    new_end = correction + jnp.where(first, 0.0, everyone)
+    return new_end[None]
+
+
 def solution(mesh):
     placed = (
         P("win", None, "slab", None, None),
@@ -147,10 +441,15 @@
         P(),
         P(),
     )
-    return jax.shard_map(
-        shards,
-        mesh=mesh,
-        in_specs=placed,
-        out_specs=P("win", None, "slab", None, None),
-        check_vma=False,
-    )
+
+    def whole(states, *rest):
+        planes = states.shape[2] // mesh.shape["slab"]
+        return jax.shard_map(
+            shards if planes >= 2 else shards_single,
+            mesh=mesh,
+            in_specs=placed,
+            out_specs=P("win", None, "slab", None, None),
+            check_vma=False,
+        )(states, *rest)
+
+    return whole

time: 112 us -> 96.2 us (0.86)
  other arithmetic: 24.8 us -> 1.04 us
  starting transfers between devices: 42.8 us -> 19.1 us
  Pallas kernels: 0 us -> 13.2 us
  waiting for transfers between devices: 41.7 us -> 52.2 us
  local copies, waits for them, and re-layouts: 1.49 us -> 8.11 us
  between operations: 0.11 us -> 2.08 us
    ppermute x1 -> x6, waiting for transfers between devices: 3.42 us -> 50.3 us  [passed_along(): return lax.ppermute(block, axis, route)]
    ppermute x12 -> x1, starting transfers between devices: 41.5 us -> 0.56 us  [shards(): lax.ppermute(advanced, 'win', [(i, (i + 1) % windows) for i in range(wind...]
    ppermute x12 -> x1, waiting for transfers between devices: 38.2 us -> 1.91 us  [shards(): lax.ppermute(advanced, 'win', [(i, (i + 1) % windows) for i in range(wind...]
    ppermute x1 -> x6, starting transfers between devices: 1.29 us -> 18.5 us  [passed_along(): return lax.ppermute(block, axis, route)]
    add x25 -> x0, other arithmetic: 17.2 us -> none  [the longest x6 12 us: advance(): displaced = displaced + time_step * velocity]
    pallas_call x0 -> x4, Pallas kernels: none -> 13.2 us  [called(): pl.pallas_call(kernel, out_shape=[jax.ShapeDtypeStruct(shape, jnp.float32...]
    unnamed x13 -> x22, local copies, waits for them, and re-layouts: 1.16 us -> 6.93 us
    concatenate x12 -> x0, other arithmetic: 2.85 us -> none  [the longest x6 2.54 us: padded_2(): block = jnp.concatenate([low, block, high], axis=dim)]
  transfers between devices with their start and end apart: 13 -> 7, of which waited for: 13 -> 7; matrix products, arithmetic and copies ran while one was open for 0% -> 0% of each run, Pallas kernels for 0% -> 0%
where the time goes in v2:
time: 96.2 us; the launch traced here: 95.7 us
  waiting for transfers between devices  52.2 us (54%)
  starting transfers between devices  19.1 us (20%)
  Pallas kernels  13.2 us (14%)
  local copies, waits for them, and re-layouts  8.11 us (8%)
  between operations  2.08 us (2%)
  other arithmetic  1.04 us (1%)
    ppermute x6, waiting for transfers between devices, passed_along(): return lax.ppermute(block, axis, route)  50.3 us
    ppermute x6, starting transfers between devices, passed_along(): return lax.ppermute(block, axis, route)  18.5 us
    pallas_call x4, Pallas kernels, called(): pl.pallas_call(kernel, out_shape=[jax.ShapeDtypeStruct(shape, jnp.float32...  13.2 us
    unnamed x22, local copies, waits for them, and re-layouts  6.93 us
  transfers between devices with their start and end apart: 7, of which 7 were waited for; matrix products, arithmetic and copies ran while one was open for 0% of the time, Pallas kernels for 0%

profile of v2, /device:TPU:13, one launch (start us, length us, event | category | flops | bytes accessed | tf_op | source)
XLA Modules:
  0.0 95.7 jit_solution(7792722470639667911)
XLA Ops:
  0.0 0.0 copy-start.9
  0.0 0.7 copy-done.9
  0.7 0.6 dynamic_slice.6
  2.5 0.0 copy-start.10
  3.2 0.0 copy-done.10
  3.2 0.6 dynamic_slice.7.amp_ref
  3.8 0.0 copy-start.7
  3.8 0.0 copy-start.8
  3.8 0.7 copy-done.7
  4.5 0.0 copy-done.8
  4.5 0.0 copy-start
  4.5 1.1 %copy-done = f32[1,6,2,64,256]{4,3,2,1,0:T(8,128)S(1)} copy-done((f32[1,6,2,64,256]{4,3,2,1,0:T(8,128)S(1)}, f32[1,6,2,64,256]{4,3,2,1,0:T(8,128)}, u32[]{:S(2)}) %copy-start) | copy-done | bytes 786456
  5.6 0.0 copy-start.5
  5.6 0.9 copy-done.5
  6.5 0.0 copy-start.6
  6.5 0.9 copy-done.6
  7.4 0.0 copy-start.1
  7.4 3.0 %shard_map.73 = (f32[2,2,64,256]{3,2,1,0:T(8,128)S(1)}, f32[3,2,64,256]{3,2,1,0:T(8,128)S(1)}, f32[3,2,64,256]{3,2,1,0:T(8,128)S(1)}, f32[7,64,256]{2,1,0:T(8,12...) custom-call(f32[8]{0:T(128)S(1)} %copy-done.7, f32[8]{0:T(128)S(1)} %copy-done.8, f32[1]{0:T(128)} %dynamic_slice.7.amp_ref, ...), custom_call_target="tpu_custom_call" | custom-call | tf_op jit(solution)/shard_map/pallas_call | solution.py:371
  10.4 0.0 copy-start.4
  10.4 0.9 copy-done.4
  11.3 3.1 %collective-permute-start = (f32[7,64,256]{2,1,0:T(8,128)}, f32[7,64,256]{2,1,0:T(8,128)S(1)}, u32[]{:S(2)}, u32[]{:S(2)}) collective-permute-start(f32[7,64,256]{2,1,0:T(8,128)} %get-tuple-element.26), channel_id=1, source_target_pairs={{0,1},{1,2},{2,3},{3,4},{4,5},{5,6},{6,7},{7,8},{8,9},{9,10},{10,1... | collective-permute-start | bytes 1376264 | tf_op jit(solution)/shard_map/ppermute | solution.py:24
  14.4 3.1 %collective-permute-start.1 = (f32[7,64,256]{2,1,0:T(8,128)S(1)}, f32[7,64,256]{2,1,0:T(8,128)S(1)}, u32[]{:S(2)}, u32[]{:S(2)}) collective-permute-start(f32[7,64,256]{2,1,0:T(8,128)S(1)} %get-tuple-element.27), channel_id=1, source_target_pairs={{1,0},{2,1},{3,2},{4,3},{5,4},{6,5},{7,6},{8,7},{9,8},{10,9},{11,1... | collective-permute-start | bytes 1376264 | tf_op jit(solution)/shard_map/ppermute | solution.py:24
  17.5 8.2 %collective-permute-done.low = f32[7,64,256]{2,1,0:T(8,128)S(1)} collective-permute-done((f32[7,64,256]{2,1,0:T(8,128)}, f32[7,64,256]{2,1,0:T(8,128)S(1)}, u32[]{:S(2)}, u32[]{:S(2)}) %collective-permute-start) | collective-permute-done | bytes 458784 | tf_op jit(solution)/shard_map/ppermute | solution.py:24
  25.7 10.8 %collective-permute-done.1.high = f32[7,64,256]{2,1,0:T(8,128)S(1)} collective-permute-done((f32[7,64,256]{2,1,0:T(8,128)S(1)}, f32[7,64,256]{2,1,0:T(8,128)S(1)}, u32[]{:S(2)}, u32[]{:S(2)}) %collective-permute-start.1) | collective-permute-done | bytes 458784 | tf_op jit(solution)/shard_map/ppermute | solution.py:24
  36.5 0.0 copy-done.1
  36.5 3.7 %shard_map.74 = (f32[6,2,64,256]{3,2,1,0:T(8,128)S(1)}, f32[3,2,64,256]{3,2,1,0:T(8,128)S(1)}, f32[6,64,256]{2,1,0:T(8,128)S(1)}, f32[6,64,256]{2,1,0:T(8,128)S(1)}, f32[2,6,64,256]{3,2,1,0:T(8,128)S(1)}) custom-call(f32[8]{0:T(128)S(1)} %copy-done.7, f32[8]{0:T(128)S(1)} %copy-done.8, s32[1]{0:T(128)} %bitcast.first_ref, f32[6,2,64,256]{3,2,1,0:T(8,128)S(1)} %bitcast.11, ...), custom_call_target="tpu_custom_call" | custom-call | tf_op jit(solution)/shard_map/pallas_call | solution.py:371
  40.3 0.0 copy-start.2
  40.3 0.9 copy-done.2
  41.1 0.0 copy-start.3
  41.1 0.9 copy-done.3
  42.0 1.9 %collective-permute-start.2 = (f32[6,64,256]{2,1,0:T(8,128)S(1)}, f32[6,64,256]{2,1,0:T(8,128)S(1)}, u32[]{:S(2)}, u32[]{:S(2)}) collective-permute-start(f32[6,64,256]{2,1,0:T(8,128)S(1)} %get-tuple-element.31), channel_id=1, source_target_pairs={{0,1},{1,2},{2,3},{3,4},{4,5},{5,6},{6,7},{7,8},{8,9},{9,10},{10,1... | collective-permute-start | bytes 1179656 | tf_op jit(solution)/shard_map/ppermute | solution.py:24
  43.9 4.3 %collective-permute-start.3 = (f32[6,64,256]{2,1,0:T(8,128)S(1)}, f32[6,64,256]{2,1,0:T(8,128)S(1)}, u32[]{:S(2)}, u32[]{:S(2)}) collective-permute-start(f32[6,64,256]{2,1,0:T(8,128)S(1)} %get-tuple-element.32), channel_id=1, source_target_pairs={{1,0},{2,1},{3,2},{4,3},{5,4},{6,5},{7,6},{8,7},{9,8},{10,9},{11,1... | collective-permute-start | bytes 1179656 | tf_op jit(solution)/shard_map/ppermute | solution.py:24
  48.2 6.8 %collective-permute-done.2.low = f32[6,64,256]{2,1,0:T(8,128)S(1)} collective-permute-done((f32[6,64,256]{2,1,0:T(8,128)S(1)}, f32[6,64,256]{2,1,0:T(8,128)S(1)}, u32[]{:S(2)}, u32[]{:S(2)}) %collective-permute-start.2) | collective-permute-done | bytes 393248 | tf_op jit(solution)/shard_map/ppermute | solution.py:24
  55.0 8.3 %collective-permute-done.3.high = f32[6,64,256]{2,1,0:T(8,128)S(1)} collective-permute-done((f32[6,64,256]{2,1,0:T(8,128)S(1)}, f32[6,64,256]{2,1,0:T(8,128)S(1)}, u32[]{:S(2)}, u32[]{:S(2)}) %collective-permute-start.3) | collective-permute-done | bytes 393248 | tf_op jit(solution)/shard_map/ppermute | solution.py:24
  63.3 4.2 %shard_map.75 = (f32[6,2,64,256]{3,2,1,0:T(8,128)S(1)}, f32[3,2,64,256]{3,2,1,0:T(8,128)S(1)}, f32[6,64,256]{2,1,0:T(8,128)S(1)}, f32[6,64,256]{2,1,0:T(8,128)S(...) custom-call(f32[8]{0:T(128)S(1)} %copy-done.7, f32[8]{0:T(128)S(1)} %copy-done.8, s32[1]{0:T(128)} %bitcast.first_ref, ...), custom_call_target="tpu_custom_call" | custom-call | tf_op jit(solution)/shard_map/pallas_call | solution.py:371
  67.5 1.9 %collective-permute-start.4 = (f32[6,64,256]{2,1,0:T(8,128)S(1)}, f32[6,64,256]{2,1,0:T(8,128)S(1)}, u32[]{:S(2)}, u32[]{:S(2)}) collective-permute-start(f32[6,64,256]{2,1,0:T(8,128)S(1)} %get-tuple-element.37), channel_id=1, source_target_pairs={{0,1},{1,2},{2,3},{3,4},{4,5},{5,6},{6,7},{7,8},{8,9},{9,10},{10,1... | collective-permute-start | bytes 1179656 | tf_op jit(solution)/shard_map/ppermute | solution.py:24
  69.4 4.3 %collective-permute-start.5 = (f32[6,64,256]{2,1,0:T(8,128)S(1)}, f32[6,64,256]{2,1,0:T(8,128)S(1)}, u32[]{:S(2)}, u32[]{:S(2)}) collective-permute-start(f32[6,64,256]{2,1,0:T(8,128)S(1)} %get-tuple-element.38), channel_id=1, source_target_pairs={{1,0},{2,1},{3,2},{4,3},{5,4},{6,5},{7,6},{8,7},{9,8},{10,9},{11,1... | collective-permute-start | bytes 1179656 | tf_op jit(solution)/shard_map/ppermute | solution.py:24
  73.7 6.8 %collective-permute-done.4.low = f32[6,64,256]{2,1,0:T(8,128)S(1)} collective-permute-done((f32[6,64,256]{2,1,0:T(8,128)S(1)}, f32[6,64,256]{2,1,0:T(8,128)S(1)}, u32[]{:S(2)}, u32[]{:S(2)}) %collective-permute-start.4) | collective-permute-done | bytes 393248 | tf_op jit(solution)/shard_map/ppermute | solution.py:24
  80.5 9.4 %collective-permute-done.5.high = f32[6,64,256]{2,1,0:T(8,128)S(1)} collective-permute-done((f32[6,64,256]{2,1,0:T(8,128)S(1)}, f32[6,64,256]{2,1,0:T(8,128)S(1)}, u32[]{:S(2)}, u32[]{:S(2)}) %collective-permute-start.5) | collective-permute-done | bytes 393248 | tf_op jit(solution)/shard_map/ppermute | solution.py:24
  89.9 2.3 %shard_map.76 = f32[6,2,64,256]{3,2,1,0:T(8,128)S(1)} custom-call(f32[8]{0:T(128)S(1)} %copy-done.7, f32[8]{0:T(128)S(1)} %copy-done.8, f32[6,2,64,256]{3,2,1,0:T(8,128)S(1)} %get-tuple-element.34.state, f32[2,2,64,256]{3,2,1,0:T(8,128)S(1)} %get-tuple-element.22.moduli, f32[3,2,64,256]{3,2,1,0:T(8,128)S(1)} %get-tuple-element.35.part, ...), custom_call_target="tpu_custom_call" | custom-call | tf_op jit(solution)/shard_map/pallas_call | solution.py:371
  92.2 0.6 collective-permute-start.6
  92.8 1.9 %collective-permute-done.6 = f32[6,2,64,256]{3,2,1,0:T(8,128)S(1)} collective-permute-done((f32[6,2,64,256]{3,2,1,0:T(8,128)S(1)}, f32[6,2,64,256]{3,2,1,0:T(8,128)S(1)}, u32[]{:S(2)}, u32[]{:S(2)}) %collective-permute-start.6) | collective-permute-done | bytes 786464 | tf_op jit(solution)/shard_map/ppermute | solution.py:429
  94.7 1.0 %add_bitcast_fusion = f32[1,6,2,64,256]{4,3,2,1,0:T(8,128)} fusion(f32[6,2,64,256]{3,2,1,0:T(8,128)S(1)} %collective-permute-done.6, f32[6,2,64,256]{3,2,1,0:T(8,128)S(1)} %get-tuple-element.33, f32[6,2,64,256]{3,2,1,0:T(8,128)S(1)} %shard_map.76, pred[]{:T(512)S(6)} %eq.3), kind=kLoop, calls=%fused_computation | loop fusion | flops 786432 | bytes 3145729 | tf_op jit(solution)/shard_map/broadcast_in_dim | solution.py:431
  (2 shorter events, 0.0 us)
Async XLA Ops:
  0.0 0.7 copy-start.9
  2.5 0.7 copy-start.10
  3.8 0.7 copy-start.7
  3.8 0.7 copy-start.8
  4.5 1.1 %copy-start = (f32[1,6,2,64,256]{4,3,2,1,0:T(8,128)S(1)}, f32[1,6,2,64,256]{4,3,2,1,0:T(8,128)}, u32[]{:S(2)}) copy-start(f32[1,6,2,64,256]{4,3,2,1,0:T(8,128)} %param.7) | copy-start | bytes 2359300
  5.6 0.9 copy-start.5
  6.5 0.9 copy-start.6
  7.4 29.1 %copy-start.1 = (f32[1,6,2,64,256]{4,3,2,1,0:T(8,128)S(1)}, f32[1,6,2,64,256]{4,3,2,1,0:T(8,128)}, u32[]{:S(2)}) copy-start(f32[1,6,2,64,256]{4,3,2,1,0:T(8,128)} %param.7) | copy-start | bytes 2359300
  10.4 0.9 copy-start.4
  11.3 14.4 %collective-permute-start = (f32[7,64,256]{2,1,0:T(8,128)}, f32[7,64,256]{2,1,0:T(8,128)S(1)}, u32[]{:S(2)}, u32[]{:S(2)}) collective-permute-start(f32[7,64,256]{2,1,0:T(8,128)} %get-tuple-element.26), channel_id=1, source_target_pairs={{0,1},{1,2},{2,3},{3,4},{4,5},{5,6},{6,7},{7,8},{8,9},{9,10},{10,1... | collective-permute-start | bytes 1376264 | tf_op jit(solution)/shard_map/ppermute | solution.py:24
  14.4 22.1 %collective-permute-start.1 = (f32[7,64,256]{2,1,0:T(8,128)S(1)}, f32[7,64,256]{2,1,0:T(8,128)S(1)}, u32[]{:S(2)}, u32[]{:S(2)}) collective-permute-start(f32[7,64,256]{2,1,0:T(8,128)S(1)} %get-tuple-element.27), channel_id=1, source_target_pairs={{1,0},{2,1},{3,2},{4,3},{5,4},{6,5},{7,6},{8,7},{9,8},{10,9},{11,1... | collective-permute-start | bytes 1376264 | tf_op jit(solution)/shard_map/ppermute | solution.py:24
  40.3 0.9 copy-start.2
  41.1 0.9 copy-start.3
  42.0 13.0 %collective-permute-start.2 = (f32[6,64,256]{2,1,0:T(8,128)S(1)}, f32[6,64,256]{2,1,0:T(8,128)S(1)}, u32[]{:S(2)}, u32[]{:S(2)}) collective-permute-start(f32[6,64,256]{2,1,0:T(8,128)S(1)} %get-tuple-element.31), channel_id=1, source_target_pairs={{0,1},{1,2},{2,3},{3,4},{4,5},{5,6},{6,7},{7,8},{8,9},{9,10},{10,1... | collective-permute-start | bytes 1179656 | tf_op jit(solution)/shard_map/ppermute | solution.py:24
  43.9 19.3 %collective-permute-start.3 = (f32[6,64,256]{2,1,0:T(8,128)S(1)}, f32[6,64,256]{2,1,0:T(8,128)S(1)}, u32[]{:S(2)}, u32[]{:S(2)}) collective-permute-start(f32[6,64,256]{2,1,0:T(8,128)S(1)} %get-tuple-element.32), channel_id=1, source_target_pairs={{1,0},{2,1},{3,2},{4,3},{5,4},{6,5},{7,6},{8,7},{9,8},{10,9},{11,1... | collective-permute-start | bytes 1179656 | tf_op jit(solution)/shard_map/ppermute | solution.py:24
  67.5 13.0 %collective-permute-start.4 = (f32[6,64,256]{2,1,0:T(8,128)S(1)}, f32[6,64,256]{2,1,0:T(8,128)S(1)}, u32[]{:S(2)}, u32[]{:S(2)}) collective-permute-start(f32[6,64,256]{2,1,0:T(8,128)S(1)} %get-tuple-element.37), channel_id=1, source_target_pairs={{0,1},{1,2},{2,3},{3,4},{4,5},{5,6},{6,7},{7,8},{8,9},{9,10},{10,1... | collective-permute-start | bytes 1179656 | tf_op jit(solution)/shard_map/ppermute | solution.py:24
  69.4 20.5 %collective-permute-start.5 = (f32[6,64,256]{2,1,0:T(8,128)S(1)}, f32[6,64,256]{2,1,0:T(8,128)S(1)}, u32[]{:S(2)}, u32[]{:S(2)}) collective-permute-start(f32[6,64,256]{2,1,0:T(8,128)S(1)} %get-tuple-element.38), channel_id=1, source_target_pairs={{1,0},{2,1},{3,2},{4,3},{5,4},{6,5},{7,6},{8,7},{9,8},{10,9},{11,1... | collective-permute-start | bytes 1179656 | tf_op jit(solution)/shard_map/ppermute | solution.py:24
  92.2 2.5 %collective-permute-start.6 = (f32[6,2,64,256]{3,2,1,0:T(8,128)S(1)}, f32[6,2,64,256]{3,2,1,0:T(8,128)S(1)}, u32[]{:S(2)}, u32[]{:S(2)}) collective-permute-start(f32[6,2,64,256]{3,2,1,0:T(8,128)S(1)} %shard_map.76), channel_id=1, source_target_pairs={{0,16},{16,0},{1,17},{17,1},{2,18},{18,2},{3,19},{19,3},{4,20},{20... | collective-permute-start | bytes 2359304 | tf_op jit(solution)/shard_map/ppermute | solution.py:429

commit v3 on v2

v3 whole, which is shorter than its diff:
```python
import functools

import jax
import jax.numpy as jnp
from jax import lax
from jax.experimental import pallas as pl
from jax.experimental.pallas import tpu as pltpu
from jax.sharding import PartitionSpec as P

FINE = 4
COARSE = 2


DT_FINE = 0.18
DT_COARSE = 0.36


def passed_along(block, axis, distance):
    devices = range(lax.axis_size(axis))
    route = [(i - distance, i) for i in devices if i - distance in devices]
    return lax.ppermute(block, axis, route)


class Inplane:
    def __init__(self, u):
        rows, columns = u[0].shape
        row = lax.broadcasted_iota(jnp.int32, (rows, columns), 0)
        column = lax.broadcasted_iota(jnp.int32, (rows, columns), 1)

        def shifted(f, axis, up):
            if up:
                edge = (row == rows - 1, column == columns - 1)[axis]
                return jnp.where(edge, 0.0, pltpu.roll(f, f.shape[axis] - 1, axis))
            edge = (row == 0, column == 0)[axis]
            return jnp.where(edge, 0.0, pltpu.roll(f, 1, axis))

        self.u = u
        self.shifted = shifted
        plus = [shifted(f, 1, True) for f in u]
        minus = [shifted(f, 1, False) for f in u]
        self.sum_x = [a + b for a, b in zip(plus, minus)]
        self.diff_x = [a - b for a, b in zip(plus, minus)]
        self.up_y = [None, shifted(u[1], 0, True), shifted(u[2], 0, True)]
        self.down_y = [None, shifted(u[1], 0, False), shifted(u[2], 0, False)]
        self.even = []
        for f, s in zip(u, self.sum_x):
            across = s + 3.0 * f
            square = shifted(across, 0, True) + shifted(across, 0, False) + 3.0 * across
            self.even.append((square + 5.0 * f) * (1.0 / 30.0))
        self.odd = [
            0.25 * self.diff_x[2],
            0.25 * (self.up_y[2] - self.down_y[2]),
            0.25 * (self.diff_x[0] + (self.up_y[1] - self.down_y[1])),
        ]

    def own(self):
        u, shifted = self.u, self.shifted
        up_x, down_x = shifted(u[0], 0, True), shifted(u[0], 0, False)
        sum_y = [up_x + down_x, self.up_y[1] + self.down_y[1], self.up_y[2] + self.down_y[2]]
        shear = [
            3.0 * e + (s + t) * (1.0 / 6.0) - (17.0 / 3.0) * f
            for e, s, t, f in zip(self.even, self.sum_x, sum_y, u)
        ]
        cross = [
            0.25 * (shifted(d, 0, True) - shifted(d, 0, False)) for d in self.diff_x[:2]
        ]
        bulk = [
            self.sum_x[0] - 2.0 * u[0] + cross[1],
            sum_y[1] - 2.0 * u[1] + cross[0],
            -2.0 * u[2],
        ]
        return shear, bulk


def towards(plane_sums, sign):
    odd = [sign * f for f in plane_sums[3:6]]
    return plane_sums[:3], [odd[0], odd[1], odd[2] + plane_sums[6]]


def sums_of(inplane):
    return (*inplane.even, *inplane.odd, inplane.u[2])


def partial_step(planes, velocity, shear, bulk, load, step):
    count = len(planes)
    outgoing = [sums_of(p) for p in planes]
    velocities, displaced = [], []
    for z, plane in enumerate(planes):
        even, other = plane.own()
        for neighbour, sign in ((z - 1, -1.0), (z + 1, 1.0)):
            if 0 <= neighbour < count:
                e, o = towards(outgoing[neighbour], sign)
                even = [a + b for a, b in zip(even, e)]
                other = [a + b for a, b in zip(other, o)]
        v = [
            velocity(c, z) + step * (shear(z) * even[c] + bulk(z) * other[c] + load(c, z))
            for c in range(3)
        ]
        velocities.append(v)
        displaced.append([plane.u[c] + step * v[c] for c in range(3)])
    return velocities, displaced, outgoing


def prepare(planes, velocity, shear, bulk, load, step, part_ref, up_ref, down_ref, rim_ref):
    count = len(planes)
    velocities, displaced, outgoing = partial_step(planes, velocity, shear, bulk, load, step)
    for z in range(count):
        for c in range(3):
            part_ref[c, z] = velocities[z][c]
    for c in range(3):
        down_ref[c] = planes[0].u[c]
        down_ref[3 + c] = displaced[0][c]
        up_ref[c] = planes[count - 1].u[c]
        up_ref[3 + c] = displaced[count - 1][c]
    for c in range(6):
        rim_ref[0, c] = outgoing[0][c]
        rim_ref[1, c] = outgoing[count - 1][c]


def zone_values(zone, shear_table, lame_table, offset):
    shear = jnp.zeros(zone.shape, jnp.float32)
    bulk = jnp.zeros(zone.shape, jnp.float32)
    for k in range(shear_table.shape[0]):
        hit = zone == k + offset
        shear = jnp.where(hit, shear_table[k], shear)
        bulk = jnp.where(hit, shear_table[k] + lame_table[k], bulk)
    return shear, bulk


def open_kernel(
    step, state_hbm, load_hbm, zones_hbm, shear_hbm, lame_hbm, amp_hbm, cycle_hbm,
    moduli, loading, part, up, down, rim,
    state, load_shape, zones, shear_table, lame_table, amp_table, cycle_index, arrived,
):
    pairs = (
        (state_hbm.at[0], state), (cycle_hbm, cycle_index), (amp_hbm, amp_table),
        (shear_hbm, shear_table), (lame_hbm, lame_table), (zones_hbm, zones),
        (load_hbm, load_shape),
    )
    copies = [
        pltpu.make_async_copy(source, target, arrived.at[i])
        for i, (source, target) in enumerate(pairs)
    ]
    for copy in copies:
        copy.start()
    for copy in copies:
        copy.wait()
    count = zones.shape[0]
    amplitude = amp_table[cycle_index[lax.axis_index("win")]]
    for z in range(count):
        moduli[0, z], moduli[1, z] = zone_values(zones[z], shear_table, lame_table, 0)
        for c in range(3):
            loading[c, z] = amplitude * load_shape[c, z].astype(jnp.float32)
    planes = [Inplane([state[c, z] for c in range(3)]) for z in range(count)]
    prepare(
        planes,
        lambda c, z: state[3 + c, z],
        lambda z: moduli[0, z],
        lambda z: moduli[1, z],
        lambda c, z: loading[c, z],
        step, part, up, down, rim,
    )
    down[6] = (zones[0] + 1).astype(jnp.float32)
    up[6] = (zones[count - 1] + 1).astype(jnp.float32)


def two_steps(step, u0, part, rim, low, high, moduli, edges, load):
    count = moduli.shape[1]
    square = step * step
    sides = ((low, 0, 0, -1.0), (high, 1, count - 1, 1.0))
    velocities = [[part[c, z] for c in range(3)] for z in range(count)]
    outer = []
    for side, (got, edge, z, sign) in enumerate(sides):
        there = Inplane([got[c] for c in range(3)])
        even, odd = towards(sums_of(there), sign)
        for c in range(3):
            velocities[z][c] = velocities[z][c] + step * (
                moduli[0, z] * even[c] + moduli[1, z] * odd[c]
            )
        here = tuple(rim[side, c] for c in range(6)) + (u0[2, z],)
        even, odd = towards(here, -sign)
        outer.append(
            [
                got[3 + c] + square * (edges[2 * side] * even[c] + edges[2 * side + 1] * odd[c])
                for c in range(3)
            ]
        )
    planes = [
        Inplane([u0[c, z] + step * velocities[z][c] for c in range(3)]) for z in range(count)
    ]
    shear = lambda z: moduli[0, z]
    bulk = lambda z: moduli[1, z]
    ends, _, _ = partial_step(planes, lambda c, z: velocities[z][c], shear, bulk, load, step)
    for side, (got, edge, z, sign) in enumerate(sides):
        even, odd = towards(sums_of(Inplane(outer[side])), sign)
        for c in range(3):
            ends[z][c] = ends[z][c] + step * (shear(z) * even[c] + bulk(z) * odd[c])
    displaced = [[planes[z].u[c] + step * ends[z][c] for c in range(3)] for z in range(count)]
    return ends, displaced


def fine_kernel(
    step, turn, last, *refs
):
    if turn == 0:
        shear_table, lame_table, *refs = refs
    else:
        edges, *refs = refs
    start, state, moduli, loading, part, rim, low, high, *outs = refs
    if turn == 0:
        *outs, edges = outs
        edges[0], edges[1] = zone_values(low[6], shear_table, lame_table, 1.0)
        edges[2], edges[3] = zone_values(high[6], shear_table, lame_table, 1.0)
    count = moduli.shape[1]
    ends, displaced = two_steps(
        step, state, part, rim, low, high, moduli, edges, lambda c, z: loading[c, z]
    )
    new_state, next_part, up, down, next_rim = outs[:5]
    for z in range(count):
        for c in range(3):
            new_state[c, z] = displaced[z][c]
            new_state[3 + c, z] = ends[z][c]
    if last:
        entry = outs[5]
        first = lax.axis_index("win") == 0
        for z in range(count):
            for c in range(6):
                entry[c, z] = jnp.where(first, new_state[c, z], start[c, z])
        next_step, load = DT_COARSE, lambda c, z: 0.0
    else:
        entry = new_state
        next_step, load = step, lambda c, z: loading[c, z]
    planes = [Inplane([entry[c, z] for c in range(3)]) for z in range(count)]
    prepare(
        planes, lambda c, z: entry[3 + c, z], lambda z: moduli[0, z], lambda z: moduli[1, z],
        load, next_step, next_part, up, down, next_rim,
    )


def coarse_open_kernel(state, moduli, part, up, down, rim):
    count = moduli.shape[1]
    planes = [Inplane([state[c, z] for c in range(3)]) for z in range(count)]
    prepare(
        planes, lambda c, z: state[3 + c, z], lambda z: moduli[0, z], lambda z: moduli[1, z],
        lambda c, z: 0.0, DT_COARSE, part, up, down, rim,
    )


def coarse_kernel(edges, state, moduli, part, rim, low, high, new_state):
    ends, displaced = two_steps(
        DT_COARSE, state, part, rim, low, high, moduli, edges, lambda c, z: 0.0
    )
    for z in range(moduli.shape[1]):
        for c in range(3):
            new_state[c, z] = displaced[z][c]
            new_state[3 + c, z] = ends[z][c]


VMEM = pl.BlockSpec(memory_space=pltpu.VMEM)
SMEM = pl.BlockSpec(memory_space=pltpu.SMEM)
HBM = pl.BlockSpec(memory_space=pltpu.HBM)


def called(kernel, outs, *operands, scalars=0, specs=None, scratch=()):
    return pl.pallas_call(
        kernel,
        out_shape=[jax.ShapeDtypeStruct(shape, jnp.float32) for shape in outs],
        in_specs=specs or [SMEM] * scalars + [VMEM] * (len(operands) - scalars),
        out_specs=[VMEM] * len(outs),
        scratch_shapes=list(scratch),
        compiler_params=pltpu.CompilerParams(vmem_limit_bytes=16 * 1024 * 1024),
    )(*operands)


def exchanged(up, down):
    return passed_along(up, "slab", 1), passed_along(down, "slab", -1)


def shards(states, load_shape, zone_ids, zone_shear, zone_lame, amp_table, cycle_index):
    windows = lax.axis_size("win")
    first = lax.axis_index("win") == 0
    start = states[0]
    count, rows, columns = zone_ids.shape
    plane = (rows, columns)
    field, state = (3, count, *plane), (6, count, *plane)
    message, rims = (6, *plane), (2, 6, *plane)

    given = (states, load_shape, zone_ids, zone_shear, zone_lame, amp_table, cycle_index)
    moduli, loading, part, up, down, rim = called(
        functools.partial(open_kernel, DT_FINE),
        [(2, count, *plane), field, field, (7, *plane), (7, *plane), rims],
        *given,
        specs=[HBM] * len(given),
        scratch=[
            pltpu.VMEM(state, states.dtype),
            pltpu.VMEM(load_shape.shape, load_shape.dtype),
            pltpu.VMEM(zone_ids.shape, zone_ids.dtype),
            *[pltpu.SMEM(table.shape, table.dtype) for table in given[3:]],
            pltpu.SemaphoreType.DMA((len(given),)),
        ],
    )
    low, high = exchanged(up, down)
    current, edges = start, None
    for turn in range(FINE // 2):
        last = turn == FINE // 2 - 1
        outs = [state, field, message, message, rims]
        outs += ([state] if last else []) + ([(4, *plane)] if turn == 0 else [])
        tables = (zone_shear, zone_lame) if turn == 0 else (edges,)
        current, part, up, down, rim, *more = called(
            functools.partial(fine_kernel, DT_FINE, turn, last), outs,
            *tables, start, current, moduli, loading, part, rim, low, high,
            scalars=2 if turn == 0 else 0,
        )
        if turn == 0:
            edges = more.pop()
        low, high = exchanged(up, down)
    fine_end, entry = current, more[0]

    def coarse_end(status, part, rim, low, high):
        return called(coarse_kernel, [state], edges, status, moduli, part, rim, low, high)[0]

    advanced = coarse_end(entry, part, rim, low, high)
    correction = fine_end - jnp.where(first, 0.0, advanced)
    for _ in range(windows - 2):
        status = correction + passed_along(advanced, "win", 1)
        part, up, down, rim = called(
            coarse_open_kernel, [field, message, message, rims], status, moduli
        )
        advanced = coarse_end(status, part, rim, *exchanged(up, down))
    everyone = lax.ppermute(advanced, "win", [(i, (i + 1) % windows) for i in range(windows)])
    new_end = correction + jnp.where(first, 0.0, everyone)
    return new_end[None]


def solution(mesh):
    placed = (
        P("win", None, "slab", None, None),
        P(None, "slab", None, None),
        P("slab", None, None),
        P(),
        P(),
        P(),
        P(),
    )

    return jax.shard_map(
        shards,
        mesh=mesh,
        in_specs=placed,
        out_specs=P("win", None, "slab", None, None),
        check_vma=False,
    )
```

time: 96.2 us -> 87.7 us (0.912)
  Pallas kernels: 13.2 us -> 8.85 us
  between operations: 2.08 us -> 0.09 us
  local copies, waits for them, and re-layouts: 8.11 us -> 6.25 us
    pallas_call x4, Pallas kernels: 13.2 us -> 8.85 us  [called(): pl.pallas_call(kernel, out_shape=[jax.ShapeDtypeStruct(shape, jnp.float32...]
    dynamic_slice x2 -> x0, local copies, waits for them, and re-layouts: 1.17 us -> none  [shards(): amplitude = amp_table[cycle_index[window_index]].reshape(1)]
    unnamed x22 -> x18, local copies, waits for them, and re-layouts: 6.93 us -> 6.25 us
where the time goes in v3:
time: 87.7 us; the launch traced here: 87.3 us
  waiting for transfers between devices  52 us (59%)
  starting transfers between devices  19.1 us (22%)
  Pallas kernels  8.85 us (10%)
  local copies, waits for them, and re-layouts  6.25 us (7%)
  other arithmetic  1.05 us (1%)
    ppermute x6, waiting for transfers between devices, passed_along(): return lax.ppermute(block, axis, route)  50.1 us
    ppermute x6, starting transfers between devices, passed_along(): return lax.ppermute(block, axis, route)  18.5 us
    pallas_call x4, Pallas kernels, called(): pl.pallas_call(kernel, out_shape=[jax.ShapeDtypeStruct(shape, jnp.float32...  8.85 us
    unnamed x18, local copies, waits for them, and re-layouts  6.25 us
    ppermute x1, waiting for transfers between devices, shards(): lax.ppermute(advanced, 'win', [(i, (i + 1) % windows) for i in range(wind...  1.91 us
  transfers between devices with their start and end apart: 7, of which 7 were waited for; matrix products, arithmetic and copies ran while one was open for 0% of the time, Pallas kernels for 0%

profile of v3, /device:TPU:13, one launch (start us, length us, event | category | flops | bytes accessed | tf_op | source)
XLA Modules:
  0.0 87.3 jit_solution(13257342072863205826)
XLA Ops:
  0.0 0.0 copy-start
  0.0 1.1 %copy-done = f32[1,6,2,64,256]{4,3,2,1,0:T(8,128)S(1)} copy-done((f32[1,6,2,64,256]{4,3,2,1,0:T(8,128)S(1)}, f32[1,6,2,64,256]{4,3,2,1,0:T(8,128)}, u32[]{:S(2)}) %copy-start) | copy-done | bytes 786456
  1.1 0.0 copy-start.1
  1.1 0.9 %copy-done.1 = bf16[3,2,64,256]{3,2,1,0:T(8,128)(2,1)S(1)} copy-done((bf16[3,2,64,256]{3,2,1,0:T(8,128)(2,1)S(1)}, bf16[3,2,64,256]{3,2,1,0:T(8,128)(2,1)}, u32[]{:S(2)}) %copy-start.1) | copy-done | bytes 196632
  2.1 0.0 copy-start.2
  2.1 0.9 %copy-done.2 = s32[2,64,256]{2,1,0:T(8,128)S(1)} copy-done((s32[2,64,256]{2,1,0:T(8,128)S(1)}, s32[2,64,256]{2,1,0:T(8,128)}, u32[]{:S(2)}) %copy-start.2) | copy-done | bytes 131096
  3.0 0.0 copy-start.3
  3.0 0.7 copy-done.3
  3.6 0.0 copy-start.5
  3.6 0.7 copy-done.5
  4.3 0.0 copy-start.7
  4.3 0.7 copy-done.7
  4.9 0.0 copy-start.8
  4.9 0.7 copy-done.8
  5.6 1.7 %shard_map.73 = (f32[2,2,64,256]{3,2,1,0:T(8,128)S(1)}, f32[3,2,64,256]{3,2,1,0:T(8,128)S(1)}, f32[3,2,64,256]{3,2,1,0:T(8,128)S(1)}, f32[7,64,256]{2,1,0:T(8,12...) custom-call(f32[1,6,2,64,256]{4,3,2,1,0:T(8,128)S(1)} %copy-done, ...), custom_call_target="tpu_custom_call" | custom-call | tf_op jit(solution)/shard_map/pallas_call | solution.py:265
  7.3 3.1 %collective-permute-start = (f32[7,64,256]{2,1,0:T(8,128)S(1)}, f32[7,64,256]{2,1,0:T(8,128)S(1)}, u32[]{:S(2)}, u32[]{:S(2)}) collective-permute-start(f32[7,64,256]{2,1,0:T(8,128)S(1)} %get-tuple-element.27), channel_id=1, source_target_pairs={{0,1},{1,2},{2,3},{3,4},{4,5},{5,6},{6,7},{7,8},{8,9},{9,10},{10,1... | collective-permute-start | bytes 1376264 | tf_op jit(solution)/shard_map/ppermute | solution.py:21
  10.4 3.1 %collective-permute-start.1 = (f32[7,64,256]{2,1,0:T(8,128)S(1)}, f32[7,64,256]{2,1,0:T(8,128)S(1)}, u32[]{:S(2)}, u32[]{:S(2)}) collective-permute-start(f32[7,64,256]{2,1,0:T(8,128)S(1)} %get-tuple-element.28), channel_id=1, source_target_pairs={{1,0},{2,1},{3,2},{4,3},{5,4},{6,5},{7,6},{8,7},{9,8},{10,9},{11,1... | collective-permute-start | bytes 1376264 | tf_op jit(solution)/shard_map/ppermute | solution.py:21
  13.5 8.0 %collective-permute-done.refs_8_ = f32[7,64,256]{2,1,0:T(8,128)S(1)} collective-permute-done((f32[7,64,256]{2,1,0:T(8,128)S(1)}, f32[7,64,256]{2,1,0:T(8,128)S(1)}, u32[]{:S(2)}, u32[]{:S(2)}) %collective-permute-start) | collective-permute-done | bytes 458784 | tf_op jit(solution)/shard_map/ppermute | solution.py:21
  21.4 10.8 %collective-permute-done.1.refs_9_ = f32[7,64,256]{2,1,0:T(8,128)S(1)} collective-permute-done((f32[7,64,256]{2,1,0:T(8,128)S(1)}, f32[7,64,256]{2,1,0:T(8,128)S(1)}, u32[]{:S(2)}, u32[]{:S(2)}) %collective-permute-start.1) | collective-permute-done | bytes 458784 | tf_op jit(solution)/shard_map/ppermute | solution.py:21
  32.3 0.0 copy-start.4
  32.3 0.0 copy-start.6
  32.3 0.7 copy-done.4
  32.9 0.0 copy-done.6
  33.0 3.1 %shard_map.74 = (f32[6,2,64,256]{3,2,1,0:T(8,128)S(1)}, f32[3,2,64,256]{3,2,1,0:T(8,128)S(1)}, f32[6,64,256]{2,1,0:T(8,128)S(1)}, f32[6,64,256]{2,1,0:T(8,128)S(...) custom-call(f32[8]{0:T(128)S(1)} %copy-done.4, f32[8]{0:T(128)S(1)} %copy-done.6, ...), custom_call_target="tpu_custom_call" | custom-call | tf_op jit(solution)/shard_map/pallas_call | solution.py:265
  36.0 1.9 %collective-permute-start.2 = (f32[6,64,256]{2,1,0:T(8,128)S(1)}, f32[6,64,256]{2,1,0:T(8,128)S(1)}, u32[]{:S(2)}, u32[]{:S(2)}) collective-permute-start(f32[6,64,256]{2,1,0:T(8,128)S(1)} %get-tuple-element.33), channel_id=1, source_target_pairs={{0,1},{1,2},{2,3},{3,4},{4,5},{5,6},{6,7},{7,8},{8,9},{9,10},{10,1... | collective-permute-start | bytes 1179656 | tf_op jit(solution)/shard_map/ppermute | solution.py:21
  38.0 4.3 %collective-permute-start.3 = (f32[6,64,256]{2,1,0:T(8,128)S(1)}, f32[6,64,256]{2,1,0:T(8,128)S(1)}, u32[]{:S(2)}, u32[]{:S(2)}) collective-permute-start(f32[6,64,256]{2,1,0:T(8,128)S(1)} %get-tuple-element.34), channel_id=1, source_target_pairs={{1,0},{2,1},{3,2},{4,3},{5,4},{6,5},{7,6},{8,7},{9,8},{10,9},{11,1... | collective-permute-start | bytes 1179656 | tf_op jit(solution)/shard_map/ppermute | solution.py:21
  42.2 6.8 %collective-permute-done.2.refs_7_ = f32[6,64,256]{2,1,0:T(8,128)S(1)} collective-permute-done((f32[6,64,256]{2,1,0:T(8,128)S(1)}, f32[6,64,256]{2,1,0:T(8,128)S(1)}, u32[]{:S(2)}, u32[]{:S(2)}) %collective-permute-start.2) | collective-permute-done | bytes 393248 | tf_op jit(solution)/shard_map/ppermute | solution.py:21
  49.0 8.3 %collective-permute-done.3.refs_8_ = f32[6,64,256]{2,1,0:T(8,128)S(1)} collective-permute-done((f32[6,64,256]{2,1,0:T(8,128)S(1)}, f32[6,64,256]{2,1,0:T(8,128)S(1)}, u32[]{:S(2)}, u32[]{:S(2)}) %collective-permute-start.3) | collective-permute-done | bytes 393248 | tf_op jit(solution)/shard_map/ppermute | solution.py:21
  57.3 2.4 %shard_map.75 = (f32[6,2,64,256]{3,2,1,0:T(8,128)S(1)}, f32[3,2,64,256]{3,2,1,0:T(8,128)S(1)}, f32[6,64,256]{2,1,0:T(8,128)S(1)}, f32[6,64,256]{2,1,0:T(8,128)S(...) custom-call(f32[4,64,256]{2,1,0:T(8,128)S(1)} %get-tuple-element.29.refs_0_.edges, ...), custom_call_target="tpu_custom_call" | custom-call | tf_op jit(solution)/shard_map/pallas_call | solution.py:265
  59.8 1.9 %collective-permute-start.4 = (f32[6,64,256]{2,1,0:T(8,128)S(1)}, f32[6,64,256]{2,1,0:T(8,128)S(1)}, u32[]{:S(2)}, u32[]{:S(2)}) collective-permute-start(f32[6,64,256]{2,1,0:T(8,128)S(1)} %get-tuple-element.39), channel_id=1, source_target_pairs={{0,1},{1,2},{2,3},{3,4},{4,5},{5,6},{6,7},{7,8},{8,9},{9,10},{10,1... | collective-permute-start | bytes 1179656 | tf_op jit(solution)/shard_map/ppermute | solution.py:21
  61.7 4.3 %collective-permute-start.5 = (f32[6,64,256]{2,1,0:T(8,128)S(1)}, f32[6,64,256]{2,1,0:T(8,128)S(1)}, u32[]{:S(2)}, u32[]{:S(2)}) collective-permute-start(f32[6,64,256]{2,1,0:T(8,128)S(1)} %get-tuple-element.40), channel_id=1, source_target_pairs={{1,0},{2,1},{3,2},{4,3},{5,4},{6,5},{7,6},{8,7},{9,8},{10,9},{11,1... | collective-permute-start | bytes 1179656 | tf_op jit(solution)/shard_map/ppermute | solution.py:21
  66.0 6.8 %collective-permute-done.4.low = f32[6,64,256]{2,1,0:T(8,128)S(1)} collective-permute-done((f32[6,64,256]{2,1,0:T(8,128)S(1)}, f32[6,64,256]{2,1,0:T(8,128)S(1)}, u32[]{:S(2)}, u32[]{:S(2)}) %collective-permute-start.4) | collective-permute-done | bytes 393248 | tf_op jit(solution)/shard_map/ppermute | solution.py:21
  72.7 9.4 %collective-permute-done.5.high = f32[6,64,256]{2,1,0:T(8,128)S(1)} collective-permute-done((f32[6,64,256]{2,1,0:T(8,128)S(1)}, f32[6,64,256]{2,1,0:T(8,128)S(1)}, u32[]{:S(2)}, u32[]{:S(2)}) %collective-permute-start.5) | collective-permute-done | bytes 393248 | tf_op jit(solution)/shard_map/ppermute | solution.py:21
  82.2 1.6 %shard_map.76 = f32[6,2,64,256]{3,2,1,0:T(8,128)S(1)} custom-call(f32[4,64,256]{2,1,0:T(8,128)S(1)} %get-tuple-element.29.refs_0_.edges, f32[6,2,64,256]{3,2,1,0:T(8,128)S(1)} %get-tuple-element.36.state, f32[2,2,64,256]{3,2,1,0:T(8,128)S(1)} %get-tuple-element.23.refs_4_.refs_3_.moduli, f32[3,2,64,256]{3,2,1,0:T(8,128)S(1)} %get-tuple-element.37.part, ...), custom_call_target="tpu_custom_call" | custom-call | tf_op jit(solution)/shard_map/pallas_call | solution.py:265
  83.8 0.6 collective-permute-start.6
  84.4 1.9 %collective-permute-done.6 = f32[6,2,64,256]{3,2,1,0:T(8,128)S(1)} collective-permute-done((f32[6,2,64,256]{3,2,1,0:T(8,128)S(1)}, f32[6,2,64,256]{3,2,1,0:T(8,128)S(1)}, u32[]{:S(2)}, u32[]{:S(2)}) %collective-permute-start.6) | collective-permute-done | bytes 786464 | tf_op jit(solution)/shard_map/ppermute | solution.py:330
  86.3 1.0 %add_bitcast_fusion = f32[1,6,2,64,256]{4,3,2,1,0:T(8,128)} fusion(f32[6,2,64,256]{3,2,1,0:T(8,128)S(1)} %collective-permute-done.6, f32[6,2,64,256]{3,2,1,0:T(8,128)S(1)} %get-tuple-element.35, f32[6,2,64,256]{3,2,1,0:T(8,128)S(1)} %shard_map.76, pred[]{:T(512)S(6)} %eq.3), kind=kLoop, calls=%fused_computation | loop fusion | flops 786432 | bytes 3145729 | tf_op jit(solution)/shard_map/broadcast_in_dim | solution.py:332
Async XLA Ops:
  0.0 1.1 %copy-start = (f32[1,6,2,64,256]{4,3,2,1,0:T(8,128)S(1)}, f32[1,6,2,64,256]{4,3,2,1,0:T(8,128)}, u32[]{:S(2)}) copy-start(f32[1,6,2,64,256]{4,3,2,1,0:T(8,128)} %state_hbm.1) | copy-start | bytes 2359300
  1.1 0.9 %copy-start.1 = (bf16[3,2,64,256]{3,2,1,0:T(8,128)(2,1)S(1)}, bf16[3,2,64,256]{3,2,1,0:T(8,128)(2,1)}, u32[]{:S(2)}) copy-start(bf16[3,2,64,256]{3,2,1,0:T(8,128)(2,1)} %load_hbm.1) | copy-start | bytes 589828
  2.1 0.9 %copy-start.2 = (s32[2,64,256]{2,1,0:T(8,128)S(1)}, s32[2,64,256]{2,1,0:T(8,128)}, u32[]{:S(2)}) copy-start(s32[2,64,256]{2,1,0:T(8,128)} %zones_hbm.1) | copy-start | bytes 393220
  3.0 0.7 copy-start.3
  3.6 0.7 copy-start.5
  4.3 0.7 copy-start.7
  4.9 0.7 copy-start.8
  7.3 14.2 %collective-permute-start = (f32[7,64,256]{2,1,0:T(8,128)S(1)}, f32[7,64,256]{2,1,0:T(8,128)S(1)}, u32[]{:S(2)}, u32[]{:S(2)}) collective-permute-start(f32[7,64,256]{2,1,0:T(8,128)S(1)} %get-tuple-element.27), channel_id=1, source_target_pairs={{0,1},{1,2},{2,3},{3,4},{4,5},{5,6},{6,7},{7,8},{8,9},{9,10},{10,1... | collective-permute-start | bytes 1376264 | tf_op jit(solution)/shard_map/ppermute | solution.py:21
  10.4 21.9 %collective-permute-start.1 = (f32[7,64,256]{2,1,0:T(8,128)S(1)}, f32[7,64,256]{2,1,0:T(8,128)S(1)}, u32[]{:S(2)}, u32[]{:S(2)}) collective-permute-start(f32[7,64,256]{2,1,0:T(8,128)S(1)} %get-tuple-element.28), channel_id=1, source_target_pairs={{1,0},{2,1},{3,2},{4,3},{5,4},{6,5},{7,6},{8,7},{9,8},{10,9},{11,1... | collective-permute-start | bytes 1376264 | tf_op jit(solution)/shard_map/ppermute | solution.py:21
  32.3 0.7 copy-start.4
  32.3 0.7 copy-start.6
  36.0 13.0 %collective-permute-start.2 = (f32[6,64,256]{2,1,0:T(8,128)S(1)}, f32[6,64,256]{2,1,0:T(8,128)S(1)}, u32[]{:S(2)}, u32[]{:S(2)}) collective-permute-start(f32[6,64,256]{2,1,0:T(8,128)S(1)} %get-tuple-element.33), channel_id=1, source_target_pairs={{0,1},{1,2},{2,3},{3,4},{4,5},{5,6},{6,7},{7,8},{8,9},{9,10},{10,1... | collective-permute-start | bytes 1179656 | tf_op jit(solution)/shard_map/ppermute | solution.py:21
  38.0 19.3 %collective-permute-start.3 = (f32[6,64,256]{2,1,0:T(8,128)S(1)}, f32[6,64,256]{2,1,0:T(8,128)S(1)}, u32[]{:S(2)}, u32[]{:S(2)}) collective-permute-start(f32[6,64,256]{2,1,0:T(8,128)S(1)} %get-tuple-element.34), channel_id=1, source_target_pairs={{1,0},{2,1},{3,2},{4,3},{5,4},{6,5},{7,6},{8,7},{9,8},{10,9},{11,1... | collective-permute-start | bytes 1179656 | tf_op jit(solution)/shard_map/ppermute | solution.py:21
  59.8 13.0 %collective-permute-start.4 = (f32[6,64,256]{2,1,0:T(8,128)S(1)}, f32[6,64,256]{2,1,0:T(8,128)S(1)}, u32[]{:S(2)}, u32[]{:S(2)}) collective-permute-start(f32[6,64,256]{2,1,0:T(8,128)S(1)} %get-tuple-element.39), channel_id=1, source_target_pairs={{0,1},{1,2},{2,3},{3,4},{4,5},{5,6},{6,7},{7,8},{8,9},{9,10},{10,1... | collective-permute-start | bytes 1179656 | tf_op jit(solution)/shard_map/ppermute | solution.py:21
  61.7 20.5 %collective-permute-start.5 = (f32[6,64,256]{2,1,0:T(8,128)S(1)}, f32[6,64,256]{2,1,0:T(8,128)S(1)}, u32[]{:S(2)}, u32[]{:S(2)}) collective-permute-start(f32[6,64,256]{2,1,0:T(8,128)S(1)} %get-tuple-element.40), channel_id=1, source_target_pairs={{1,0},{2,1},{3,2},{4,3},{5,4},{6,5},{7,6},{8,7},{9,8},{10,9},{11,1... | collective-permute-start | bytes 1179656 | tf_op jit(solution)/shard_map/ppermute | solution.py:21
  83.8 2.5 %collective-permute-start.6 = (f32[6,2,64,256]{3,2,1,0:T(8,128)S(1)}, f32[6,2,64,256]{3,2,1,0:T(8,128)S(1)}, u32[]{:S(2)}, u32[]{:S(2)}) collective-permute-start(f32[6,2,64,256]{3,2,1,0:T(8,128)S(1)} %shard_map.76), channel_id=1, source_target_pairs={{0,16},{16,0},{1,17},{17,1},{2,18},{18,2},{3,19},{19,3},{4,20},{20... | collective-permute-start | bytes 2359304 | tf_op jit(solution)/shard_map/ppermute | solution.py:330

commit v4 on v3

--- a/solution.py
+++ b/solution.py
@@ -8,17 +8,8 @@
 from jax.sharding import PartitionSpec as P
 
 FINE = 4
-COARSE = 2
-
-
 DT_FINE = 0.18
 DT_COARSE = 0.36
-
-
-def passed_along(block, axis, distance):
-    devices = range(lax.axis_size(axis))
-    route = [(i - distance, i) for i in devices if i - distance in devices]
-    return lax.ppermute(block, axis, route)
 
 
 class Inplane:
@@ -199,86 +190,100 @@
     return ends, displaced
 
 
-def fine_kernel(
-    step, turn, last, *refs
-):
+def fine_kernel(step, turn, last, *refs):
     if turn == 0:
-        shear_table, lame_table, *refs = refs
+        shear_hbm, lame_hbm, *refs = refs
+        *refs, shear_table, lame_table, arrived = refs
+        copies = [
+            pltpu.make_async_copy(shear_hbm, shear_table, arrived.at[0]),
+            pltpu.make_async_copy(lame_hbm, lame_table, arrived.at[1]),
+        ]
+        for copy in copies:
+            copy.start()
     else:
         edges, *refs = refs
-    start, state, moduli, loading, part, rim, low, high, *outs = refs
+    state, moduli, loading, part, rim, low, high, *outs = refs
     if turn == 0:
         *outs, edges = outs
+        for copy in copies:
+            copy.wait()
         edges[0], edges[1] = zone_values(low[6], shear_table, lame_table, 1.0)
         edges[2], edges[3] = zone_values(high[6], shear_table, lame_table, 1.0)
     count = moduli.shape[1]
-    ends, displaced = two_steps(
-        step, state, part, rim, low, high, moduli, edges, lambda c, z: loading[c, z]
-    )
-    new_state, next_part, up, down, next_rim = outs[:5]
+    load = lambda c, z: loading[c, z]
+    ends, displaced = two_steps(step, state, part, rim, low, high, moduli, edges, load)
+    new_state = outs[0]
     for z in range(count):
         for c in range(3):
             new_state[c, z] = displaced[z][c]
             new_state[3 + c, z] = ends[z][c]
-    if last:
-        entry = outs[5]
-        first = lax.axis_index("win") == 0
-        for z in range(count):
-            for c in range(6):
-                entry[c, z] = jnp.where(first, new_state[c, z], start[c, z])
-        next_step, load = DT_COARSE, lambda c, z: 0.0
-    else:
-        entry = new_state
-        next_step, load = step, lambda c, z: loading[c, z]
-    planes = [Inplane([entry[c, z] for c in range(3)]) for z in range(count)]
+    if not last:
+        planes = [Inplane(displaced[z]) for z in range(count)]
+        prepare(
+            planes, lambda c, z: ends[z][c], lambda z: moduli[0, z], lambda z: moduli[1, z],
+            load, step, *outs[1:],
+        )
+
+
+def coarse_open_kernel(before, start, moduli, difference, part, up, down, rim):
+    count = moduli.shape[1]
+    for z in range(count):
+        for c in range(6):
+            difference[c, z] = before[c, z] - start[c, z]
+    planes = [Inplane([difference[c, z] for c in range(3)]) for z in range(count)]
     prepare(
-        planes, lambda c, z: entry[3 + c, z], lambda z: moduli[0, z], lambda z: moduli[1, z],
-        load, next_step, next_part, up, down, next_rim,
-    )
-
-
-def coarse_open_kernel(state, moduli, part, up, down, rim):
-    count = moduli.shape[1]
-    planes = [Inplane([state[c, z] for c in range(3)]) for z in range(count)]
-    prepare(
-        planes, lambda c, z: state[3 + c, z], lambda z: moduli[0, z], lambda z: moduli[1, z],
-        lambda c, z: 0.0, DT_COARSE, part, up, down, rim,
-    )
-
-
-def coarse_kernel(edges, state, moduli, part, rim, low, high, new_state):
+        planes, lambda c, z: difference[3 + c, z], lambda z: moduli[0, z],
+        lambda z: moduli[1, z], lambda c, z: 0.0, DT_COARSE, part, up, down, rim,
+    )
+
+
+def coarse_kernel(edges, state, moduli, part, rim, low, high, fine_end, new_end):
     ends, displaced = two_steps(
         DT_COARSE, state, part, rim, low, high, moduli, edges, lambda c, z: 0.0
     )
+    first = lax.axis_index("win") == 0
     for z in range(moduli.shape[1]):
         for c in range(3):
-            new_state[c, z] = displaced[z][c]
-            new_state[3 + c, z] = ends[z][c]
+            new_end[c, z] = fine_end[c, z] + jnp.where(first, 0.0, displaced[z][c])
+            new_end[3 + c, z] = fine_end[3 + c, z] + jnp.where(first, 0.0, ends[z][c])
 
 
 VMEM = pl.BlockSpec(memory_space=pltpu.VMEM)
-SMEM = pl.BlockSpec(memory_space=pltpu.SMEM)
 HBM = pl.BlockSpec(memory_space=pltpu.HBM)
 
 
-def called(kernel, outs, *operands, scalars=0, specs=None, scratch=()):
+def called(kernel, outs, *operands, in_specs=None, scratch=()):
     return pl.pallas_call(
         kernel,
         out_shape=[jax.ShapeDtypeStruct(shape, jnp.float32) for shape in outs],
-        in_specs=specs or [SMEM] * scalars + [VMEM] * (len(operands) - scalars),
+        in_specs=in_specs or [VMEM] * len(operands),
         out_specs=[VMEM] * len(outs),
         scratch_shapes=list(scratch),
         compiler_params=pltpu.CompilerParams(vmem_limit_bytes=16 * 1024 * 1024),
     )(*operands)
 
 
-def exchanged(up, down):
-    return passed_along(up, "slab", 1), passed_along(down, "slab", -1)
+def exchanged(up, down, first_window=0):
+    windows, slabs = lax.axis_size("win"), lax.axis_size("slab")
+
+    def passed(block, distance):
+        route = [
+            (n * slabs + i - distance, n * slabs + i)
+            for n in range(first_window, windows)
+            for i in range(slabs)
+            if 0 <= i - distance < slabs
+        ]
+        return lax.ppermute(block, ("win", "slab"), route)
+
+    return passed(up, 1), passed(down, -1)
+
+
+def in_hbm(*arrays):
+    return [pltpu.with_memory_space_constraint(a, pltpu.HBM) for a in arrays]
 
 
 def shards(states, load_shape, zone_ids, zone_shear, zone_lame, amp_table, cycle_index):
     windows = lax.axis_size("win")
-    first = lax.axis_index("win") == 0
     start = states[0]
     count, rows, columns = zone_ids.shape
     plane = (rows, columns)
@@ -286,49 +291,48 @@
     message, rims = (6, *plane), (2, 6, *plane)
 
     given = (states, load_shape, zone_ids, zone_shear, zone_lame, amp_table, cycle_index)
+    tables = [pltpu.SMEM(table.shape, table.dtype) for table in given[3:]]
     moduli, loading, part, up, down, rim = called(
         functools.partial(open_kernel, DT_FINE),
         [(2, count, *plane), field, field, (7, *plane), (7, *plane), rims],
-        *given,
-        specs=[HBM] * len(given),
+        *in_hbm(*given),
+        in_specs=[HBM] * len(given),
         scratch=[
             pltpu.VMEM(state, states.dtype),
             pltpu.VMEM(load_shape.shape, load_shape.dtype),
             pltpu.VMEM(zone_ids.shape, zone_ids.dtype),
-            *[pltpu.SMEM(table.shape, table.dtype) for table in given[3:]],
+            *tables,
             pltpu.SemaphoreType.DMA((len(given),)),
         ],
     )
-    low, high = exchanged(up, down)
-    current, edges = start, None
+    fine_end, edges = start, None
     for turn in range(FINE // 2):
         last = turn == FINE // 2 - 1
-        outs = [state, field, message, message, rims]
-        outs += ([state] if last else []) + ([(4, *plane)] if turn == 0 else [])
-        tables = (zone_shear, zone_lame) if turn == 0 else (edges,)
-        current, part, up, down, rim, *more = called(
-            functools.partial(fine_kernel, DT_FINE, turn, last), outs,
-            *tables, start, current, moduli, loading, part, rim, low, high,
-            scalars=2 if turn == 0 else 0,
+        low, high = exchanged(up, down)
+        outs = [state] + ([] if last else [field, message, message, rims])
+        operands = [fine_end, moduli, loading, part, rim, low, high]
+        fine = functools.partial(fine_kernel, DT_FINE, turn, last)
+        if turn == 0:
+            fine_end, *more, edges = called(
+                fine, [*outs, (4, *plane)], *in_hbm(zone_shear, zone_lame), *operands,
+                in_specs=[HBM] * 2 + [VMEM] * len(operands),
+                scratch=[*tables[:2], pltpu.SemaphoreType.DMA((2,))],
+            )
+        else:
+            fine_end, *more = called(fine, outs, edges, *operands)
+        if not last:
+            part, up, down, rim = more
+
+    new_end = fine_end
+    for _ in range(windows - 1):
+        before = lax.ppermute(new_end, "win", [(i, (i + 1) % windows) for i in range(windows)])
+        difference, part, up, down, rim = called(
+            coarse_open_kernel, [state, field, message, message, rims], before, start, moduli
         )
-        if turn == 0:
-            edges = more.pop()
-        low, high = exchanged(up, down)
-    fine_end, entry = current, more[0]
-
-    def coarse_end(status, part, rim, low, high):
-        return called(coarse_kernel, [state], edges, status, moduli, part, rim, low, high)[0]
-
-    advanced = coarse_end(entry, part, rim, low, high)
-    correction = fine_end - jnp.where(first, 0.0, advanced)
-    for _ in range(windows - 2):
-        status = correction + passed_along(advanced, "win", 1)
-        part, up, down, rim = called(
-            coarse_open_kernel, [field, message, message, rims], status, moduli
-        )
-        advanced = coarse_end(status, part, rim, *exchanged(up, down))
-    everyone = lax.ppermute(advanced, "win", [(i, (i + 1) % windows) for i in range(windows)])
-    new_end = correction + jnp.where(first, 0.0, everyone)
+        low, high = exchanged(up, down, 1)
+        new_end = called(
+            coarse_kernel, [state], edges, difference, moduli, part, rim, low, high, fine_end
+        )[0]
     return new_end[None]
 
 

time: 87.7 us -> 74.2 us (0.85)
  waiting for transfers between devices: 52 us -> 44.2 us
  local copies, waits for them, and re-layouts: 6.25 us -> 0.01 us
  Pallas kernels: 8.85 us -> 10.5 us
  other arithmetic: 1.05 us -> 0 us
    ppermute x7, waiting for transfers between devices: 52 us -> 44.2 us  [the longest x6 42.3 us: passed(): return lax.ppermute(block, ('win', 'slab'), route)]
    unnamed x18 -> x2, local copies, waits for them, and re-layouts: 6.25 us -> 0.01 us
    pallas_call x4 -> x5, Pallas kernels: 8.85 us -> 10.5 us  [called(): pl.pallas_call(kernel, out_shape=[jax.ShapeDtypeStruct(shape, jnp.float32...]
    broadcast_in_dim x1 -> x0, other arithmetic: 1.05 us -> none  [shards(): return new_end[None]]
where the time goes in v4:
time: 74.2 us; the launch traced here: 73.9 us
  waiting for transfers between devices  44.2 us (60%)
  starting transfers between devices  19.1 us (26%)
  Pallas kernels  10.5 us (14%)
    ppermute x6, waiting for transfers between devices, passed(): return lax.ppermute(block, ('win', 'slab'), route)  42.3 us
    ppermute x6, starting transfers between devices, passed(): return lax.ppermute(block, ('win', 'slab'), route)  18.5 us
    pallas_call x5, Pallas kernels, called(): pl.pallas_call(kernel, out_shape=[jax.ShapeDtypeStruct(shape, jnp.float32...  10.5 us
    ppermute x1, waiting for transfers between devices, shards(): lax.ppermute(new_end, 'win', [(i, (i + 1) % windows) for i in range(windo...  1.91 us
  transfers between devices with their start and end apart: 7, of which 7 were waited for; matrix products, arithmetic and copies ran while one was open for 0% of the time, Pallas kernels for 0%

profile of v4, /device:TPU:13, one launch (start us, length us, event | category | flops | bytes accessed | tf_op | source)
XLA Modules:
  0.0 73.9 jit_solution(503513928347515598)
XLA Ops:
  0.0 0.0 copy-start
  0.0 2.3 %shard_map.73 = (f32[2,2,64,256]{3,2,1,0:T(8,128)S(1)}, f32[3,2,64,256]{3,2,1,0:T(8,128)S(1)}, f32[3,2,64,256]{3,2,1,0:T(8,128)S(1)}, f32[7,64,256]{2,1,0:T(8,12...) custom-call(f32[1,6,2,64,256]{4,3,2,1,0:T(8,128)} %state_hbm.1, bf16[3,2,64,256]{3,2,1,0:T(8,128)(2,1)} %load_hbm.1, ...), custom_call_target="tpu_custom_call" | custom-call | tf_op jit(solution)/shard_map/pallas_call | solution.py:256
  2.3 3.1 %collective-permute-start = (f32[7,64,256]{2,1,0:T(8,128)S(1)}, f32[7,64,256]{2,1,0:T(8,128)S(1)}, u32[]{:S(2)}, u32[]{:S(2)}) collective-permute-start(f32[7,64,256]{2,1,0:T(8,128)S(1)} %get-tuple-element.26), channel_id=1, source_target_pairs={{0,1},{1,2},{2,3},{3,4},{4,5},{5,6},{6,7},{7,8},{8,9},{9,10},{10,1... | collective-permute-start | bytes 1376264 | tf_op jit(solution)/shard_map/ppermute | solution.py:276
  5.4 3.1 %collective-permute-start.1 = (f32[7,64,256]{2,1,0:T(8,128)S(1)}, f32[7,64,256]{2,1,0:T(8,128)S(1)}, u32[]{:S(2)}, u32[]{:S(2)}) collective-permute-start(f32[7,64,256]{2,1,0:T(8,128)S(1)} %get-tuple-element.27), channel_id=1, source_target_pairs={{1,0},{2,1},{3,2},{4,3},{5,4},{6,5},{7,6},{8,7},{9,8},{10,9},{11,1... | collective-permute-start | bytes 1376264 | tf_op jit(solution)/shard_map/ppermute | solution.py:276
  8.5 8.0 %collective-permute-done.refs_7_ = f32[7,64,256]{2,1,0:T(8,128)S(1)} collective-permute-done((f32[7,64,256]{2,1,0:T(8,128)S(1)}, f32[7,64,256]{2,1,0:T(8,128)S(1)}, u32[]{:S(2)}, u32[]{:S(2)}) %collective-permute-start) | collective-permute-done | bytes 458784 | tf_op jit(solution)/shard_map/ppermute | solution.py:276
  16.5 10.8 %collective-permute-done.1.refs_8_ = f32[7,64,256]{2,1,0:T(8,128)S(1)} collective-permute-done((f32[7,64,256]{2,1,0:T(8,128)S(1)}, f32[7,64,256]{2,1,0:T(8,128)S(1)}, u32[]{:S(2)}, u32[]{:S(2)}) %collective-permute-start.1) | collective-permute-done | bytes 458784 | tf_op jit(solution)/shard_map/ppermute | solution.py:276
  27.3 0.0 copy-done
  27.3 3.1 %shard_map.74 = (f32[6,2,64,256]{3,2,1,0:T(8,128)S(1)}, f32[3,2,64,256]{3,2,1,0:T(8,128)S(1)}, f32[6,64,256]{2,1,0:T(8,128)S(1)}, f32[6,64,256]{2,1,0:T(8,128)S(...) custom-call(f32[8]{0:T(128)} %refs_0_.1, f32[8]{0:T(128)} %refs_1_.1, f32[6,2,64,256]{3,2,1,0:T(8,128)S(1)} %bitcast.2, ...), custom_call_target="tpu_custom_call" | custom-call | tf_op jit(solution)/shard_map/pallas_call | solution.py:256
  30.5 1.9 %collective-permute-start.2 = (f32[6,64,256]{2,1,0:T(8,128)S(1)}, f32[6,64,256]{2,1,0:T(8,128)S(1)}, u32[]{:S(2)}, u32[]{:S(2)}) collective-permute-start(f32[6,64,256]{2,1,0:T(8,128)S(1)} %get-tuple-element.32), channel_id=1, source_target_pairs={{0,1},{1,2},{2,3},{3,4},{4,5},{5,6},{6,7},{7,8},{8,9},{9,10},{10,1... | collective-permute-start | bytes 1179656 | tf_op jit(solution)/shard_map/ppermute | solution.py:276
  32.4 4.3 %collective-permute-start.3 = (f32[6,64,256]{2,1,0:T(8,128)S(1)}, f32[6,64,256]{2,1,0:T(8,128)S(1)}, u32[]{:S(2)}, u32[]{:S(2)}) collective-permute-start(f32[6,64,256]{2,1,0:T(8,128)S(1)} %get-tuple-element.33), channel_id=1, source_target_pairs={{1,0},{2,1},{3,2},{4,3},{5,4},{6,5},{7,6},{8,7},{9,8},{10,9},{11,1... | collective-permute-start | bytes 1179656 | tf_op jit(solution)/shard_map/ppermute | solution.py:276
  36.7 6.8 %collective-permute-done.2.refs_6_ = f32[6,64,256]{2,1,0:T(8,128)S(1)} collective-permute-done((f32[6,64,256]{2,1,0:T(8,128)S(1)}, f32[6,64,256]{2,1,0:T(8,128)S(1)}, u32[]{:S(2)}, u32[]{:S(2)}) %collective-permute-start.2) | collective-permute-done | bytes 393248 | tf_op jit(solution)/shard_map/ppermute | solution.py:276
  43.5 8.3 %collective-permute-done.3.refs_7_ = f32[6,64,256]{2,1,0:T(8,128)S(1)} collective-permute-done((f32[6,64,256]{2,1,0:T(8,128)S(1)}, f32[6,64,256]{2,1,0:T(8,128)S(1)}, u32[]{:S(2)}, u32[]{:S(2)}) %collective-permute-start.3) | collective-permute-done | bytes 393248 | tf_op jit(solution)/shard_map/ppermute | solution.py:276
  51.7 1.7 %shard_map.75.fine_end = f32[6,2,64,256]{3,2,1,0:T(8,128)S(1)} custom-call(f32[4,64,256]{2,1,0:T(8,128)S(1)} %get-tuple-element.28.refs_0_.edges, f32[6,2,64,256]{3,2,1,0:T(8,128)S(1)} %get-tuple-element.29.refs_1_, f32[2,2,64,256]{3,2,1,0:T(8,128)S(1)} %get-tuple-element.22.refs_3_.refs_2_.moduli, f32[3,2,64,256]{3,2,1,0:T(8,128)S(1)} %get-tuple-element.23.refs_4_.refs_3_, ...), custom_call_target="tpu_custom_call" | custom-call | tf_op jit(solution)/shard_map/pallas_call | solution.py:256
  53.4 0.6 collective-permute-start.4
  54.0 1.9 %collective-permute-done.4.before = f32[6,2,64,256]{3,2,1,0:T(8,128)S(1)} collective-permute-done((f32[6,2,64,256]{3,2,1,0:T(8,128)S(1)}, f32[6,2,64,256]{3,2,1,0:T(8,128)S(1)}, u32[]{:S(2)}, u32[]{:S(2)}) %collective-permute-start.4) | collective-permute-done | bytes 786464 | tf_op jit(solution)/shard_map/ppermute | solution.py:328
  55.9 0.8 %shard_map.76 = (f32[6,2,64,256]{3,2,1,0:T(8,128)S(1)}, f32[3,2,64,256]{3,2,1,0:T(8,128)S(1)}, f32[6,64,256]{2,1,0:T(8,128)S(1)}, f32[6,64,256]{2,1,0:T(8,128)S(1)}, f32[2,6,64,256]{3,2,1,0:T(8,128)S(1)}) custom-call(f32[6,2,64,256]{3,2,1,0:T(8,128)S(1)} %collective-permute-done.4.before, f32[6,2,64,256]{3,2,1,0:T(8,128)S(1)} %bitcast.3, ...), custom_call_target="tpu_custom_call" | custom-call | tf_op jit(solution)/shard_map/pallas_call | solution.py:256
  56.7 1.9 %collective-permute-start.5 = (f32[6,64,256]{2,1,0:T(8,128)S(1)}, f32[6,64,256]{2,1,0:T(8,128)S(1)}, u32[]{:S(2)}, u32[]{:S(2)}) collective-permute-start(f32[6,64,256]{2,1,0:T(8,128)S(1)} %get-tuple-element.37), channel_id=1, source_target_pairs={{16,17},{17,18},{18,19},{19,20},{20,21},{21,22},{22,23},{23,24},{2... | collective-permute-start | bytes 1179656 | tf_op jit(solution)/shard_map/ppermute | solution.py:276
  58.6 4.3 %collective-permute-start.6 = (f32[6,64,256]{2,1,0:T(8,128)S(1)}, f32[6,64,256]{2,1,0:T(8,128)S(1)}, u32[]{:S(2)}, u32[]{:S(2)}) collective-permute-start(f32[6,64,256]{2,1,0:T(8,128)S(1)} %get-tuple-element.38), channel_id=1, source_target_pairs={{17,16},{18,17},{19,18},{20,19},{21,20},{22,21},{23,22},{24,23},{2... | collective-permute-start | bytes 1179656 | tf_op jit(solution)/shard_map/ppermute | solution.py:276
  62.9 3.2 %collective-permute-done.5.low = f32[6,64,256]{2,1,0:T(8,128)S(1)} collective-permute-done((f32[6,64,256]{2,1,0:T(8,128)S(1)}, f32[6,64,256]{2,1,0:T(8,128)S(1)}, u32[]{:S(2)}, u32[]{:S(2)}) %collective-permute-start.5) | collective-permute-done | bytes 393248 | tf_op jit(solution)/shard_map/ppermute | solution.py:276
  66.1 5.2 %collective-permute-done.6.high = f32[6,64,256]{2,1,0:T(8,128)S(1)} collective-permute-done((f32[6,64,256]{2,1,0:T(8,128)S(1)}, f32[6,64,256]{2,1,0:T(8,128)S(1)}, u32[]{:S(2)}, u32[]{:S(2)}) %collective-permute-start.6) | collective-permute-done | bytes 393248 | tf_op jit(solution)/shard_map/ppermute | solution.py:276
  71.3 2.6 %shard_map.77 = f32[6,2,64,256]{3,2,1,0:T(8,128)} custom-call(f32[4,64,256]{2,1,0:T(8,128)S(1)} %get-tuple-element.28.refs_0_.edges, f32[6,2,64,256]{3,2,1,0:T(8,128)S(1)} %get-tuple-element.34.state, f32[2,2,64,256]{3,2,1,0:T(8,128)S(1)} %get-tuple-element.22.refs_3_.refs_2_.moduli, f32[3,2,64,256]{3,2,1,0:T(8,128)S(1)} %get-tuple-element.35.part, ...), custom_call_target="tpu_custom_call" | custom-call | tf_op jit(solution)/shard_map/pallas_call | solution.py:256
Async XLA Ops:
  0.0 27.3 %copy-start = (f32[1,6,2,64,256]{4,3,2,1,0:T(8,128)S(1)}, f32[1,6,2,64,256]{4,3,2,1,0:T(8,128)}, u32[]{:S(2)}) copy-start(f32[1,6,2,64,256]{4,3,2,1,0:T(8,128)} %state_hbm.1) | copy-start | bytes 2359300
  2.3 14.2 %collective-permute-start = (f32[7,64,256]{2,1,0:T(8,128)S(1)}, f32[7,64,256]{2,1,0:T(8,128)S(1)}, u32[]{:S(2)}, u32[]{:S(2)}) collective-permute-start(f32[7,64,256]{2,1,0:T(8,128)S(1)} %get-tuple-element.26), channel_id=1, source_target_pairs={{0,1},{1,2},{2,3},{3,4},{4,5},{5,6},{6,7},{7,8},{8,9},{9,10},{10,1... | collective-permute-start | bytes 1376264 | tf_op jit(solution)/shard_map/ppermute | solution.py:276
  5.4 21.9 %collective-permute-start.1 = (f32[7,64,256]{2,1,0:T(8,128)S(1)}, f32[7,64,256]{2,1,0:T(8,128)S(1)}, u32[]{:S(2)}, u32[]{:S(2)}) collective-permute-start(f32[7,64,256]{2,1,0:T(8,128)S(1)} %get-tuple-element.27), channel_id=1, source_target_pairs={{1,0},{2,1},{3,2},{4,3},{5,4},{6,5},{7,6},{8,7},{9,8},{10,9},{11,1... | collective-permute-start | bytes 1376264 | tf_op jit(solution)/shard_map/ppermute | solution.py:276
  30.5 13.0 %collective-permute-start.2 = (f32[6,64,256]{2,1,0:T(8,128)S(1)}, f32[6,64,256]{2,1,0:T(8,128)S(1)}, u32[]{:S(2)}, u32[]{:S(2)}) collective-permute-start(f32[6,64,256]{2,1,0:T(8,128)S(1)} %get-tuple-element.32), channel_id=1, source_target_pairs={{0,1},{1,2},{2,3},{3,4},{4,5},{5,6},{6,7},{7,8},{8,9},{9,10},{10,1... | collective-permute-start | bytes 1179656 | tf_op jit(solution)/shard_map/ppermute | solution.py:276
  32.4 19.3 %collective-permute-start.3 = (f32[6,64,256]{2,1,0:T(8,128)S(1)}, f32[6,64,256]{2,1,0:T(8,128)S(1)}, u32[]{:S(2)}, u32[]{:S(2)}) collective-permute-start(f32[6,64,256]{2,1,0:T(8,128)S(1)} %get-tuple-element.33), channel_id=1, source_target_pairs={{1,0},{2,1},{3,2},{4,3},{5,4},{6,5},{7,6},{8,7},{9,8},{10,9},{11,1... | collective-permute-start | bytes 1179656 | tf_op jit(solution)/shard_map/ppermute | solution.py:276
  53.4 2.5 %collective-permute-start.4 = (f32[6,2,64,256]{3,2,1,0:T(8,128)S(1)}, f32[6,2,64,256]{3,2,1,0:T(8,128)S(1)}, u32[]{:S(2)}, u32[]{:S(2)}) collective-permute-start(f32[6,2,64,256]{3,2,1,0:T(8,128)S(1)} %shard_map.75.fine_end), channel_id=1, source_target_pairs={{0,16},{16,0},{1,17},{17,1},{2,18},{18,2},{3,19},{19,3},{4,20},{20... | collective-permute-start | bytes 2359304 | tf_op jit(solution)/shard_map/ppermute | solution.py:328
  56.7 9.4 %collective-permute-start.5 = (f32[6,64,256]{2,1,0:T(8,128)S(1)}, f32[6,64,256]{2,1,0:T(8,128)S(1)}, u32[]{:S(2)}, u32[]{:S(2)}) collective-permute-start(f32[6,64,256]{2,1,0:T(8,128)S(1)} %get-tuple-element.37), channel_id=1, source_target_pairs={{16,17},{17,18},{18,19},{19,20},{20,21},{21,22},{22,23},{23,24},{2... | collective-permute-start | bytes 1179656 | tf_op jit(solution)/shard_map/ppermute | solution.py:276
  58.6 12.7 %collective-permute-start.6 = (f32[6,64,256]{2,1,0:T(8,128)S(1)}, f32[6,64,256]{2,1,0:T(8,128)S(1)}, u32[]{:S(2)}, u32[]{:S(2)}) collective-permute-start(f32[6,64,256]{2,1,0:T(8,128)S(1)} %get-tuple-element.38), channel_id=1, source_target_pairs={{17,16},{18,17},{19,18},{20,19},{21,20},{22,21},{23,22},{24,23},{2... | collective-permute-start | bytes 1179656 | tf_op jit(solution)/shard_map/ppermute | solution.py:276

commit v5 on v4

--- a/solution.py
+++ b/solution.py
@@ -190,7 +190,20 @@
     return ends, displaced
 
 
-def fine_kernel(step, turn, last, *refs):
+def released_kernel(up, down, token, later_up, later_down):
+    @pl.when(lax.axis_index("win") != 0)
+    def _():
+        later_up[...] = up[...]
+        later_down[...] = down[...]
+
+
+def fine_kernel(step, turn, last, group, *refs):
+    @pl.when((lax.axis_index("win") == 0) == (group == 0))
+    def _():
+        fine_pair(step, turn, last, *refs)
+
+
+def fine_pair(step, turn, last, *refs):
     if turn == 0:
         shear_hbm, lame_hbm, *refs = refs
         *refs, shear_table, lame_table, arrived = refs
@@ -237,15 +250,20 @@
     )
 
 
-def coarse_kernel(edges, state, moduli, part, rim, low, high, fine_end, new_end):
-    ends, displaced = two_steps(
-        DT_COARSE, state, part, rim, low, high, moduli, edges, lambda c, z: 0.0
-    )
-    first = lax.axis_index("win") == 0
-    for z in range(moduli.shape[1]):
-        for c in range(3):
-            new_end[c, z] = fine_end[c, z] + jnp.where(first, 0.0, displaced[z][c])
-            new_end[3 + c, z] = fine_end[3 + c, z] + jnp.where(first, 0.0, ends[z][c])
+def coarse_kernel(edges, state, moduli, part, rim, low, high, before_end, fine_end, new_end):
+    @pl.when(lax.axis_index("win") == 0)
+    def _():
+        new_end[...] = before_end[...]
+
+    @pl.when(lax.axis_index("win") != 0)
+    def _():
+        ends, displaced = two_steps(
+            DT_COARSE, state, part, rim, low, high, moduli, edges, lambda c, z: 0.0
+        )
+        for z in range(moduli.shape[1]):
+            for c in range(3):
+                new_end[c, z] = fine_end[c, z] + displaced[z][c]
+                new_end[3 + c, z] = fine_end[3 + c, z] + ends[z][c]
 
 
 VMEM = pl.BlockSpec(memory_space=pltpu.VMEM)
@@ -263,13 +281,13 @@
     )(*operands)
 
 
-def exchanged(up, down, first_window=0):
+def exchanged(up, down, group):
     windows, slabs = lax.axis_size("win"), lax.axis_size("slab")
 
     def passed(block, distance):
         route = [
             (n * slabs + i - distance, n * slabs + i)
-            for n in range(first_window, windows)
+            for n in (range(1, windows) if group else range(1))
             for i in range(slabs)
             if 0 <= i - distance < slabs
         ]
@@ -305,33 +323,64 @@
             pltpu.SemaphoreType.DMA((len(given),)),
         ],
     )
-    fine_end, edges = start, None
+    def fine(turn, group, edges, *operands):
+        last = turn == FINE // 2 - 1
+        outs = [state] + ([] if last else [field, message, message, rims])
+        kernel = functools.partial(fine_kernel, DT_FINE, turn, last, group)
+        if turn:
+            return called(kernel, outs, edges, *operands)
+        return called(
+            kernel, [*outs, (4, *plane)], *in_hbm(zone_shear, zone_lame), *operands,
+            in_specs=[HBM] * 2 + [VMEM] * len(operands),
+            scratch=[*tables[:2], pltpu.SemaphoreType.DMA((2,))],
+        )
+
+    after = lax.optimization_barrier
+    fixed = moduli, loading
+    low, high = exchanged(up, down, 0)
+    token = lax.ppermute(low[0, :8, :128], "win", [(n, n + 1) for n in range(windows - 1)])
+    later_up, later_down = called(
+        released_kernel, [(7, *plane), (7, *plane)], up, down, token
+    )
+    later_low, later_high = exchanged(later_up, later_down, 1)
+    ends, parts, rim_of, edges = [start, start], [part, part], [rim, rim], [None, None]
     for turn in range(FINE // 2):
         last = turn == FINE // 2 - 1
-        low, high = exchanged(up, down)
-        outs = [state] + ([] if last else [field, message, message, rims])
-        operands = [fine_end, moduli, loading, part, rim, low, high]
-        fine = functools.partial(fine_kernel, DT_FINE, turn, last)
-        if turn == 0:
-            fine_end, *more, edges = called(
-                fine, [*outs, (4, *plane)], *in_hbm(zone_shear, zone_lame), *operands,
-                in_specs=[HBM] * 2 + [VMEM] * len(operands),
-                scratch=[*tables[:2], pltpu.SemaphoreType.DMA((2,))],
-            )
-        else:
-            fine_end, *more = called(fine, outs, edges, *operands)
-        if not last:
-            part, up, down, rim = more
-
-    new_end = fine_end
-    for _ in range(windows - 1):
+        got = [(low, high), (later_low, later_high)]
+        for group in (0, 1):
+            if group == 0 or not last:
+                ends[group], *more = fine(
+                    turn, group, edges[group], ends[group], *fixed, parts[group], rim_of[group],
+                    *got[group],
+                )
+                if turn == 0:
+                    edges[group] = more.pop()
+                if not last:
+                    parts[group], up, down, rim_of[group] = more
+                    if group == 0:
+                        low, high = exchanged(up, down, 0)
+                        later_low, later_high, _ = after((later_low, later_high, parts[0]))
+                        got[1] = later_low, later_high
+                    else:
+                        later_low, later_high = exchanged(up, down, 1)
+                        low, high, _ = after((low, high, parts[1]))
+
+    new_end = ends[0]
+    for link in range(windows - 1):
         before = lax.ppermute(new_end, "win", [(i, (i + 1) % windows) for i in range(windows)])
         difference, part, up, down, rim = called(
             coarse_open_kernel, [state, field, message, message, rims], before, start, moduli
         )
         low, high = exchanged(up, down, 1)
+        if link == 0:
+            later_low, later_high, _ = after((later_low, later_high, part))
+            fine_end = fine(
+                FINE // 2 - 1, 1, edges[1], ends[1], *fixed, parts[1], rim_of[1],
+                later_low, later_high,
+            )[0]
         new_end = called(
-            coarse_kernel, [state], edges, difference, moduli, part, rim, low, high, fine_end
+            coarse_kernel, [state],
+            edges[1], difference, moduli, part, rim, low, high, ends[0], fine_end,
         )[0]
     return new_end[None]
 

time: 74.2 us -> 69.1 us (0.931)
  the two profiles are of different devices: /device:TPU:13 before, /device:TPU:9 now
where the time goes in v5:
time: 69.1 us; the launch traced here: 68.8 us
  starting transfers between devices  29.6 us (43%)
  waiting for transfers between devices  28.3 us (41%)
  Pallas kernels  10.6 us (15%)
    ppermute x10, starting transfers between devices, passed(): return lax.ppermute(block, ('win', 'slab'), route)  24 us
    ppermute x10, waiting for transfers between devices, passed(): return lax.ppermute(block, ('win', 'slab'), route)  16.2 us
    ppermute x1, waiting for transfers between devices, shards(): lax.ppermute(low[0, :8, :128], 'win', [(n, n + 1) for n in range(windows...  12.2 us
    pallas_call x8, Pallas kernels, called(): pl.pallas_call(kernel, out_shape=[jax.ShapeDtypeStruct(shape, jnp.float32...  10.6 us
    ppermute x1, starting transfers between devices, shards(): lax.ppermute(new_end, 'win', [(i, (i + 1) % windows) for i in range(windo...  4.37 us
  transfers between devices with their start and end apart: 12, of which 6 were waited for; matrix products, arithmetic and copies ran while one was open for 0% of the time, Pallas kernels for 8%

profile of v5, /device:TPU:9, one launch (start us, length us, event | category | flops | bytes accessed | tf_op | source)
XLA Modules:
  0.0 68.8 jit_solution(12305598992878899117)
XLA Ops:
  0.0 0.0 copy-start
  0.0 2.3 %shard_map.73 = (f32[2,2,64,256]{3,2,1,0:T(8,128)S(1)}, f32[3,2,64,256]{3,2,1,0:T(8,128)S(1)}, f32[3,2,64,256]{3,2,1,0:T(8,128)S(1)}, f32[7,64,256]{2,1,0:T(8,12...) custom-call(f32[1,6,2,64,256]{4,3,2,1,0:T(8,128)} %state_hbm.1, bf16[3,2,64,256]{3,2,1,0:T(8,128)(2,1)} %load_hbm.1, ...), custom_call_target="tpu_custom_call" | custom-call | tf_op jit(solution)/shard_map/pallas_call | solution.py:274
  2.3 0.7 %collective-permute-start = (f32[7,64,256]{2,1,0:T(8,128)S(1)}, f32[7,64,256]{2,1,0:T(8,128)S(1)}, u32[]{:S(2)}, u32[]{:S(2)}) collective-permute-start(f32[7,64,256]{2,1,0:T(8,128)S(1)} %get-tuple-element.40.up), channel_id=1, source_target_pairs={{0,1},{1,2},{2,3},{3,4},{4,5},{5,6},{6,7},{7,8},{8,9},{9,10},{10,1... | collective-permute-start | bytes 1376264 | tf_op jit(solution)/shard_map/ppermute | solution.py:294
  3.0 0.7 %collective-permute-start.4 = (f32[7,64,256]{2,1,0:T(8,128)S(1)}, f32[7,64,256]{2,1,0:T(8,128)S(1)}, u32[]{:S(2)}, u32[]{:S(2)}) collective-permute-start(f32[7,64,256]{2,1,0:T(8,128)S(1)} %get-tuple-element.41.down), channel_id=1, source_target_pairs={{1,0},{2,1},{3,2},{4,3},{5,4},{6,5},{7,6},{8,7},{9,8},{10,9},{11,1... | collective-permute-start | bytes 1376264 | tf_op jit(solution)/shard_map/ppermute | solution.py:294
  3.7 0.0 collective-permute-done.refs_7_
  3.7 1.3 %collective-permute-start.1 = (f32[8,128]{1,0:T(8,128)S(1)}, f32[8,128]{1,0:T(8,128)S(1)}, u32[]{:S(2)}, u32[]{:S(2)}) collective-permute-start(f32[8,128]{1,0:T(8,128)S(1)} %slice_bitcast_fusion), channel_id=1, source_target_pairs={{0,16},{1,17},{2,18},{3,19},{4,20},{5,21},{6,22},{7,23},{8,24},{9,... | collective-permute-start | bytes 12296 | tf_op jit(solution)/shard_map/ppermute | solution.py:341
  5.0 12.2 %collective-permute-done.1.token = f32[8,128]{1,0:T(8,128)S(1)} collective-permute-done((f32[8,128]{1,0:T(8,128)S(1)}, f32[8,128]{1,0:T(8,128)S(1)}, u32[]{:S(2)}, u32[]{:S(2)}) %collective-permute-start.1) | collective-permute-done | bytes 4128 | tf_op jit(solution)/shard_map/ppermute | solution.py:341
  17.2 0.1 shard_map.74
  17.3 1.9 %collective-permute-start.2 = (f32[7,64,256]{2,1,0:T(8,128)S(1)}, f32[7,64,256]{2,1,0:T(8,128)S(1)}, u32[]{:S(2)}, u32[]{:S(2)}) collective-permute-start(f32[7,64,256]{2,1,0:T(8,128)S(1)} %get-tuple-element.42), channel_id=1, source_target_pairs={{16,17},{17,18},{18,19},{19,20},{20,21},{21,22},{22,23},{23,24},{2... | collective-permute-start | bytes 1376264 | tf_op jit(solution)/shard_map/ppermute | solution.py:294
  19.2 5.2 %collective-permute-start.3 = (f32[7,64,256]{2,1,0:T(8,128)S(1)}, f32[7,64,256]{2,1,0:T(8,128)S(1)}, u32[]{:S(2)}, u32[]{:S(2)}) collective-permute-start(f32[7,64,256]{2,1,0:T(8,128)S(1)} %get-tuple-element.43), channel_id=1, source_target_pairs={{17,16},{18,17},{19,18},{20,19},{21,20},{22,21},{23,22},{24,23},{2... | collective-permute-start | bytes 1376264 | tf_op jit(solution)/shard_map/ppermute | solution.py:294
  24.4 0.0 collective-permute-done.4.refs_8_
  24.4 0.0 copy-done
  24.4 0.7 collective-permute-start.5
  25.1 0.7 collective-permute-start.6
  25.8 2.6 %collective-permute-done.2.refs_7_ = f32[7,64,256]{2,1,0:T(8,128)S(1)} collective-permute-done((f32[7,64,256]{2,1,0:T(8,128)S(1)}, f32[7,64,256]{2,1,0:T(8,128)S(1)}, u32[]{:S(2)}, u32[]{:S(2)}) %collective-permute-start.2) | collective-permute-done | bytes 458784 | tf_op jit(solution)/shard_map/ppermute | solution.py:294
  28.4 6.2 %collective-permute-done.3.refs_8_ = f32[7,64,256]{2,1,0:T(8,128)S(1)} collective-permute-done((f32[7,64,256]{2,1,0:T(8,128)S(1)}, f32[7,64,256]{2,1,0:T(8,128)S(1)}, u32[]{:S(2)}, u32[]{:S(2)}) %collective-permute-start.3) | collective-permute-done | bytes 458784 | tf_op jit(solution)/shard_map/ppermute | solution.py:294
  34.6 3.1 %shard_map.76 = (f32[6,2,64,256]{3,2,1,0:T(8,128)S(1)}, f32[3,2,64,256]{3,2,1,0:T(8,128)S(1)}, f32[6,64,256]{2,1,0:T(8,128)S(1)}, f32[6,64,256]{2,1,0:T(8,128)S(...) custom-call(f32[8]{0:T(128)} %refs_0_.3, f32[8]{0:T(128)} %refs_1_.3, f32[6,2,64,256]{3,2,1,0:T(8,128)S(1)} %bitcast.5, ...), custom_call_target="tpu_custom_call" | custom-call | tf_op jit(solution)/shard_map/pallas_call | solution.py:274
  37.8 0.0 collective-permute-done.5.refs_6_
  37.8 0.0 collective-permute-done.6.refs_7_
  37.8 4.4 %collective-permute-start.7 = (f32[6,2,64,256]{3,2,1,0:T(8,128)S(1)}, f32[6,2,64,256]{3,2,1,0:T(8,128)S(1)}, u32[]{:S(2)}, u32[]{:S(2)}) collective-permute-start(f32[6,2,64,256]{3,2,1,0:T(8,128)S(1)} %shard_map.77.before_end), channel_id=1, source_target_pairs={{0,16},{16,0},{1,17},{17,1},{2,18},{18,2},{3,19},{19,3},{4,20},{20... | collective-permute-start | bytes 2359304 | tf_op jit(solution)/shard_map/ppermute | solution.py:370
  42.2 3.2 %collective-permute-start.10 = (f32[6,64,256]{2,1,0:T(8,128)S(1)}, f32[6,64,256]{2,1,0:T(8,128)S(1)}, u32[]{:S(2)}, u32[]{:S(2)}) collective-permute-start(f32[6,64,256]{2,1,0:T(8,128)S(1)} %get-tuple-element.63), channel_id=1, source_target_pairs={{16,17},{17,18},{18,19},{19,20},{20,21},{21,22},{22,23},{23,24},{2... | collective-permute-start | bytes 1179656 | tf_op jit(solution)/shard_map/ppermute | solution.py:294
  45.4 3.8 %collective-permute-start.11 = (f32[6,64,256]{2,1,0:T(8,128)S(1)}, f32[6,64,256]{2,1,0:T(8,128)S(1)}, u32[]{:S(2)}, u32[]{:S(2)}) collective-permute-start(f32[6,64,256]{2,1,0:T(8,128)S(1)} %get-tuple-element.64), channel_id=1, source_target_pairs={{17,16},{18,17},{19,18},{20,19},{21,20},{22,21},{23,22},{24,23},{2... | collective-permute-start | bytes 1179656 | tf_op jit(solution)/shard_map/ppermute | solution.py:294
  49.3 0.0 collective-permute-done.7.before
  49.3 0.8 %shard_map.78 = (f32[6,2,64,256]{3,2,1,0:T(8,128)S(1)}, f32[3,2,64,256]{3,2,1,0:T(8,128)S(1)}, f32[6,64,256]{2,1,0:T(8,128)S(1)}, f32[6,64,256]{2,1,0:T(8,128)S(1)}, f32[2,6,64,256]{3,2,1,0:T(8,128)S(1)}) custom-call(f32[6,2,64,256]{3,2,1,0:T(8,128)S(1)} %collective-permute-done.7.before, f32[6,2,64,256]{3,2,1,0:T(8,128)S(1)} %bitcast.6, ...), custom_call_target="tpu_custom_call" | custom-call | tf_op jit(solution)/shard_map/pallas_call | solution.py:274
  50.1 3.0 %collective-permute-start.8 = (f32[6,64,256]{2,1,0:T(8,128)S(1)}, f32[6,64,256]{2,1,0:T(8,128)S(1)}, u32[]{:S(2)}, u32[]{:S(2)}) collective-permute-start(f32[6,64,256]{2,1,0:T(8,128)S(1)} %get-tuple-element.59), channel_id=1, source_target_pairs={{16,17},{17,18},{18,19},{19,20},{20,21},{21,22},{22,23},{23,24},{2... | collective-permute-start | bytes 1179656 | tf_op jit(solution)/shard_map/ppermute | solution.py:294
  53.1 4.1 %collective-permute-start.9 = (f32[6,64,256]{2,1,0:T(8,128)S(1)}, f32[6,64,256]{2,1,0:T(8,128)S(1)}, u32[]{:S(2)}, u32[]{:S(2)}) collective-permute-start(f32[6,64,256]{2,1,0:T(8,128)S(1)} %get-tuple-element.60), channel_id=1, source_target_pairs={{17,16},{18,17},{19,18},{20,19},{21,20},{22,21},{23,22},{24,23},{2... | collective-permute-start | bytes 1179656 | tf_op jit(solution)/shard_map/ppermute | solution.py:294
  57.2 0.0 collective-permute-done.10.refs_6_
  57.2 0.6 collective-permute-done.11.refs_7_
  57.8 1.7 %shard_map.79.fine_end = f32[6,2,64,256]{3,2,1,0:T(8,128)S(1)} custom-call(f32[4,64,256]{2,1,0:T(8,128)S(1)} %get-tuple-element.47.refs_0_.edges, f32[6,2,64,256]{3,2,1,0:T(8,128)S(1)} %get-tuple-element.61.refs_1_, f32[2,2,64,256]{3,2,1,0:T(8,128)S(1)} %get-tuple-element.36.refs_3_.refs_2_.moduli, f32[3,2,64,256]{3,2,1,0:T(8,128)S(1)} %get-tuple-element.37.refs_4_.refs_3_, ...), custom_call_target="tpu_custom_call" | custom-call | tf_op jit(solution)/shard_map/pallas_call | solution.py:274
  59.4 4.0 %collective-permute-done.8.low = f32[6,64,256]{2,1,0:T(8,128)S(1)} collective-permute-done((f32[6,64,256]{2,1,0:T(8,128)S(1)}, f32[6,64,256]{2,1,0:T(8,128)S(1)}, u32[]{:S(2)}, u32[]{:S(2)}) %collective-permute-start.8) | collective-permute-done | bytes 393248 | tf_op jit(solution)/shard_map/ppermute | solution.py:294
  63.4 2.8 %collective-permute-done.9.high = f32[6,64,256]{2,1,0:T(8,128)S(1)} collective-permute-done((f32[6,64,256]{2,1,0:T(8,128)S(1)}, f32[6,64,256]{2,1,0:T(8,128)S(1)}, u32[]{:S(2)}, u32[]{:S(2)}) %collective-permute-start.9) | collective-permute-done | bytes 393248 | tf_op jit(solution)/shard_map/ppermute | solution.py:294
  66.2 2.6 %shard_map.80 = f32[6,2,64,256]{3,2,1,0:T(8,128)} custom-call(f32[4,64,256]{2,1,0:T(8,128)S(1)} %get-tuple-element.47.refs_0_.edges, f32[6,2,64,256]{3,2,1,0:T(8,128)S(1)} %get-tuple-element.56.state, f32[2,2,64,256]{3,2,1,0:T(8,128)S(1)} %get-tuple-element.36.refs_3_.refs_2_.moduli, f32[3,2,64,256]{3,2,1,0:T(8,128)S(1)} %get-tuple-element.57.part, ...), custom_call_target="tpu_custom_call" | custom-call | tf_op jit(solution)/shard_map/pallas_call | solution.py:274
  (3 shorter events, 0.1 us)
Async XLA Ops:
  0.0 24.4 %copy-start = (f32[1,6,2,64,256]{4,3,2,1,0:T(8,128)S(1)}, f32[1,6,2,64,256]{4,3,2,1,0:T(8,128)}, u32[]{:S(2)}) copy-start(f32[1,6,2,64,256]{4,3,2,1,0:T(8,128)} %state_hbm.1) | copy-start | bytes 2359300
  2.3 1.4 %collective-permute-start = (f32[7,64,256]{2,1,0:T(8,128)S(1)}, f32[7,64,256]{2,1,0:T(8,128)S(1)}, u32[]{:S(2)}, u32[]{:S(2)}) collective-permute-start(f32[7,64,256]{2,1,0:T(8,128)S(1)} %get-tuple-element.40.up), channel_id=1, source_target_pairs={{0,1},{1,2},{2,3},{3,4},{4,5},{5,6},{6,7},{7,8},{8,9},{9,10},{10,1... | collective-permute-start | bytes 1376264 | tf_op jit(solution)/shard_map/ppermute | solution.py:294
  3.0 21.3 %collective-permute-start.4 = (f32[7,64,256]{2,1,0:T(8,128)S(1)}, f32[7,64,256]{2,1,0:T(8,128)S(1)}, u32[]{:S(2)}, u32[]{:S(2)}) collective-permute-start(f32[7,64,256]{2,1,0:T(8,128)S(1)} %get-tuple-element.41.down), channel_id=1, source_target_pairs={{1,0},{2,1},{3,2},{4,3},{5,4},{6,5},{7,6},{8,7},{9,8},{10,9},{11,1... | collective-permute-start | bytes 1376264 | tf_op jit(solution)/shard_map/ppermute | solution.py:294
  3.7 13.5 %collective-permute-start.1 = (f32[8,128]{1,0:T(8,128)S(1)}, f32[8,128]{1,0:T(8,128)S(1)}, u32[]{:S(2)}, u32[]{:S(2)}) collective-permute-start(f32[8,128]{1,0:T(8,128)S(1)} %slice_bitcast_fusion), channel_id=1, source_target_pairs={{0,16},{1,17},{2,18},{3,19},{4,20},{5,21},{6,22},{7,23},{8,24},{9,... | collective-permute-start | bytes 12296 | tf_op jit(solution)/shard_map/ppermute | solution.py:341
  17.3 11.1 %collective-permute-start.2 = (f32[7,64,256]{2,1,0:T(8,128)S(1)}, f32[7,64,256]{2,1,0:T(8,128)S(1)}, u32[]{:S(2)}, u32[]{:S(2)}) collective-permute-start(f32[7,64,256]{2,1,0:T(8,128)S(1)} %get-tuple-element.42), channel_id=1, source_target_pairs={{16,17},{17,18},{18,19},{19,20},{20,21},{21,22},{22,23},{23,24},{2... | collective-permute-start | bytes 1376264 | tf_op jit(solution)/shard_map/ppermute | solution.py:294
  19.2 15.4 %collective-permute-start.3 = (f32[7,64,256]{2,1,0:T(8,128)S(1)}, f32[7,64,256]{2,1,0:T(8,128)S(1)}, u32[]{:S(2)}, u32[]{:S(2)}) collective-permute-start(f32[7,64,256]{2,1,0:T(8,128)S(1)} %get-tuple-element.43), channel_id=1, source_target_pairs={{17,16},{18,17},{19,18},{20,19},{21,20},{22,21},{23,22},{24,23},{2... | collective-permute-start | bytes 1376264 | tf_op jit(solution)/shard_map/ppermute | solution.py:294
  24.4 13.4 %collective-permute-start.5 = (f32[6,64,256]{2,1,0:T(8,128)S(1)}, f32[6,64,256]{2,1,0:T(8,128)S(1)}, u32[]{:S(2)}, u32[]{:S(2)}) collective-permute-start(f32[6,64,256]{2,1,0:T(8,128)S(1)} %get-tuple-element.51), channel_id=1, source_target_pairs={{0,1},{1,2},{2,3},{3,4},{4,5},{5,6},{6,7},{7,8},{8,9},{9,10},{10,1... | collective-permute-start | bytes 1179656 | tf_op jit(solution)/shard_map/ppermute | solution.py:294
  25.1 12.7 %collective-permute-start.6 = (f32[6,64,256]{2,1,0:T(8,128)S(1)}, f32[6,64,256]{2,1,0:T(8,128)S(1)}, u32[]{:S(2)}, u32[]{:S(2)}) collective-permute-start(f32[6,64,256]{2,1,0:T(8,128)S(1)} %get-tuple-element.52), channel_id=1, source_target_pairs={{1,0},{2,1},{3,2},{4,3},{5,4},{6,5},{7,6},{8,7},{9,8},{10,9},{11,1... | collective-permute-start | bytes 1179656 | tf_op jit(solution)/shard_map/ppermute | solution.py:294
  37.8 11.5 %collective-permute-start.7 = (f32[6,2,64,256]{3,2,1,0:T(8,128)S(1)}, f32[6,2,64,256]{3,2,1,0:T(8,128)S(1)}, u32[]{:S(2)}, u32[]{:S(2)}) collective-permute-start(f32[6,2,64,256]{3,2,1,0:T(8,128)S(1)} %shard_map.77.before_end), channel_id=1, source_target_pairs={{0,16},{16,0},{1,17},{17,1},{2,18},{18,2},{3,19},{19,3},{4,20},{20... | collective-permute-start | bytes 2359304 | tf_op jit(solution)/shard_map/ppermute | solution.py:370
  42.2 15.0 %collective-permute-start.10 = (f32[6,64,256]{2,1,0:T(8,128)S(1)}, f32[6,64,256]{2,1,0:T(8,128)S(1)}, u32[]{:S(2)}, u32[]{:S(2)}) collective-permute-start(f32[6,64,256]{2,1,0:T(8,128)S(1)} %get-tuple-element.63), channel_id=1, source_target_pairs={{16,17},{17,18},{18,19},{19,20},{20,21},{21,22},{22,23},{23,24},{2... | collective-permute-start | bytes 1179656 | tf_op jit(solution)/shard_map/ppermute | solution.py:294
  45.4 12.4 %collective-permute-start.11 = (f32[6,64,256]{2,1,0:T(8,128)S(1)}, f32[6,64,256]{2,1,0:T(8,128)S(1)}, u32[]{:S(2)}, u32[]{:S(2)}) collective-permute-start(f32[6,64,256]{2,1,0:T(8,128)S(1)} %get-tuple-element.64), channel_id=1, source_target_pairs={{17,16},{18,17},{19,18},{20,19},{21,20},{22,21},{23,22},{24,23},{2... | collective-permute-start | bytes 1179656 | tf_op jit(solution)/shard_map/ppermute | solution.py:294
  50.1 13.3 %collective-permute-start.8 = (f32[6,64,256]{2,1,0:T(8,128)S(1)}, f32[6,64,256]{2,1,0:T(8,128)S(1)}, u32[]{:S(2)}, u32[]{:S(2)}) collective-permute-start(f32[6,64,256]{2,1,0:T(8,128)S(1)} %get-tuple-element.59), channel_id=1, source_target_pairs={{16,17},{17,18},{18,19},{19,20},{20,21},{21,22},{22,23},{23,24},{2... | collective-permute-start | bytes 1179656 | tf_op jit(solution)/shard_map/ppermute | solution.py:294
  53.1 13.1 %collective-permute-start.9 = (f32[6,64,256]{2,1,0:T(8,128)S(1)}, f32[6,64,256]{2,1,0:T(8,128)S(1)}, u32[]{:S(2)}, u32[]{:S(2)}) collective-permute-start(f32[6,64,256]{2,1,0:T(8,128)S(1)} %get-tuple-element.60), channel_id=1, source_target_pairs={{17,16},{18,17},{19,18},{20,19},{21,20},{22,21},{23,22},{24,23},{2... | collective-permute-start | bytes 1179656 | tf_op jit(solution)/shard_map/ppermute | solution.py:294

commit v6 on v5

--- a/solution.py
+++ b/solution.py
@@ -120,7 +120,7 @@
 
 def open_kernel(
     step, state_hbm, load_hbm, zones_hbm, shear_hbm, lame_hbm, amp_hbm, cycle_hbm,
-    moduli, loading, part, up, down, rim,
+    moduli, loading, part, up, down, rim, zone_up, zone_down,
     state, load_shape, zones, shear_table, lame_table, amp_table, cycle_index, arrived,
 ):
     pairs = (
@@ -151,8 +151,8 @@
         lambda c, z: loading[c, z],
         step, part, up, down, rim,
     )
-    down[6] = (zones[0] + 1).astype(jnp.float32)
-    up[6] = (zones[count - 1] + 1).astype(jnp.float32)
+    zone_down[...] = (zones[0] + 1).astype(jnp.float32)
+    zone_up[...] = (zones[count - 1] + 1).astype(jnp.float32)
 
 
 def two_steps(step, u0, part, rim, low, high, moduli, edges, load):
@@ -190,38 +190,33 @@
     return ends, displaced
 
 
-def released_kernel(up, down, token, later_up, later_down):
+def edge_kernel(
+    shear_hbm, lame_hbm, zone_low, zone_high, up, down, edges, later_up, later_down,
+    shear_table, lame_table, arrived,
+):
     @pl.when(lax.axis_index("win") != 0)
     def _():
-        later_up[...] = up[...]
-        later_down[...] = down[...]
-
-
-def fine_kernel(step, turn, last, group, *refs):
-    @pl.when((lax.axis_index("win") == 0) == (group == 0))
-    def _():
-        fine_pair(step, turn, last, *refs)
-
-
-def fine_pair(step, turn, last, *refs):
-    if turn == 0:
-        shear_hbm, lame_hbm, *refs = refs
-        *refs, shear_table, lame_table, arrived = refs
         copies = [
             pltpu.make_async_copy(shear_hbm, shear_table, arrived.at[0]),
             pltpu.make_async_copy(lame_hbm, lame_table, arrived.at[1]),
         ]
         for copy in copies:
             copy.start()
-    else:
-        edges, *refs = refs
-    state, moduli, loading, part, rim, low, high, *outs = refs
-    if turn == 0:
-        *outs, edges = outs
+        later_up[...] = up[...]
+        later_down[...] = down[...]
         for copy in copies:
             copy.wait()
-        edges[0], edges[1] = zone_values(low[6], shear_table, lame_table, 1.0)
-        edges[2], edges[3] = zone_values(high[6], shear_table, lame_table, 1.0)
+        edges[0], edges[1] = zone_values(zone_low[...], shear_table, lame_table, 1.0)
+        edges[2], edges[3] = zone_values(zone_high[...], shear_table, lame_table, 1.0)
+
+
+def fine_kernel(step, last, group, *refs):
+    @pl.when((lax.axis_index("win") == 0) == (group == 0))
+    def _():
+        fine_pair(step, last, *refs)
+
+
+def fine_pair(step, last, edges, state, moduli, loading, part, rim, low, high, *outs):
     count = moduli.shape[1]
     load = lambda c, z: loading[c, z]
     ends, displaced = two_steps(step, state, part, rim, low, high, moduli, edges, load)
@@ -310,9 +305,9 @@
 
     given = (states, load_shape, zone_ids, zone_shear, zone_lame, amp_table, cycle_index)
     tables = [pltpu.SMEM(table.shape, table.dtype) for table in given[3:]]
-    moduli, loading, part, up, down, rim = called(
+    moduli, loading, part, up, down, rim, zone_up, zone_down = called(
         functools.partial(open_kernel, DT_FINE),
-        [(2, count, *plane), field, field, (7, *plane), (7, *plane), rims],
+        [(2, count, *plane), field, field, message, message, rims, plane, plane],
         *in_hbm(*given),
         in_specs=[HBM] * len(given),
         scratch=[
@@ -323,27 +318,26 @@
             pltpu.SemaphoreType.DMA((len(given),)),
         ],
     )
-    def fine(turn, group, edges, *operands):
+    def fine(turn, group, *operands):
         last = turn == FINE // 2 - 1
-        outs = [state] + ([] if last else [field, message, message, rims])
-        kernel = functools.partial(fine_kernel, DT_FINE, turn, last, group)
-        if turn:
-            return called(kernel, outs, edges, *operands)
         return called(
-            kernel, [*outs, (4, *plane)], *in_hbm(zone_shear, zone_lame), *operands,
-            in_specs=[HBM] * 2 + [VMEM] * len(operands),
-            scratch=[*tables[:2], pltpu.SemaphoreType.DMA((2,))],
+            functools.partial(fine_kernel, DT_FINE, last, group),
+            [state] + ([] if last else [field, message, message, rims]),
+            *operands,
         )
 
     after = lax.optimization_barrier
     fixed = moduli, loading
     low, high = exchanged(up, down, 0)
-    token = lax.ppermute(low[0, :8, :128], "win", [(n, n + 1) for n in range(windows - 1)])
-    later_up, later_down = called(
-        released_kernel, [(7, *plane), (7, *plane)], up, down, token
-    )
+    edges, later_up, later_down = called(
+        edge_kernel, [(4, *plane), message, message],
+        *in_hbm(zone_shear, zone_lame), *exchanged(zone_up, zone_down, 1), up, down,
+        in_specs=[HBM] * 2 + [VMEM] * 4,
+        scratch=[*tables[:2], pltpu.SemaphoreType.DMA((2,))],
+    )
+    edges = lax.ppermute(edges, "win", [(1, 0)]), edges
     later_low, later_high = exchanged(later_up, later_down, 1)
-    ends, parts, rim_of, edges = [start, start], [part, part], [rim, rim], [None, None]
+    ends, parts, rim_of = [start, start], [part, part], [rim, rim]
     for turn in range(FINE // 2):
         last = turn == FINE // 2 - 1
         got = [(low, high), (later_low, later_high)]
@@ -353,8 +347,6 @@
                     turn, group, edges[group], ends[group], *fixed, parts[group], rim_of[group],
                     *got[group],
                 )
-                if turn == 0:
-                    edges[group] = more.pop()
                 if not last:
                     parts[group], up, down, rim_of[group] = more
                     if group == 0:
@@ -367,7 +359,7 @@
 
     new_end = ends[0]
     for link in range(windows - 1):
-        before = lax.ppermute(new_end, "win", [(i, (i + 1) % windows) for i in range(windows)])
+        before = lax.ppermute(new_end, "win", [(n, n + 1) for n in range(windows - 1)])
         difference, part, up, down, rim = called(
             coarse_open_kernel, [state, field, message, message, rims], before, start, moduli
         )

time: 69.1 us -> 64.2 us (0.929)
  the two profiles are of different devices: /device:TPU:9 before, /device:TPU:13 now
where the time goes in v6:
time: 64.2 us; the launch traced here: 63.1 us
  starting transfers between devices  30.1 us (47%)
  waiting for transfers between devices  22.2 us (35%)
  Pallas kernels  10.6 us (17%)
    ppermute x12, starting transfers between devices, passed(): return lax.ppermute(block, ('win', 'slab'), route)  27.5 us
    ppermute x12, waiting for transfers between devices, passed(): return lax.ppermute(block, ('win', 'slab'), route)  22.2 us
    pallas_call x8, Pallas kernels, called(): pl.pallas_call(kernel, out_shape=[jax.ShapeDtypeStruct(shape, jnp.float32...  10.6 us
    ppermute x1, starting transfers between devices, shards(): edges = (lax.ppermute(edges, 'win', [(1, 0)]), edges)  1.31 us
    ppermute x1, starting transfers between devices, shards(): lax.ppermute(new_end, 'win', [(n, n + 1) for n in range(windows - 1)])  1.29 us
  transfers between devices with their start and end apart: 14, of which 6 were waited for; matrix products, arithmetic and copies ran while one was open for 0% of the time, Pallas kernels for 9%

profile of v6, /device:TPU:13, one launch (start us, length us, event | category | flops | bytes accessed | tf_op | source)
XLA Modules:
  0.0 63.1 jit_solution(4545087871715109607)
XLA Ops:
  0.0 0.0 copy-start
  0.0 2.3 %shard_map.73 = (f32[2,2,64,256]{3,2,1,0:T(8,128)S(1)}, f32[3,2,64,256]{3,2,1,0:T(8,128)S(1)}, f32[3,2,64,256]{3,2,1,0:T(8,128)S(1)}, f32[6,64,256]{2,1,0:T(8,12...) custom-call(f32[1,6,2,64,256]{4,3,2,1,0:T(8,128)} %state_hbm.1, ...), custom_call_target="tpu_custom_call" | custom-call | tf_op jit(solution)/shard_map/pallas_call | solution.py:269
  2.3 0.7 %collective-permute-start.3 = (f32[6,64,256]{2,1,0:T(8,128)S(1)}, f32[6,64,256]{2,1,0:T(8,128)S(1)}, u32[]{:S(2)}, u32[]{:S(2)}) collective-permute-start(f32[6,64,256]{2,1,0:T(8,128)S(1)} %get-tuple-element.39.up), channel_id=1, source_target_pairs={{0,1},{1,2},{2,3},{3,4},{4,5},{5,6},{6,7},{7,8},{8,9},{9,10},{10,1... | collective-permute-start | bytes 1179656 | tf_op jit(solution)/shard_map/ppermute | solution.py:289
  3.0 0.7 %collective-permute-start.4 = (f32[6,64,256]{2,1,0:T(8,128)S(1)}, f32[6,64,256]{2,1,0:T(8,128)S(1)}, u32[]{:S(2)}, u32[]{:S(2)}) collective-permute-start(f32[6,64,256]{2,1,0:T(8,128)S(1)} %get-tuple-element.40.down), channel_id=1, source_target_pairs={{1,0},{2,1},{3,2},{4,3},{5,4},{6,5},{7,6},{8,7},{9,8},{10,9},{11,1... | collective-permute-start | bytes 1179656 | tf_op jit(solution)/shard_map/ppermute | solution.py:289
  3.7 3.1 %collective-permute-start = (f32[64,256]{1,0:T(8,128)S(1)}, f32[64,256]{1,0:T(8,128)S(1)}, u32[]{:S(2)}, u32[]{:S(2)}) collective-permute-start(f32[64,256]{1,0:T(8,128)S(1)} %get-tuple-element.37), channel_id=1, source_target_pairs={{16,17},{17,18},{18,19},{19,20},{20,21},{21,22},{22,23},{23,24},{2... | collective-permute-start | bytes 196616 | tf_op jit(solution)/shard_map/ppermute | solution.py:289
  6.8 3.1 %collective-permute-start.1 = (f32[64,256]{1,0:T(8,128)S(1)}, f32[64,256]{1,0:T(8,128)S(1)}, u32[]{:S(2)}, u32[]{:S(2)}) collective-permute-start(f32[64,256]{1,0:T(8,128)S(1)} %get-tuple-element.38), channel_id=1, source_target_pairs={{17,16},{18,17},{19,18},{20,19},{21,20},{22,21},{23,22},{24,23},{2... | collective-permute-start | bytes 196616 | tf_op jit(solution)/shard_map/ppermute | solution.py:289
  9.9 0.7 %collective-permute-done.zone_low = f32[64,256]{1,0:T(8,128)S(1)} collective-permute-done((f32[64,256]{1,0:T(8,128)S(1)}, f32[64,256]{1,0:T(8,128)S(1)}, u32[]{:S(2)}, u32[]{:S(2)}) %collective-permute-start) | collective-permute-done | bytes 65568 | tf_op jit(solution)/shard_map/ppermute | solution.py:289
  10.6 4.6 %collective-permute-done.1.zone_high = f32[64,256]{1,0:T(8,128)S(1)} collective-permute-done((f32[64,256]{1,0:T(8,128)S(1)}, f32[64,256]{1,0:T(8,128)S(1)}, u32[]{:S(2)}, u32[]{:S(2)}) %collective-permute-start.1) | collective-permute-done | bytes 65568 | tf_op jit(solution)/shard_map/ppermute | solution.py:289
  15.2 0.8 %shard_map.74 = (f32[4,64,256]{2,1,0:T(8,128)S(1)}, f32[6,64,256]{2,1,0:T(8,128)S(1)}, f32[6,64,256]{2,1,0:T(8,128)S(1)}) custom-call(f32[8]{0:T(128)} %shear_hbm.3, f32[8]{0:T(128)} %lame_hbm.3, f32[64,256]{1,0:T(8,128)S(1)} %collective-permute-done.zone_low, f32[64,256]{1,0:T(8,128)S(1)} %collective-permute-done.1.zone_high, ...), custom_call_target="tpu_custom_call" | custom-call | tf_op jit(solution)/shard_map/pallas_call | solution.py:269
  16.0 1.3 %collective-permute-start.2 = (f32[4,64,256]{2,1,0:T(8,128)S(1)}, f32[4,64,256]{2,1,0:T(8,128)S(1)}, u32[]{:S(2)}, u32[]{:S(2)}) collective-permute-start(f32[4,64,256]{2,1,0:T(8,128)S(1)} %get-tuple-element.41.refs_0_.edges), channel_id=1, source_target_pairs={{16,0},{17,1},{18,2},{19,3},{20,4},{21,5},{22,6},{23,7},{24,8},{25... | collective-permute-start | bytes 786440 | tf_op jit(solution)/shard_map/ppermute | solution.py:338
  17.4 2.5 %collective-permute-start.7 = (f32[6,64,256]{2,1,0:T(8,128)S(1)}, f32[6,64,256]{2,1,0:T(8,128)S(1)}, u32[]{:S(2)}, u32[]{:S(2)}) collective-permute-start(f32[6,64,256]{2,1,0:T(8,128)S(1)} %get-tuple-element.51), channel_id=1, source_target_pairs={{16,17},{17,18},{18,19},{19,20},{20,21},{21,22},{22,23},{23,24},{2... | collective-permute-start | bytes 1179656 | tf_op jit(solution)/shard_map/ppermute | solution.py:289
  19.9 3.7 %collective-permute-start.8 = (f32[6,64,256]{2,1,0:T(8,128)S(1)}, f32[6,64,256]{2,1,0:T(8,128)S(1)}, u32[]{:S(2)}, u32[]{:S(2)}) collective-permute-start(f32[6,64,256]{2,1,0:T(8,128)S(1)} %get-tuple-element.52), channel_id=1, source_target_pairs={{17,16},{18,17},{19,18},{20,19},{21,20},{22,21},{23,22},{24,23},{2... | collective-permute-start | bytes 1179656 | tf_op jit(solution)/shard_map/ppermute | solution.py:289
  23.6 0.0 collective-permute-done.2.refs_0_
  23.6 0.0 collective-permute-done.3.refs_6_
  23.6 0.0 collective-permute-done.4.refs_7_
  23.6 0.0 copy-done
  23.6 0.7 %collective-permute-start.5 = (f32[6,64,256]{2,1,0:T(8,128)S(1)}, f32[6,64,256]{2,1,0:T(8,128)S(1)}, u32[]{:S(2)}, u32[]{:S(2)}) collective-permute-start(f32[6,64,256]{2,1,0:T(8,128)S(1)} %get-tuple-element.49), channel_id=1, source_target_pairs={{0,1},{1,2},{2,3},{3,4},{4,5},{5,6},{6,7},{7,8},{8,9},{9,10},{10,1... | collective-permute-start | bytes 1179656 | tf_op jit(solution)/shard_map/ppermute | solution.py:289
  24.3 0.7 %collective-permute-start.6 = (f32[6,64,256]{2,1,0:T(8,128)S(1)}, f32[6,64,256]{2,1,0:T(8,128)S(1)}, u32[]{:S(2)}, u32[]{:S(2)}) collective-permute-start(f32[6,64,256]{2,1,0:T(8,128)S(1)} %get-tuple-element.50), channel_id=1, source_target_pairs={{1,0},{2,1},{3,2},{4,3},{5,4},{6,5},{7,6},{8,7},{9,8},{10,9},{11,1... | collective-permute-start | bytes 1179656 | tf_op jit(solution)/shard_map/ppermute | solution.py:289
  25.0 1.8 %collective-permute-done.7.refs_6_ = f32[6,64,256]{2,1,0:T(8,128)S(1)} collective-permute-done((f32[6,64,256]{2,1,0:T(8,128)S(1)}, f32[6,64,256]{2,1,0:T(8,128)S(1)}, u32[]{:S(2)}, u32[]{:S(2)}) %collective-permute-start.7) | collective-permute-done | bytes 393248 | tf_op jit(solution)/shard_map/ppermute | solution.py:289
  26.8 8.6 %collective-permute-done.8.refs_7_ = f32[6,64,256]{2,1,0:T(8,128)S(1)} collective-permute-done((f32[6,64,256]{2,1,0:T(8,128)S(1)}, f32[6,64,256]{2,1,0:T(8,128)S(1)}, u32[]{:S(2)}, u32[]{:S(2)}) %collective-permute-start.8) | collective-permute-done | bytes 393248 | tf_op jit(solution)/shard_map/ppermute | solution.py:289
  35.4 2.4 %shard_map.76 = (f32[6,2,64,256]{3,2,1,0:T(8,128)S(1)}, f32[3,2,64,256]{3,2,1,0:T(8,128)S(1)}, f32[6,64,256]{2,1,0:T(8,128)S(1)}, f32[6,64,256]{2,1,0:T(8,128)S(1)}, f32[2,6,64,256]{3,2,1,0:T(8,128)S(1)}) custom-call(f32[4,64,256]{2,1,0:T(8,128)S(1)} %get-tuple-element.41.refs_0_.edges, f32[6,2,64,256]{3,2,1,0:T(8,128)S(1)} %bitcast.3, ...), custom_call_target="tpu_custom_call" | custom-call | tf_op jit(solution)/shard_map/pallas_call | solution.py:269
  37.7 0.0 collective-permute-done.5.refs_6_
  37.8 0.0 collective-permute-done.6.refs_7_
  37.8 1.3 %collective-permute-start.9 = (f32[6,2,64,256]{3,2,1,0:T(8,128)S(1)}, f32[6,2,64,256]{3,2,1,0:T(8,128)S(1)}, u32[]{:S(2)}, u32[]{:S(2)}) collective-permute-start(f32[6,2,64,256]{3,2,1,0:T(8,128)S(1)} %shard_map.77.before_end), channel_id=1, source_target_pairs={{0,16},{1,17},{2,18},{3,19},{4,20},{5,21},{6,22},{7,23},{8,24},{9,... | collective-permute-start | bytes 2359304 | tf_op jit(solution)/shard_map/ppermute | solution.py:362
  39.1 1.9 %collective-permute-start.12 = (f32[6,64,256]{2,1,0:T(8,128)S(1)}, f32[6,64,256]{2,1,0:T(8,128)S(1)}, u32[]{:S(2)}, u32[]{:S(2)}) collective-permute-start(f32[6,64,256]{2,1,0:T(8,128)S(1)} %get-tuple-element.65), channel_id=1, source_target_pairs={{16,17},{17,18},{18,19},{19,20},{20,21},{21,22},{22,23},{23,24},{2... | collective-permute-start | bytes 1179656 | tf_op jit(solution)/shard_map/ppermute | solution.py:289
  41.0 4.3 %collective-permute-start.13 = (f32[6,64,256]{2,1,0:T(8,128)S(1)}, f32[6,64,256]{2,1,0:T(8,128)S(1)}, u32[]{:S(2)}, u32[]{:S(2)}) collective-permute-start(f32[6,64,256]{2,1,0:T(8,128)S(1)} %get-tuple-element.66), channel_id=1, source_target_pairs={{17,16},{18,17},{19,18},{20,19},{21,20},{22,21},{23,22},{24,23},{2... | collective-permute-start | bytes 1179656 | tf_op jit(solution)/shard_map/ppermute | solution.py:289
  45.3 0.0 collective-permute-done.9.before
  45.3 0.8 %shard_map.78 = (f32[6,2,64,256]{3,2,1,0:T(8,128)S(1)}, f32[3,2,64,256]{3,2,1,0:T(8,128)S(1)}, f32[6,64,256]{2,1,0:T(8,128)S(1)}, f32[6,64,256]{2,1,0:T(8,128)S(1)}, f32[2,6,64,256]{3,2,1,0:T(8,128)S(1)}) custom-call(f32[6,2,64,256]{3,2,1,0:T(8,128)S(1)} %collective-permute-done.9.before, f32[6,2,64,256]{3,2,1,0:T(8,128)S(1)} %bitcast.4, ...), custom_call_target="tpu_custom_call" | custom-call | tf_op jit(solution)/shard_map/pallas_call | solution.py:269
  46.1 1.9 %collective-permute-start.10 = (f32[6,64,256]{2,1,0:T(8,128)S(1)}, f32[6,64,256]{2,1,0:T(8,128)S(1)}, u32[]{:S(2)}, u32[]{:S(2)}) collective-permute-start(f32[6,64,256]{2,1,0:T(8,128)S(1)} %get-tuple-element.61), channel_id=1, source_target_pairs={{16,17},{17,18},{18,19},{19,20},{20,21},{21,22},{22,23},{23,24},{2... | collective-permute-start | bytes 1179656 | tf_op jit(solution)/shard_map/ppermute | solution.py:289
  48.0 4.3 %collective-permute-start.11 = (f32[6,64,256]{2,1,0:T(8,128)S(1)}, f32[6,64,256]{2,1,0:T(8,128)S(1)}, u32[]{:S(2)}, u32[]{:S(2)}) collective-permute-start(f32[6,64,256]{2,1,0:T(8,128)S(1)} %get-tuple-element.62), channel_id=1, source_target_pairs={{17,16},{18,17},{19,18},{20,19},{21,20},{22,21},{23,22},{24,23},{2... | collective-permute-start | bytes 1179656 | tf_op jit(solution)/shard_map/ppermute | solution.py:289
  52.3 0.0 collective-permute-done.12.refs_6_
  52.3 4.0 %collective-permute-done.13.refs_7_ = f32[6,64,256]{2,1,0:T(8,128)S(1)} collective-permute-done((f32[6,64,256]{2,1,0:T(8,128)S(1)}, f32[6,64,256]{2,1,0:T(8,128)S(1)}, u32[]{:S(2)}, u32[]{:S(2)}) %collective-permute-start.13) | collective-permute-done | bytes 393248 | tf_op jit(solution)/shard_map/ppermute | solution.py:289
  56.3 1.7 %shard_map.79.fine_end = f32[6,2,64,256]{3,2,1,0:T(8,128)S(1)} custom-call(f32[4,64,256]{2,1,0:T(8,128)S(1)} %get-tuple-element.41.refs_0_.edges, f32[6,2,64,256]{3,2,1,0:T(8,128)S(1)} %get-tuple-element.63.refs_1_, f32[2,2,64,256]{3,2,1,0:T(8,128)S(1)} %get-tuple-element.42.refs_2_.moduli, f32[3,2,64,256]{3,2,1,0:T(8,128)S(1)} %get-tuple-element.43.refs_3_, ...), custom_call_target="tpu_custom_call" | custom-call | tf_op jit(solution)/shard_map/pallas_call | solution.py:269
  58.0 0.0 collective-permute-done.10.low
  58.0 2.5 %collective-permute-done.11.high = f32[6,64,256]{2,1,0:T(8,128)S(1)} collective-permute-done((f32[6,64,256]{2,1,0:T(8,128)S(1)}, f32[6,64,256]{2,1,0:T(8,128)S(1)}, u32[]{:S(2)}, u32[]{:S(2)}) %collective-permute-start.11) | collective-permute-done | bytes 393248 | tf_op jit(solution)/shard_map/ppermute | solution.py:289
  60.5 2.6 %shard_map.80 = f32[6,2,64,256]{3,2,1,0:T(8,128)} custom-call(f32[4,64,256]{2,1,0:T(8,128)S(1)} %get-tuple-element.41.refs_0_.edges, f32[6,2,64,256]{3,2,1,0:T(8,128)S(1)} %get-tuple-element.58.state, f32[2,2,64,256]{3,2,1,0:T(8,128)S(1)} %get-tuple-element.42.refs_2_.moduli, f32[3,2,64,256]{3,2,1,0:T(8,128)S(1)} %get-tuple-element.59.part, ...), custom_call_target="tpu_custom_call" | custom-call | tf_op jit(solution)/shard_map/pallas_call | solution.py:269
  (2 shorter events, 0.0 us)
Async XLA Ops:
  0.0 23.6 %copy-start = (f32[1,6,2,64,256]{4,3,2,1,0:T(8,128)S(1)}, f32[1,6,2,64,256]{4,3,2,1,0:T(8,128)}, u32[]{:S(2)}) copy-start(f32[1,6,2,64,256]{4,3,2,1,0:T(8,128)} %state_hbm.1) | copy-start | bytes 2359300
  2.3 21.3 %collective-permute-start.3 = (f32[6,64,256]{2,1,0:T(8,128)S(1)}, f32[6,64,256]{2,1,0:T(8,128)S(1)}, u32[]{:S(2)}, u32[]{:S(2)}) collective-permute-start(f32[6,64,256]{2,1,0:T(8,128)S(1)} %get-tuple-element.39.up), channel_id=1, source_target_pairs={{0,1},{1,2},{2,3},{3,4},{4,5},{5,6},{6,7},{7,8},{8,9},{9,10},{10,1... | collective-permute-start | bytes 1179656 | tf_op jit(solution)/shard_map/ppermute | solution.py:289
  3.0 20.6 %collective-permute-start.4 = (f32[6,64,256]{2,1,0:T(8,128)S(1)}, f32[6,64,256]{2,1,0:T(8,128)S(1)}, u32[]{:S(2)}, u32[]{:S(2)}) collective-permute-start(f32[6,64,256]{2,1,0:T(8,128)S(1)} %get-tuple-element.40.down), channel_id=1, source_target_pairs={{1,0},{2,1},{3,2},{4,3},{5,4},{6,5},{7,6},{8,7},{9,8},{10,9},{11,1... | collective-permute-start | bytes 1179656 | tf_op jit(solution)/shard_map/ppermute | solution.py:289
  3.7 6.9 %collective-permute-start = (f32[64,256]{1,0:T(8,128)S(1)}, f32[64,256]{1,0:T(8,128)S(1)}, u32[]{:S(2)}, u32[]{:S(2)}) collective-permute-start(f32[64,256]{1,0:T(8,128)S(1)} %get-tuple-element.37), channel_id=1, source_target_pairs={{16,17},{17,18},{18,19},{19,20},{20,21},{21,22},{22,23},{23,24},{2... | collective-permute-start | bytes 196616 | tf_op jit(solution)/shard_map/ppermute | solution.py:289
  6.8 8.4 %collective-permute-start.1 = (f32[64,256]{1,0:T(8,128)S(1)}, f32[64,256]{1,0:T(8,128)S(1)}, u32[]{:S(2)}, u32[]{:S(2)}) collective-permute-start(f32[64,256]{1,0:T(8,128)S(1)} %get-tuple-element.38), channel_id=1, source_target_pairs={{17,16},{18,17},{19,18},{20,19},{21,20},{22,21},{23,22},{24,23},{2... | collective-permute-start | bytes 196616 | tf_op jit(solution)/shard_map/ppermute | solution.py:289
  16.0 7.5 %collective-permute-start.2 = (f32[4,64,256]{2,1,0:T(8,128)S(1)}, f32[4,64,256]{2,1,0:T(8,128)S(1)}, u32[]{:S(2)}, u32[]{:S(2)}) collective-permute-start(f32[4,64,256]{2,1,0:T(8,128)S(1)} %get-tuple-element.41.refs_0_.edges), channel_id=1, source_target_pairs={{16,0},{17,1},{18,2},{19,3},{20,4},{21,5},{22,6},{23,7},{24,8},{25... | collective-permute-start | bytes 786440 | tf_op jit(solution)/shard_map/ppermute | solution.py:338
  17.4 9.4 %collective-permute-start.7 = (f32[6,64,256]{2,1,0:T(8,128)S(1)}, f32[6,64,256]{2,1,0:T(8,128)S(1)}, u32[]{:S(2)}, u32[]{:S(2)}) collective-permute-start(f32[6,64,256]{2,1,0:T(8,128)S(1)} %get-tuple-element.51), channel_id=1, source_target_pairs={{16,17},{17,18},{18,19},{19,20},{20,21},{21,22},{22,23},{23,24},{2... | collective-permute-start | bytes 1179656 | tf_op jit(solution)/shard_map/ppermute | solution.py:289
  19.9 15.5 %collective-permute-start.8 = (f32[6,64,256]{2,1,0:T(8,128)S(1)}, f32[6,64,256]{2,1,0:T(8,128)S(1)}, u32[]{:S(2)}, u32[]{:S(2)}) collective-permute-start(f32[6,64,256]{2,1,0:T(8,128)S(1)} %get-tuple-element.52), channel_id=1, source_target_pairs={{17,16},{18,17},{19,18},{20,19},{21,20},{22,21},{23,22},{24,23},{2... | collective-permute-start | bytes 1179656 | tf_op jit(solution)/shard_map/ppermute | solution.py:289
  23.6 14.1 %collective-permute-start.5 = (f32[6,64,256]{2,1,0:T(8,128)S(1)}, f32[6,64,256]{2,1,0:T(8,128)S(1)}, u32[]{:S(2)}, u32[]{:S(2)}) collective-permute-start(f32[6,64,256]{2,1,0:T(8,128)S(1)} %get-tuple-element.49), channel_id=1, source_target_pairs={{0,1},{1,2},{2,3},{3,4},{4,5},{5,6},{6,7},{7,8},{8,9},{9,10},{10,1... | collective-permute-start | bytes 1179656 | tf_op jit(solution)/shard_map/ppermute | solution.py:289
  24.3 13.4 %collective-permute-start.6 = (f32[6,64,256]{2,1,0:T(8,128)S(1)}, f32[6,64,256]{2,1,0:T(8,128)S(1)}, u32[]{:S(2)}, u32[]{:S(2)}) collective-permute-start(f32[6,64,256]{2,1,0:T(8,128)S(1)} %get-tuple-element.50), channel_id=1, source_target_pairs={{1,0},{2,1},{3,2},{4,3},{5,4},{6,5},{7,6},{8,7},{9,8},{10,9},{11,1... | collective-permute-start | bytes 1179656 | tf_op jit(solution)/shard_map/ppermute | solution.py:289
  37.8 7.5 %collective-permute-start.9 = (f32[6,2,64,256]{3,2,1,0:T(8,128)S(1)}, f32[6,2,64,256]{3,2,1,0:T(8,128)S(1)}, u32[]{:S(2)}, u32[]{:S(2)}) collective-permute-start(f32[6,2,64,256]{3,2,1,0:T(8,128)S(1)} %shard_map.77.before_end), channel_id=1, source_target_pairs={{0,16},{1,17},{2,18},{3,19},{4,20},{5,21},{6,22},{7,23},{8,24},{9,... | collective-permute-start | bytes 2359304 | tf_op jit(solution)/shard_map/ppermute | solution.py:362
  39.1 13.2 %collective-permute-start.12 = (f32[6,64,256]{2,1,0:T(8,128)S(1)}, f32[6,64,256]{2,1,0:T(8,128)S(1)}, u32[]{:S(2)}, u32[]{:S(2)}) collective-permute-start(f32[6,64,256]{2,1,0:T(8,128)S(1)} %get-tuple-element.65), channel_id=1, source_target_pairs={{16,17},{17,18},{18,19},{19,20},{20,21},{21,22},{22,23},{23,24},{2... | collective-permute-start | bytes 1179656 | tf_op jit(solution)/shard_map/ppermute | solution.py:289
  41.0 15.3 %collective-permute-start.13 = (f32[6,64,256]{2,1,0:T(8,128)S(1)}, f32[6,64,256]{2,1,0:T(8,128)S(1)}, u32[]{:S(2)}, u32[]{:S(2)}) collective-permute-start(f32[6,64,256]{2,1,0:T(8,128)S(1)} %get-tuple-element.66), channel_id=1, source_target_pairs={{17,16},{18,17},{19,18},{20,19},{21,20},{22,21},{23,22},{24,23},{2... | collective-permute-start | bytes 1179656 | tf_op jit(solution)/shard_map/ppermute | solution.py:289
  46.1 11.9 %collective-permute-start.10 = (f32[6,64,256]{2,1,0:T(8,128)S(1)}, f32[6,64,256]{2,1,0:T(8,128)S(1)}, u32[]{:S(2)}, u32[]{:S(2)}) collective-permute-start(f32[6,64,256]{2,1,0:T(8,128)S(1)} %get-tuple-element.61), channel_id=1, source_target_pairs={{16,17},{17,18},{18,19},{19,20},{20,21},{21,22},{22,23},{23,24},{2... | collective-permute-start | bytes 1179656 | tf_op jit(solution)/shard_map/ppermute | solution.py:289
  48.0 12.5 %collective-permute-start.11 = (f32[6,64,256]{2,1,0:T(8,128)S(1)}, f32[6,64,256]{2,1,0:T(8,128)S(1)}, u32[]{:S(2)}, u32[]{:S(2)}) collective-permute-start(f32[6,64,256]{2,1,0:T(8,128)S(1)} %get-tuple-element.62), channel_id=1, source_target_pairs={{17,16},{18,17},{19,18},{20,19},{21,20},{22,21},{23,22},{24,23},{2... | collective-permute-start | bytes 1179656 | tf_op jit(solution)/shard_map/ppermute | solution.py:289

commit v7 on v6

--- a/solution.py
+++ b/solution.py
@@ -15,15 +15,23 @@
 class Inplane:
     def __init__(self, u):
         rows, columns = u[0].shape
-        row = lax.broadcasted_iota(jnp.int32, (rows, columns), 0)
-        column = lax.broadcasted_iota(jnp.int32, (rows, columns), 1)
+        tile, lanes = 8, columns // 2
+        row = lax.broadcasted_iota(jnp.int32, (tile, columns), 0)
+        lane = lax.broadcasted_iota(jnp.int32, (rows, lanes), 1)
 
         def shifted(f, axis, up):
+            turned = pltpu.roll(f, f.shape[axis] - 1 if up else 1, axis)
+            if axis == 0 and up:
+                edge = jnp.where(row == tile - 1, 0.0, turned[rows - tile :])
+                return jnp.concatenate([turned[: rows - tile], edge], axis=0)
+            if axis == 0:
+                edge = jnp.where(row == 0, 0.0, turned[:tile])
+                return jnp.concatenate([edge, turned[tile:]], axis=0)
             if up:
-                edge = (row == rows - 1, column == columns - 1)[axis]
-                return jnp.where(edge, 0.0, pltpu.roll(f, f.shape[axis] - 1, axis))
-            edge = (row == 0, column == 0)[axis]
-            return jnp.where(edge, 0.0, pltpu.roll(f, 1, axis))
+                edge = jnp.where(lane == lanes - 1, 0.0, turned[:, lanes:])
+                return jnp.concatenate([turned[:, :lanes], edge], axis=1)
+            edge = jnp.where(lane == 0, 0.0, turned[:, :lanes])
+            return jnp.concatenate([edge, turned[:, lanes:]], axis=1)
 
         self.u = u
         self.shifted = shifted
@@ -72,10 +80,10 @@
     return (*inplane.even, *inplane.odd, inplane.u[2])
 
 
-def partial_step(planes, velocity, shear, bulk, load, step):
+def own_sums(planes):
     count = len(planes)
     outgoing = [sums_of(p) for p in planes]
-    velocities, displaced = [], []
+    sums = []
     for z, plane in enumerate(planes):
         even, other = plane.own()
         for neighbour, sign in ((z - 1, -1.0), (z + 1, 1.0)):
@@ -83,50 +91,54 @@
                 e, o = towards(outgoing[neighbour], sign)
                 even = [a + b for a, b in zip(even, e)]
                 other = [a + b for a, b in zip(other, o)]
-        v = [
-            velocity(c, z) + step * (shear(z) * even[c] + bulk(z) * other[c] + load(c, z))
-            for c in range(3)
-        ]
-        velocities.append(v)
-        displaced.append([plane.u[c] + step * v[c] for c in range(3)])
-    return velocities, displaced, outgoing
-
-
-def prepare(planes, velocity, shear, bulk, load, step, part_ref, up_ref, down_ref, rim_ref):
-    count = len(planes)
-    velocities, displaced, outgoing = partial_step(planes, velocity, shear, bulk, load, step)
-    for z in range(count):
+        sums.append((even, other))
+    return sums, outgoing
+
+
+def moved(sums, u, velocity, shear, bulk, load, step):
+    even, other = sums
+    v = [velocity[c] + step * (shear * even[c] + bulk * other[c] + load[c]) for c in range(3)]
+    return v, [u[c] + step * v[c] for c in range(3)]
+
+
+def prepare(sums, planes, velocity, shear, bulk, load, step, part_ref, up_ref, down_ref, rim_ref):
+    sums, outgoing = sums
+    last = len(planes) - 1
+    for z, plane in enumerate(planes):
+        v, displaced = moved(
+            sums[z], plane.u, [velocity(c, z) for c in range(3)], shear(z), bulk(z),
+            [load(c, z) for c in range(3)], step,
+        )
         for c in range(3):
-            part_ref[c, z] = velocities[z][c]
-    for c in range(3):
-        down_ref[c] = planes[0].u[c]
-        down_ref[3 + c] = displaced[0][c]
-        up_ref[c] = planes[count - 1].u[c]
-        up_ref[3 + c] = displaced[count - 1][c]
+            part_ref[c, z] = v[c]
+            for edge, ref in ((0, down_ref), (last, up_ref)):
+                if z == edge:
+                    ref[c] = plane.u[c]
+                    ref[3 + c] = displaced[c]
     for c in range(6):
         rim_ref[0, c] = outgoing[0][c]
-        rim_ref[1, c] = outgoing[count - 1][c]
-
-
-def zone_values(zone, shear_table, lame_table, offset):
+        rim_ref[1, c] = outgoing[last][c]
+
+
+def zone_values(zone, shear_of, lame_of, zones, offset):
     shear = jnp.zeros(zone.shape, jnp.float32)
     bulk = jnp.zeros(zone.shape, jnp.float32)
-    for k in range(shear_table.shape[0]):
+    for k in range(zones):
         hit = zone == k + offset
-        shear = jnp.where(hit, shear_table[k], shear)
-        bulk = jnp.where(hit, shear_table[k] + lame_table[k], bulk)
+        shear = jnp.where(hit, shear_of(k), shear)
+        bulk = jnp.where(hit, shear_of(k) + lame_of(k), bulk)
     return shear, bulk
 
 
 def open_kernel(
     step, state_hbm, load_hbm, zones_hbm, shear_hbm, lame_hbm, amp_hbm, cycle_hbm,
-    moduli, loading, part, up, down, rim, zone_up, zone_down,
+    moduli, loading, part, up, down, rim, zone_up, zone_down, zone_rows,
     state, load_shape, zones, shear_table, lame_table, amp_table, cycle_index, arrived,
 ):
     pairs = (
-        (state_hbm.at[0], state), (cycle_hbm, cycle_index), (amp_hbm, amp_table),
-        (shear_hbm, shear_table), (lame_hbm, lame_table), (zones_hbm, zones),
-        (load_hbm, load_shape),
+        (state_hbm.at[0, :3], state.at[:3]), (shear_hbm, shear_table), (lame_hbm, lame_table),
+        (zones_hbm, zones), (cycle_hbm, cycle_index), (amp_hbm, amp_table),
+        (load_hbm, load_shape), (state_hbm.at[0, 3:], state.at[3:]),
     )
     copies = [
         pltpu.make_async_copy(source, target, arrived.at[i])
@@ -134,17 +146,23 @@
     ]
     for copy in copies:
         copy.start()
-    for copy in copies:
+    copies[0].wait()
+    count, _, columns = zones.shape
+    planes = [Inplane([state[c, z] for c in range(3)]) for z in range(count)]
+    sums = own_sums(planes)
+    for copy in copies[1:]:
         copy.wait()
-    count = zones.shape[0]
+    kinds = shear_table.shape[0]
+    for z in range(count):
+        moduli[0, z], moduli[1, z] = zone_values(
+            zones[z], lambda k: shear_table[k], lambda k: lame_table[k], kinds, 0
+        )
     amplitude = amp_table[cycle_index[lax.axis_index("win")]]
     for z in range(count):
-        moduli[0, z], moduli[1, z] = zone_values(zones[z], shear_table, lame_table, 0)
         for c in range(3):
             loading[c, z] = amplitude * load_shape[c, z].astype(jnp.float32)
-    planes = [Inplane([state[c, z] for c in range(3)]) for z in range(count)]
     prepare(
-        planes,
+        sums, planes,
         lambda c, z: state[3 + c, z],
         lambda z: moduli[0, z],
         lambda z: moduli[1, z],
@@ -153,6 +171,9 @@
     )
     zone_down[...] = (zones[0] + 1).astype(jnp.float32)
     zone_up[...] = (zones[count - 1] + 1).astype(jnp.float32)
+    for k in range(kinds):
+        zone_rows[k] = jnp.full((1, columns), shear_table[k], jnp.float32)
+        zone_rows[kinds + k] = jnp.full((1, columns), lame_table[k], jnp.float32)
 
 
 def two_steps(step, u0, part, rim, low, high, moduli, edges, load):
@@ -179,35 +200,36 @@
     planes = [
         Inplane([u0[c, z] + step * velocities[z][c] for c in range(3)]) for z in range(count)
     ]
-    shear = lambda z: moduli[0, z]
-    bulk = lambda z: moduli[1, z]
-    ends, _, _ = partial_step(planes, lambda c, z: velocities[z][c], shear, bulk, load, step)
+    sums, _ = own_sums(planes)
     for side, (got, edge, z, sign) in enumerate(sides):
-        even, odd = towards(sums_of(Inplane(outer[side])), sign)
-        for c in range(3):
-            ends[z][c] = ends[z][c] + step * (shear(z) * even[c] + bulk(z) * odd[c])
-    displaced = [[planes[z].u[c] + step * ends[z][c] for c in range(3)] for z in range(count)]
-    return ends, displaced
-
-
-def edge_kernel(
-    shear_hbm, lame_hbm, zone_low, zone_high, up, down, edges, later_up, later_down,
-    shear_table, lame_table, arrived,
-):
+        part_of = towards(sums_of(Inplane(outer[side])), sign)
+        sums[z] = tuple([a + b for a, b in zip(x, y)] for x, y in zip(sums[z], part_of))
+    return [
+        moved(
+            sums[z], planes[z].u, velocities[z], moduli[0, z], moduli[1, z],
+            [load(c, z) for c in range(3)], step,
+        )
+        for z in range(count)
+    ]
+
+
+def edge_kernel(zone_low, zone_high, zone_rows, up, down, edges, later_up, later_down):
     @pl.when(lax.axis_index("win") != 0)
     def _():
-        copies = [
-            pltpu.make_async_copy(shear_hbm, shear_table, arrived.at[0]),
-            pltpu.make_async_copy(lame_hbm, lame_table, arrived.at[1]),
-        ]
-        for copy in copies:
-            copy.start()
+        kinds = zone_rows.shape[0] // 2
+        for i, zone in enumerate((zone_low, zone_high)):
+            edges[2 * i], edges[2 * i + 1] = zone_values(
+                zone[...], lambda k: zone_rows[k], lambda k: zone_rows[kinds + k], kinds, 1.0
+            )
         later_up[...] = up[...]
         later_down[...] = down[...]
-        for copy in copies:
-            copy.wait()
-        edges[0], edges[1] = zone_values(zone_low[...], shear_table, lame_table, 1.0)
-        edges[2], edges[3] = zone_values(zone_high[...], shear_table, lame_table, 1.0)
+
+
+def stored(state, ends):
+    for z, (v, u) in enumerate(ends):
+        for c in range(3):
+            state[c, z] = u[c]
+            state[3 + c, z] = v[c]
 
 
 def fine_kernel(step, last, group, *refs):
@@ -217,60 +239,69 @@
 
 
 def fine_pair(step, last, edges, state, moduli, loading, part, rim, low, high, *outs):
-    count = moduli.shape[1]
     load = lambda c, z: loading[c, z]
-    ends, displaced = two_steps(step, state, part, rim, low, high, moduli, edges, load)
-    new_state = outs[0]
-    for z in range(count):
-        for c in range(3):
-            new_state[c, z] = displaced[z][c]
-            new_state[3 + c, z] = ends[z][c]
+    ends = two_steps(step, state, part, rim, low, high, moduli, edges, load)
+    stored(outs[0], ends)
     if not last:
-        planes = [Inplane(displaced[z]) for z in range(count)]
+        planes = [Inplane(u) for _, u in ends]
         prepare(
-            planes, lambda c, z: ends[z][c], lambda z: moduli[0, z], lambda z: moduli[1, z],
-            load, step, *outs[1:],
+            own_sums(planes), planes, lambda c, z: ends[z][0][c], lambda z: moduli[0, z],
+            lambda z: moduli[1, z], load, step, *outs[1:],
         )
 
 
 def coarse_open_kernel(before, start, moduli, difference, part, up, down, rim):
     count = moduli.shape[1]
+    planes = []
     for z in range(count):
         for c in range(6):
             difference[c, z] = before[c, z] - start[c, z]
-    planes = [Inplane([difference[c, z] for c in range(3)]) for z in range(count)]
+        planes.append(Inplane([difference[c, z] for c in range(3)]))
     prepare(
-        planes, lambda c, z: difference[3 + c, z], lambda z: moduli[0, z],
+        own_sums(planes), planes, lambda c, z: difference[3 + c, z], lambda z: moduli[0, z],
         lambda z: moduli[1, z], lambda c, z: 0.0, DT_COARSE, part, up, down, rim,
     )
 
 
-def coarse_kernel(edges, state, moduli, part, rim, low, high, before_end, fine_end, new_end):
+def coarse_kernel(
+    edges, state, moduli, part, rim, low, high, before_end, fine_end, new_end, end, left
+):
+    copies = [
+        pltpu.make_async_copy(end.at[:, z], new_end.at[:, z], left.at[z])
+        for z in range(moduli.shape[1])
+    ]
+
     @pl.when(lax.axis_index("win") == 0)
     def _():
-        new_end[...] = before_end[...]
+        end[...] = before_end[...]
+        for copy in copies:
+            copy.start()
 
     @pl.when(lax.axis_index("win") != 0)
     def _():
-        ends, displaced = two_steps(
+        ends = two_steps(
             DT_COARSE, state, part, rim, low, high, moduli, edges, lambda c, z: 0.0
         )
-        for z in range(moduli.shape[1]):
+        for z, (v, u) in enumerate(ends):
             for c in range(3):
-                new_end[c, z] = fine_end[c, z] + displaced[z][c]
-                new_end[3 + c, z] = fine_end[3 + c, z] + ends[z][c]
+                end[c, z] = fine_end[c, z] + u[c]
+                end[3 + c, z] = fine_end[3 + c, z] + v[c]
+            copies[z].start()
+
+    for copy in copies:
+        copy.wait()
 
 
 VMEM = pl.BlockSpec(memory_space=pltpu.VMEM)
 HBM = pl.BlockSpec(memory_space=pltpu.HBM)
 
 
-def called(kernel, outs, *operands, in_specs=None, scratch=()):
+def called(kernel, outs, *operands, in_specs=None, out_specs=None, scratch=()):
     return pl.pallas_call(
         kernel,
         out_shape=[jax.ShapeDtypeStruct(shape, jnp.float32) for shape in outs],
         in_specs=in_specs or [VMEM] * len(operands),
-        out_specs=[VMEM] * len(outs),
+        out_specs=out_specs or [VMEM] * len(outs),
         scratch_shapes=list(scratch),
         compiler_params=pltpu.CompilerParams(vmem_limit_bytes=16 * 1024 * 1024),
     )(*operands)
@@ -305,9 +336,10 @@
 
     given = (states, load_shape, zone_ids, zone_shear, zone_lame, amp_table, cycle_index)
     tables = [pltpu.SMEM(table.shape, table.dtype) for table in given[3:]]
-    moduli, loading, part, up, down, rim, zone_up, zone_down = called(
+    zone_rows = (2 * zone_shear.shape[0], 1, columns)
+    moduli, loading, part, up, down, rim, zone_up, zone_down, zone_rows = called(
         functools.partial(open_kernel, DT_FINE),
-        [(2, count, *plane), field, field, message, message, rims, plane, plane],
+        [(2, count, *plane), field, field, message, message, rims, plane, plane, zone_rows],
         *in_hbm(*given),
         in_specs=[HBM] * len(given),
         scratch=[
@@ -315,7 +347,7 @@
             pltpu.VMEM(load_shape.shape, load_shape.dtype),
             pltpu.VMEM(zone_ids.shape, zone_ids.dtype),
             *tables,
-            pltpu.SemaphoreType.DMA((len(given),)),
+            pltpu.SemaphoreType.DMA((len(given) + 1,)),
         ],
     )
     def fine(turn, group, *operands):
@@ -331,9 +363,7 @@
     low, high = exchanged(up, down, 0)
     edges, later_up, later_down = called(
         edge_kernel, [(4, *plane), message, message],
-        *in_hbm(zone_shear, zone_lame), *exchanged(zone_up, zone_down, 1), up, down,
-        in_specs=[HBM] * 2 + [VMEM] * 4,
-        scratch=[*tables[:2], pltpu.SemaphoreType.DMA((2,))],
+        *exchanged(zone_up, zone_down, 1), zone_rows, up, down,
     )
     edges = lax.ppermute(edges, "win", [(1, 0)]), edges
     later_low, later_high = exchanged(later_up, later_down, 1)
@@ -373,6 +403,8 @@
         new_end = called(
             coarse_kernel, [state],
             edges[1], difference, moduli, part, rim, low, high, ends[0], fine_end,
+            out_specs=[HBM],
+            scratch=[pltpu.VMEM(state, jnp.float32), pltpu.SemaphoreType.DMA((count,))],
         )[0]
     return new_end[None]
 

time: 64.2 us -> 62.7 us (0.977)
  Pallas kernels: 10.6 us -> 9.63 us
    pallas_call x8, Pallas kernels: 10.6 us -> 9.63 us  [called(): pl.pallas_call(kernel, out_shape=[jax.ShapeDtypeStruct(shape, jnp.float32...]
    ppermute x12, waiting for transfers between devices: 22.2 us -> 21.6 us  [passed(): return lax.ppermute(block, ('win', 'slab'), route)]
  transfers between devices with their start and end apart: 14 -> 14, of which waited for: 6 -> 6; matrix products, arithmetic and copies ran while one was open for 0% -> 0% of each run, Pallas kernels for 9% -> 8%
where the time goes in v7:
time: 62.7 us; the launch traced here: 61.7 us
  starting transfers between devices  30.1 us (48%)
  waiting for transfers between devices  21.6 us (34%)
  Pallas kernels  9.63 us (15%)
    ppermute x12, starting transfers between devices, passed(): return lax.ppermute(block, ('win', 'slab'), route)  27.5 us
    ppermute x12, waiting for transfers between devices, passed(): return lax.ppermute(block, ('win', 'slab'), route)  21.6 us
    pallas_call x8, Pallas kernels, called(): pl.pallas_call(kernel, out_shape=[jax.ShapeDtypeStruct(shape, jnp.float32...  9.63 us
    ppermute x1, starting transfers between devices, shards(): edges = (lax.ppermute(edges, 'win', [(1, 0)]), edges)  1.31 us
    ppermute x1, starting transfers between devices, shards(): lax.ppermute(new_end, 'win', [(n, n + 1) for n in range(windows - 1)])  1.29 us
  transfers between devices with their start and end apart: 14, of which 6 were waited for; matrix products, arithmetic and copies ran while one was open for 0% of the time, Pallas kernels for 8%

profile of v7, /device:TPU:13, one launch (start us, length us, event | category | flops | bytes accessed | tf_op | source)
XLA Modules:
  0.0 61.7 jit_solution(5220670567326236726)
XLA Ops:
  0.0 0.0 copy-start
  0.0 2.2 %shard_map.73 = (f32[2,2,64,256]{3,2,1,0:T(8,128)S(1)}, f32[3,2,64,256]{3,2,1,0:T(8,128)S(1)}, f32[3,2,64,256]{3,2,1,0:T(8,128)S(1)}, f32[6,64,256]{2,1,0:T(8,12...) custom-call(f32[1,6,2,64,256]{4,3,2,1,0:T(8,128)} %state_hbm.1, ...), custom_call_target="tpu_custom_call" | custom-call | tf_op jit(solution)/shard_map/pallas_call | solution.py:300
  2.3 0.7 %collective-permute-start.3 = (f32[6,64,256]{2,1,0:T(8,128)S(1)}, f32[6,64,256]{2,1,0:T(8,128)S(1)}, u32[]{:S(2)}, u32[]{:S(2)}) collective-permute-start(f32[6,64,256]{2,1,0:T(8,128)S(1)} %get-tuple-element.41.up), channel_id=1, source_target_pairs={{0,1},{1,2},{2,3},{3,4},{4,5},{5,6},{6,7},{7,8},{8,9},{9,10},{10,1... | collective-permute-start | bytes 1179656 | tf_op jit(solution)/shard_map/ppermute | solution.py:320
  2.9 0.7 %collective-permute-start.4 = (f32[6,64,256]{2,1,0:T(8,128)S(1)}, f32[6,64,256]{2,1,0:T(8,128)S(1)}, u32[]{:S(2)}, u32[]{:S(2)}) collective-permute-start(f32[6,64,256]{2,1,0:T(8,128)S(1)} %get-tuple-element.42.down), channel_id=1, source_target_pairs={{1,0},{2,1},{3,2},{4,3},{5,4},{6,5},{7,6},{8,7},{9,8},{10,9},{11,1... | collective-permute-start | bytes 1179656 | tf_op jit(solution)/shard_map/ppermute | solution.py:320
  3.6 3.1 %collective-permute-start = (f32[64,256]{1,0:T(8,128)S(1)}, f32[64,256]{1,0:T(8,128)S(1)}, u32[]{:S(2)}, u32[]{:S(2)}) collective-permute-start(f32[64,256]{1,0:T(8,128)S(1)} %get-tuple-element.38), channel_id=1, source_target_pairs={{16,17},{17,18},{18,19},{19,20},{20,21},{21,22},{22,23},{23,24},{2... | collective-permute-start | bytes 196616 | tf_op jit(solution)/shard_map/ppermute | solution.py:320
  6.8 3.1 %collective-permute-start.1 = (f32[64,256]{1,0:T(8,128)S(1)}, f32[64,256]{1,0:T(8,128)S(1)}, u32[]{:S(2)}, u32[]{:S(2)}) collective-permute-start(f32[64,256]{1,0:T(8,128)S(1)} %get-tuple-element.39), channel_id=1, source_target_pairs={{17,16},{18,17},{19,18},{20,19},{21,20},{22,21},{23,22},{24,23},{2... | collective-permute-start | bytes 196616 | tf_op jit(solution)/shard_map/ppermute | solution.py:320
  9.8 0.7 %collective-permute-done.zone_low = f32[64,256]{1,0:T(8,128)S(1)} collective-permute-done((f32[64,256]{1,0:T(8,128)S(1)}, f32[64,256]{1,0:T(8,128)S(1)}, u32[]{:S(2)}, u32[]{:S(2)}) %collective-permute-start) | collective-permute-done | bytes 65568 | tf_op jit(solution)/shard_map/ppermute | solution.py:320
  10.5 4.6 %collective-permute-done.1.zone_high = f32[64,256]{1,0:T(8,128)S(1)} collective-permute-done((f32[64,256]{1,0:T(8,128)S(1)}, f32[64,256]{1,0:T(8,128)S(1)}, u32[]{:S(2)}, u32[]{:S(2)}) %collective-permute-start.1) | collective-permute-done | bytes 65568 | tf_op jit(solution)/shard_map/ppermute | solution.py:320
  15.2 0.1 shard_map.74
  15.3 1.3 %collective-permute-start.2 = (f32[4,64,256]{2,1,0:T(8,128)S(1)}, f32[4,64,256]{2,1,0:T(8,128)S(1)}, u32[]{:S(2)}, u32[]{:S(2)}) collective-permute-start(f32[4,64,256]{2,1,0:T(8,128)S(1)} %get-tuple-element.43.refs_0_.edges), channel_id=1, source_target_pairs={{16,0},{17,1},{18,2},{19,3},{20,4},{21,5},{22,6},{23,7},{24,8},{25... | collective-permute-start | bytes 786440 | tf_op jit(solution)/shard_map/ppermute | solution.py:368
  16.6 2.5 %collective-permute-start.7 = (f32[6,64,256]{2,1,0:T(8,128)S(1)}, f32[6,64,256]{2,1,0:T(8,128)S(1)}, u32[]{:S(2)}, u32[]{:S(2)}) collective-permute-start(f32[6,64,256]{2,1,0:T(8,128)S(1)} %get-tuple-element.53), channel_id=1, source_target_pairs={{16,17},{17,18},{18,19},{19,20},{20,21},{21,22},{22,23},{23,24},{2... | collective-permute-start | bytes 1179656 | tf_op jit(solution)/shard_map/ppermute | solution.py:320
  19.1 3.7 %collective-permute-start.8 = (f32[6,64,256]{2,1,0:T(8,128)S(1)}, f32[6,64,256]{2,1,0:T(8,128)S(1)}, u32[]{:S(2)}, u32[]{:S(2)}) collective-permute-start(f32[6,64,256]{2,1,0:T(8,128)S(1)} %get-tuple-element.54), channel_id=1, source_target_pairs={{17,16},{18,17},{19,18},{20,19},{21,20},{22,21},{23,22},{24,23},{2... | collective-permute-start | bytes 1179656 | tf_op jit(solution)/shard_map/ppermute | solution.py:320
  22.8 0.0 collective-permute-done.2.refs_0_
  22.8 0.0 collective-permute-done.3.refs_6_
  22.8 0.0 collective-permute-done.4.refs_7_
  22.8 0.0 copy-done
  22.9 0.7 %collective-permute-start.5 = (f32[6,64,256]{2,1,0:T(8,128)S(1)}, f32[6,64,256]{2,1,0:T(8,128)S(1)}, u32[]{:S(2)}, u32[]{:S(2)}) collective-permute-start(f32[6,64,256]{2,1,0:T(8,128)S(1)} %get-tuple-element.51), channel_id=1, source_target_pairs={{0,1},{1,2},{2,3},{3,4},{4,5},{5,6},{6,7},{7,8},{8,9},{9,10},{10,1... | collective-permute-start | bytes 1179656 | tf_op jit(solution)/shard_map/ppermute | solution.py:320
  23.6 0.7 %collective-permute-start.6 = (f32[6,64,256]{2,1,0:T(8,128)S(1)}, f32[6,64,256]{2,1,0:T(8,128)S(1)}, u32[]{:S(2)}, u32[]{:S(2)}) collective-permute-start(f32[6,64,256]{2,1,0:T(8,128)S(1)} %get-tuple-element.52), channel_id=1, source_target_pairs={{1,0},{2,1},{3,2},{4,3},{5,4},{6,5},{7,6},{8,7},{9,8},{10,9},{11,1... | collective-permute-start | bytes 1179656 | tf_op jit(solution)/shard_map/ppermute | solution.py:320
  24.3 1.8 %collective-permute-done.7.refs_6_ = f32[6,64,256]{2,1,0:T(8,128)S(1)} collective-permute-done((f32[6,64,256]{2,1,0:T(8,128)S(1)}, f32[6,64,256]{2,1,0:T(8,128)S(1)}, u32[]{:S(2)}, u32[]{:S(2)}) %collective-permute-start.7) | collective-permute-done | bytes 393248 | tf_op jit(solution)/shard_map/ppermute | solution.py:320
  26.0 7.9 %collective-permute-done.8.refs_7_ = f32[6,64,256]{2,1,0:T(8,128)S(1)} collective-permute-done((f32[6,64,256]{2,1,0:T(8,128)S(1)}, f32[6,64,256]{2,1,0:T(8,128)S(1)}, u32[]{:S(2)}, u32[]{:S(2)}) %collective-permute-start.8) | collective-permute-done | bytes 393248 | tf_op jit(solution)/shard_map/ppermute | solution.py:320
  34.0 2.4 %shard_map.76 = (f32[6,2,64,256]{3,2,1,0:T(8,128)S(1)}, f32[3,2,64,256]{3,2,1,0:T(8,128)S(1)}, f32[6,64,256]{2,1,0:T(8,128)S(1)}, f32[6,64,256]{2,1,0:T(8,128)S(1)}, f32[2,6,64,256]{3,2,1,0:T(8,128)S(1)}) custom-call(f32[4,64,256]{2,1,0:T(8,128)S(1)} %get-tuple-element.43.refs_0_.edges, f32[6,2,64,256]{3,2,1,0:T(8,128)S(1)} %bitcast.3, ...), custom_call_target="tpu_custom_call" | custom-call | tf_op jit(solution)/shard_map/pallas_call | solution.py:300
  36.3 0.0 collective-permute-done.5.refs_6_
  36.3 0.0 collective-permute-done.6.refs_7_
  36.4 1.3 %collective-permute-start.9 = (f32[6,2,64,256]{3,2,1,0:T(8,128)S(1)}, f32[6,2,64,256]{3,2,1,0:T(8,128)S(1)}, u32[]{:S(2)}, u32[]{:S(2)}) collective-permute-start(f32[6,2,64,256]{3,2,1,0:T(8,128)S(1)} %shard_map.77.before_end), channel_id=1, source_target_pairs={{0,16},{1,17},{2,18},{3,19},{4,20},{5,21},{6,22},{7,23},{8,24},{9,... | collective-permute-start | bytes 2359304 | tf_op jit(solution)/shard_map/ppermute | solution.py:392
  37.7 1.9 %collective-permute-start.12 = (f32[6,64,256]{2,1,0:T(8,128)S(1)}, f32[6,64,256]{2,1,0:T(8,128)S(1)}, u32[]{:S(2)}, u32[]{:S(2)}) collective-permute-start(f32[6,64,256]{2,1,0:T(8,128)S(1)} %get-tuple-element.67), channel_id=1, source_target_pairs={{16,17},{17,18},{18,19},{19,20},{20,21},{21,22},{22,23},{23,24},{2... | collective-permute-start | bytes 1179656 | tf_op jit(solution)/shard_map/ppermute | solution.py:320
  39.6 4.3 %collective-permute-start.13 = (f32[6,64,256]{2,1,0:T(8,128)S(1)}, f32[6,64,256]{2,1,0:T(8,128)S(1)}, u32[]{:S(2)}, u32[]{:S(2)}) collective-permute-start(f32[6,64,256]{2,1,0:T(8,128)S(1)} %get-tuple-element.68), channel_id=1, source_target_pairs={{17,16},{18,17},{19,18},{20,19},{21,20},{22,21},{23,22},{24,23},{2... | collective-permute-start | bytes 1179656 | tf_op jit(solution)/shard_map/ppermute | solution.py:320
  43.9 0.0 collective-permute-done.9.before
  43.9 0.8 %shard_map.78 = (f32[6,2,64,256]{3,2,1,0:T(8,128)S(1)}, f32[3,2,64,256]{3,2,1,0:T(8,128)S(1)}, f32[6,64,256]{2,1,0:T(8,128)S(1)}, f32[6,64,256]{2,1,0:T(8,128)S(1)}, f32[2,6,64,256]{3,2,1,0:T(8,128)S(1)}) custom-call(f32[6,2,64,256]{3,2,1,0:T(8,128)S(1)} %collective-permute-done.9.before, f32[6,2,64,256]{3,2,1,0:T(8,128)S(1)} %bitcast.4, ...), custom_call_target="tpu_custom_call" | custom-call | tf_op jit(solution)/shard_map/pallas_call | solution.py:300
  44.7 1.9 %collective-permute-start.10 = (f32[6,64,256]{2,1,0:T(8,128)S(1)}, f32[6,64,256]{2,1,0:T(8,128)S(1)}, u32[]{:S(2)}, u32[]{:S(2)}) collective-permute-start(f32[6,64,256]{2,1,0:T(8,128)S(1)} %get-tuple-element.63), channel_id=1, source_target_pairs={{16,17},{17,18},{18,19},{19,20},{20,21},{21,22},{22,23},{23,24},{2... | collective-permute-start | bytes 1179656 | tf_op jit(solution)/shard_map/ppermute | solution.py:320
  46.6 4.3 %collective-permute-start.11 = (f32[6,64,256]{2,1,0:T(8,128)S(1)}, f32[6,64,256]{2,1,0:T(8,128)S(1)}, u32[]{:S(2)}, u32[]{:S(2)}) collective-permute-start(f32[6,64,256]{2,1,0:T(8,128)S(1)} %get-tuple-element.64), channel_id=1, source_target_pairs={{17,16},{18,17},{19,18},{20,19},{21,20},{22,21},{23,22},{24,23},{2... | collective-permute-start | bytes 1179656 | tf_op jit(solution)/shard_map/ppermute | solution.py:320
  50.9 0.0 collective-permute-done.12.refs_6_
  50.9 4.0 %collective-permute-done.13.refs_7_ = f32[6,64,256]{2,1,0:T(8,128)S(1)} collective-permute-done((f32[6,64,256]{2,1,0:T(8,128)S(1)}, f32[6,64,256]{2,1,0:T(8,128)S(1)}, u32[]{:S(2)}, u32[]{:S(2)}) %collective-permute-start.13) | collective-permute-done | bytes 393248 | tf_op jit(solution)/shard_map/ppermute | solution.py:320
  54.9 1.6 %shard_map.79.fine_end = f32[6,2,64,256]{3,2,1,0:T(8,128)S(1)} custom-call(f32[4,64,256]{2,1,0:T(8,128)S(1)} %get-tuple-element.43.refs_0_.edges, f32[6,2,64,256]{3,2,1,0:T(8,128)S(1)} %get-tuple-element.65.refs_1_, f32[2,2,64,256]{3,2,1,0:T(8,128)S(1)} %get-tuple-element.44.refs_2_.moduli, f32[3,2,64,256]{3,2,1,0:T(8,128)S(1)} %get-tuple-element.45.refs_3_, ...), custom_call_target="tpu_custom_call" | custom-call | tf_op jit(solution)/shard_map/pallas_call | solution.py:300
  56.5 0.0 collective-permute-done.10.low
  56.6 2.6 %collective-permute-done.11.high = f32[6,64,256]{2,1,0:T(8,128)S(1)} collective-permute-done((f32[6,64,256]{2,1,0:T(8,128)S(1)}, f32[6,64,256]{2,1,0:T(8,128)S(1)}, u32[]{:S(2)}, u32[]{:S(2)}) %collective-permute-start.11) | collective-permute-done | bytes 393248 | tf_op jit(solution)/shard_map/ppermute | solution.py:320
  59.1 2.4 %shard_map.80 = f32[6,2,64,256]{3,2,1,0:T(8,128)} custom-call(f32[4,64,256]{2,1,0:T(8,128)S(1)} %get-tuple-element.43.refs_0_.edges, f32[6,2,64,256]{3,2,1,0:T(8,128)S(1)} %get-tuple-element.60.state, f32[2,2,64,256]{3,2,1,0:T(8,128)S(1)} %get-tuple-element.44.refs_2_.moduli, f32[3,2,64,256]{3,2,1,0:T(8,128)S(1)} %get-tuple-element.61.part, ...), custom_call_target="tpu_custom_call" | custom-call | tf_op jit(solution)/shard_map/pallas_call | solution.py:300
  (2 shorter events, 0.0 us)
Async XLA Ops:
  0.0 22.8 %copy-start = (f32[1,6,2,64,256]{4,3,2,1,0:T(8,128)S(1)}, f32[1,6,2,64,256]{4,3,2,1,0:T(8,128)}, u32[]{:S(2)}) copy-start(f32[1,6,2,64,256]{4,3,2,1,0:T(8,128)} %state_hbm.1) | copy-start | bytes 2359300
  2.3 20.6 %collective-permute-start.3 = (f32[6,64,256]{2,1,0:T(8,128)S(1)}, f32[6,64,256]{2,1,0:T(8,128)S(1)}, u32[]{:S(2)}, u32[]{:S(2)}) collective-permute-start(f32[6,64,256]{2,1,0:T(8,128)S(1)} %get-tuple-element.41.up), channel_id=1, source_target_pairs={{0,1},{1,2},{2,3},{3,4},{4,5},{5,6},{6,7},{7,8},{8,9},{9,10},{10,1... | collective-permute-start | bytes 1179656 | tf_op jit(solution)/shard_map/ppermute | solution.py:320
  2.9 19.9 %collective-permute-start.4 = (f32[6,64,256]{2,1,0:T(8,128)S(1)}, f32[6,64,256]{2,1,0:T(8,128)S(1)}, u32[]{:S(2)}, u32[]{:S(2)}) collective-permute-start(f32[6,64,256]{2,1,0:T(8,128)S(1)} %get-tuple-element.42.down), channel_id=1, source_target_pairs={{1,0},{2,1},{3,2},{4,3},{5,4},{6,5},{7,6},{8,7},{9,8},{10,9},{11,1... | collective-permute-start | bytes 1179656 | tf_op jit(solution)/shard_map/ppermute | solution.py:320
  3.6 6.9 %collective-permute-start = (f32[64,256]{1,0:T(8,128)S(1)}, f32[64,256]{1,0:T(8,128)S(1)}, u32[]{:S(2)}, u32[]{:S(2)}) collective-permute-start(f32[64,256]{1,0:T(8,128)S(1)} %get-tuple-element.38), channel_id=1, source_target_pairs={{16,17},{17,18},{18,19},{19,20},{20,21},{21,22},{22,23},{23,24},{2... | collective-permute-start | bytes 196616 | tf_op jit(solution)/shard_map/ppermute | solution.py:320
  6.8 8.4 %collective-permute-start.1 = (f32[64,256]{1,0:T(8,128)S(1)}, f32[64,256]{1,0:T(8,128)S(1)}, u32[]{:S(2)}, u32[]{:S(2)}) collective-permute-start(f32[64,256]{1,0:T(8,128)S(1)} %get-tuple-element.39), channel_id=1, source_target_pairs={{17,16},{18,17},{19,18},{20,19},{21,20},{22,21},{23,22},{24,23},{2... | collective-permute-start | bytes 196616 | tf_op jit(solution)/shard_map/ppermute | solution.py:320
  15.3 7.5 %collective-permute-start.2 = (f32[4,64,256]{2,1,0:T(8,128)S(1)}, f32[4,64,256]{2,1,0:T(8,128)S(1)}, u32[]{:S(2)}, u32[]{:S(2)}) collective-permute-start(f32[4,64,256]{2,1,0:T(8,128)S(1)} %get-tuple-element.43.refs_0_.edges), channel_id=1, source_target_pairs={{16,0},{17,1},{18,2},{19,3},{20,4},{21,5},{22,6},{23,7},{24,8},{25... | collective-permute-start | bytes 786440 | tf_op jit(solution)/shard_map/ppermute | solution.py:368
  16.6 9.4 %collective-permute-start.7 = (f32[6,64,256]{2,1,0:T(8,128)S(1)}, f32[6,64,256]{2,1,0:T(8,128)S(1)}, u32[]{:S(2)}, u32[]{:S(2)}) collective-permute-start(f32[6,64,256]{2,1,0:T(8,128)S(1)} %get-tuple-element.53), channel_id=1, source_target_pairs={{16,17},{17,18},{18,19},{19,20},{20,21},{21,22},{22,23},{23,24},{2... | collective-permute-start | bytes 1179656 | tf_op jit(solution)/shard_map/ppermute | solution.py:320
  19.1 14.8 %collective-permute-start.8 = (f32[6,64,256]{2,1,0:T(8,128)S(1)}, f32[6,64,256]{2,1,0:T(8,128)S(1)}, u32[]{:S(2)}, u32[]{:S(2)}) collective-permute-start(f32[6,64,256]{2,1,0:T(8,128)S(1)} %get-tuple-element.54), channel_id=1, source_target_pairs={{17,16},{18,17},{19,18},{20,19},{21,20},{22,21},{23,22},{24,23},{2... | collective-permute-start | bytes 1179656 | tf_op jit(solution)/shard_map/ppermute | solution.py:320
  22.9 13.4 %collective-permute-start.5 = (f32[6,64,256]{2,1,0:T(8,128)S(1)}, f32[6,64,256]{2,1,0:T(8,128)S(1)}, u32[]{:S(2)}, u32[]{:S(2)}) collective-permute-start(f32[6,64,256]{2,1,0:T(8,128)S(1)} %get-tuple-element.51), channel_id=1, source_target_pairs={{0,1},{1,2},{2,3},{3,4},{4,5},{5,6},{6,7},{7,8},{8,9},{9,10},{10,1... | collective-permute-start | bytes 1179656 | tf_op jit(solution)/shard_map/ppermute | solution.py:320
  23.6 12.8 %collective-permute-start.6 = (f32[6,64,256]{2,1,0:T(8,128)S(1)}, f32[6,64,256]{2,1,0:T(8,128)S(1)}, u32[]{:S(2)}, u32[]{:S(2)}) collective-permute-start(f32[6,64,256]{2,1,0:T(8,128)S(1)} %get-tuple-element.52), channel_id=1, source_target_pairs={{1,0},{2,1},{3,2},{4,3},{5,4},{6,5},{7,6},{8,7},{9,8},{10,9},{11,1... | collective-permute-start | bytes 1179656 | tf_op jit(solution)/shard_map/ppermute | solution.py:320
  36.4 7.5 %collective-permute-start.9 = (f32[6,2,64,256]{3,2,1,0:T(8,128)S(1)}, f32[6,2,64,256]{3,2,1,0:T(8,128)S(1)}, u32[]{:S(2)}, u32[]{:S(2)}) collective-permute-start(f32[6,2,64,256]{3,2,1,0:T(8,128)S(1)} %shard_map.77.before_end), channel_id=1, source_target_pairs={{0,16},{1,17},{2,18},{3,19},{4,20},{5,21},{6,22},{7,23},{8,24},{9,... | collective-permute-start | bytes 2359304 | tf_op jit(solution)/shard_map/ppermute | solution.py:392
  37.7 13.2 %collective-permute-start.12 = (f32[6,64,256]{2,1,0:T(8,128)S(1)}, f32[6,64,256]{2,1,0:T(8,128)S(1)}, u32[]{:S(2)}, u32[]{:S(2)}) collective-permute-start(f32[6,64,256]{2,1,0:T(8,128)S(1)} %get-tuple-element.67), channel_id=1, source_target_pairs={{16,17},{17,18},{18,19},{19,20},{20,21},{21,22},{22,23},{23,24},{2... | collective-permute-start | bytes 1179656 | tf_op jit(solution)/shard_map/ppermute | solution.py:320
  39.6 15.3 %collective-permute-start.13 = (f32[6,64,256]{2,1,0:T(8,128)S(1)}, f32[6,64,256]{2,1,0:T(8,128)S(1)}, u32[]{:S(2)}, u32[]{:S(2)}) collective-permute-start(f32[6,64,256]{2,1,0:T(8,128)S(1)} %get-tuple-element.68), channel_id=1, source_target_pairs={{17,16},{18,17},{19,18},{20,19},{21,20},{22,21},{23,22},{24,23},{2... | collective-permute-start | bytes 1179656 | tf_op jit(solution)/shard_map/ppermute | solution.py:320
  44.7 11.9 %collective-permute-start.10 = (f32[6,64,256]{2,1,0:T(8,128)S(1)}, f32[6,64,256]{2,1,0:T(8,128)S(1)}, u32[]{:S(2)}, u32[]{:S(2)}) collective-permute-start(f32[6,64,256]{2,1,0:T(8,128)S(1)} %get-tuple-element.63), channel_id=1, source_target_pairs={{16,17},{17,18},{18,19},{19,20},{20,21},{21,22},{22,23},{23,24},{2... | collective-permute-start | bytes 1179656 | tf_op jit(solution)/shard_map/ppermute | solution.py:320
  46.6 12.5 %collective-permute-start.11 = (f32[6,64,256]{2,1,0:T(8,128)S(1)}, f32[6,64,256]{2,1,0:T(8,128)S(1)}, u32[]{:S(2)}, u32[]{:S(2)}) collective-permute-start(f32[6,64,256]{2,1,0:T(8,128)S(1)} %get-tuple-element.64), channel_id=1, source_target_pairs={{17,16},{18,17},{19,18},{20,19},{21,20},{22,21},{23,22},{24,23},{2... | collective-permute-start | bytes 1179656 | tf_op jit(solution)/shard_map/ppermute | solution.py:320

commit v8 on v7

--- a/solution.py
+++ b/solution.py
@@ -365,7 +365,9 @@
         edge_kernel, [(4, *plane), message, message],
         *exchanged(zone_up, zone_down, 1), zone_rows, up, down,
     )
-    edges = lax.ppermute(edges, "win", [(1, 0)]), edges
+    edges = lax.ppermute(
+        edges, "win", [(0, 1), (1, 0)] + [(n, n) for n in range(2, windows)]
+    ), edges
     later_low, later_high = exchanged(later_up, later_down, 1)
     ends, parts, rim_of = [start, start], [part, part], [rim, rim]
     for turn in range(FINE // 2):

time: 62.7 us -> 60.2 us (0.960); the launches traced: 61.7 us -> 59.8 us
  waiting for transfers between devices: 21.6 us -> 19.8 us
    ppermute x12, waiting for transfers between devices: 21.6 us -> 17.9 us  [passed(): return lax.ppermute(block, ('win', 'slab'), route)]
    ppermute x1, waiting for transfers between devices: 0.01 us -> 1.97 us  [shards(): lax.ppermute(new_end, 'win', [(n, n + 1) for n in range(windows - 1)])]
    ppermute x1, starting transfers between devices: 1.31 us -> 0.07 us  [shards(): lax.ppermute(edges, 'win', [(0, 1), (1, 0)] + [(n, n) for n in range(2, w...]
    ppermute x12, starting transfers between devices: 27.5 us -> 28.4 us  [passed(): return lax.ppermute(block, ('win', 'slab'), route)]
  transfers between devices with their start and end apart: 14 -> 14, of which waited for: 6 -> 7; matrix products, arithmetic and copies ran while one was open for 0% -> 0% of each run, Pallas kernels for 8% -> 9%
where the time goes in v8:
time: 60.2 us; the launch traced here: 59.8 us
  starting transfers between devices  29.8 us (50%)
  waiting for transfers between devices  19.8 us (33%)
  Pallas kernels  9.82 us (16%)
    ppermute x12, starting transfers between devices, passed(): return lax.ppermute(block, ('win', 'slab'), route)  28.4 us
    ppermute x12, waiting for transfers between devices, passed(): return lax.ppermute(block, ('win', 'slab'), route)  17.9 us
    pallas_call x8, Pallas kernels, called(): pl.pallas_call(kernel, out_shape=[jax.ShapeDtypeStruct(shape, jnp.float32...  9.82 us
    ppermute x1, waiting for transfers between devices, shards(): lax.ppermute(new_end, 'win', [(n, n + 1) for n in range(windows - 1)])  1.97 us
    ppermute x1, starting transfers between devices, shards(): lax.ppermute(new_end, 'win', [(n, n + 1) for n in range(windows - 1)])  1.29 us
  transfers between devices with their start and end apart: 14, of which 7 were waited for; matrix products, arithmetic and copies ran while one was open for 0% of the time, Pallas kernels for 9%

profile of v8, /device:TPU:13, one launch (start us, length us, event | category | flops | bytes accessed | tf_op | source)
XLA Modules:
  0.0 59.8 jit_solution(9963816815187713180)
XLA Ops:
  0.0 0.0 copy-start
  0.0 2.2 %shard_map.73 = (f32[2,2,64,256]{3,2,1,0:T(8,128)S(1)}, f32[3,2,64,256]{3,2,1,0:T(8,128)S(1)}, f32[3,2,64,256]{3,2,1,0:T(8,128)S(1)}, f32[6,64,256]{2,1,0:T(8,12...) custom-call(f32[1,6,2,64,256]{4,3,2,1,0:T(8,128)} %state_hbm.1, ...), custom_call_target="tpu_custom_call" | custom-call | tf_op jit(solution)/shard_map/pallas_call | solution.py:300
  2.3 0.7 %collective-permute-start.3 = (f32[6,64,256]{2,1,0:T(8,128)S(1)}, f32[6,64,256]{2,1,0:T(8,128)S(1)}, u32[]{:S(2)}, u32[]{:S(2)}) collective-permute-start(f32[6,64,256]{2,1,0:T(8,128)S(1)} %get-tuple-element.41.up), channel_id=1, source_target_pairs={{0,1},{1,2},{2,3},{3,4},{4,5},{5,6},{6,7},{7,8},{8,9},{9,10},{10,1... | collective-permute-start | bytes 1179656 | tf_op jit(solution)/shard_map/ppermute | solution.py:320
  2.9 0.7 %collective-permute-start.4 = (f32[6,64,256]{2,1,0:T(8,128)S(1)}, f32[6,64,256]{2,1,0:T(8,128)S(1)}, u32[]{:S(2)}, u32[]{:S(2)}) collective-permute-start(f32[6,64,256]{2,1,0:T(8,128)S(1)} %get-tuple-element.42.down), channel_id=1, source_target_pairs={{1,0},{2,1},{3,2},{4,3},{5,4},{6,5},{7,6},{8,7},{9,8},{10,9},{11,1... | collective-permute-start | bytes 1179656 | tf_op jit(solution)/shard_map/ppermute | solution.py:320
  3.6 3.1 %collective-permute-start = (f32[64,256]{1,0:T(8,128)S(1)}, f32[64,256]{1,0:T(8,128)S(1)}, u32[]{:S(2)}, u32[]{:S(2)}) collective-permute-start(f32[64,256]{1,0:T(8,128)S(1)} %get-tuple-element.38), channel_id=1, source_target_pairs={{16,17},{17,18},{18,19},{19,20},{20,21},{21,22},{22,23},{23,24},{2... | collective-permute-start | bytes 196616 | tf_op jit(solution)/shard_map/ppermute | solution.py:320
  6.8 3.1 %collective-permute-start.1 = (f32[64,256]{1,0:T(8,128)S(1)}, f32[64,256]{1,0:T(8,128)S(1)}, u32[]{:S(2)}, u32[]{:S(2)}) collective-permute-start(f32[64,256]{1,0:T(8,128)S(1)} %get-tuple-element.39), channel_id=1, source_target_pairs={{17,16},{18,17},{19,18},{20,19},{21,20},{22,21},{23,22},{24,23},{2... | collective-permute-start | bytes 196616 | tf_op jit(solution)/shard_map/ppermute | solution.py:320
  9.8 0.7 %collective-permute-done.zone_low = f32[64,256]{1,0:T(8,128)S(1)} collective-permute-done((f32[64,256]{1,0:T(8,128)S(1)}, f32[64,256]{1,0:T(8,128)S(1)}, u32[]{:S(2)}, u32[]{:S(2)}) %collective-permute-start) | collective-permute-done | bytes 65568 | tf_op jit(solution)/shard_map/ppermute | solution.py:320
  10.5 4.6 %collective-permute-done.1.zone_high = f32[64,256]{1,0:T(8,128)S(1)} collective-permute-done((f32[64,256]{1,0:T(8,128)S(1)}, f32[64,256]{1,0:T(8,128)S(1)}, u32[]{:S(2)}, u32[]{:S(2)}) %collective-permute-start.1) | collective-permute-done | bytes 65568 | tf_op jit(solution)/shard_map/ppermute | solution.py:320
  15.2 0.1 shard_map.74
  15.3 0.1 collective-permute-start.2
  15.4 2.5 %collective-permute-start.7 = (f32[6,64,256]{2,1,0:T(8,128)S(1)}, f32[6,64,256]{2,1,0:T(8,128)S(1)}, u32[]{:S(2)}, u32[]{:S(2)}) collective-permute-start(f32[6,64,256]{2,1,0:T(8,128)S(1)} %get-tuple-element.53), channel_id=1, source_target_pairs={{16,17},{17,18},{18,19},{19,20},{20,21},{21,22},{22,23},{23,24},{2... | collective-permute-start | bytes 1179656 | tf_op jit(solution)/shard_map/ppermute | solution.py:320
  17.9 3.7 %collective-permute-start.8 = (f32[6,64,256]{2,1,0:T(8,128)S(1)}, f32[6,64,256]{2,1,0:T(8,128)S(1)}, u32[]{:S(2)}, u32[]{:S(2)}) collective-permute-start(f32[6,64,256]{2,1,0:T(8,128)S(1)} %get-tuple-element.54), channel_id=1, source_target_pairs={{17,16},{18,17},{19,18},{20,19},{21,20},{22,21},{23,22},{24,23},{2... | collective-permute-start | bytes 1179656 | tf_op jit(solution)/shard_map/ppermute | solution.py:320
  21.6 0.0 collective-permute-done.2.refs_0_
  21.6 0.0 collective-permute-done.3.refs_6_
  21.6 0.0 collective-permute-done.4.refs_7_
  21.6 0.0 copy-done
  21.6 0.7 %collective-permute-start.5 = (f32[6,64,256]{2,1,0:T(8,128)S(1)}, f32[6,64,256]{2,1,0:T(8,128)S(1)}, u32[]{:S(2)}, u32[]{:S(2)}) collective-permute-start(f32[6,64,256]{2,1,0:T(8,128)S(1)} %get-tuple-element.51), channel_id=1, source_target_pairs={{0,1},{1,2},{2,3},{3,4},{4,5},{5,6},{6,7},{7,8},{8,9},{9,10},{10,1... | collective-permute-start | bytes 1179656 | tf_op jit(solution)/shard_map/ppermute | solution.py:320
  22.3 0.7 %collective-permute-start.6 = (f32[6,64,256]{2,1,0:T(8,128)S(1)}, f32[6,64,256]{2,1,0:T(8,128)S(1)}, u32[]{:S(2)}, u32[]{:S(2)}) collective-permute-start(f32[6,64,256]{2,1,0:T(8,128)S(1)} %get-tuple-element.52), channel_id=1, source_target_pairs={{1,0},{2,1},{3,2},{4,3},{5,4},{6,5},{7,6},{8,7},{9,8},{10,9},{11,1... | collective-permute-start | bytes 1179656 | tf_op jit(solution)/shard_map/ppermute | solution.py:320
  23.0 1.8 %collective-permute-done.7.refs_6_ = f32[6,64,256]{2,1,0:T(8,128)S(1)} collective-permute-done((f32[6,64,256]{2,1,0:T(8,128)S(1)}, f32[6,64,256]{2,1,0:T(8,128)S(1)}, u32[]{:S(2)}, u32[]{:S(2)}) %collective-permute-start.7) | collective-permute-done | bytes 393248 | tf_op jit(solution)/shard_map/ppermute | solution.py:320
  24.8 3.8 %collective-permute-done.8.refs_7_ = f32[6,64,256]{2,1,0:T(8,128)S(1)} collective-permute-done((f32[6,64,256]{2,1,0:T(8,128)S(1)}, f32[6,64,256]{2,1,0:T(8,128)S(1)}, u32[]{:S(2)}, u32[]{:S(2)}) %collective-permute-start.8) | collective-permute-done | bytes 393248 | tf_op jit(solution)/shard_map/ppermute | solution.py:320
  28.6 2.4 %shard_map.76 = (f32[6,2,64,256]{3,2,1,0:T(8,128)S(1)}, f32[3,2,64,256]{3,2,1,0:T(8,128)S(1)}, f32[6,64,256]{2,1,0:T(8,128)S(1)}, f32[6,64,256]{2,1,0:T(8,128)S(1)}, f32[2,6,64,256]{3,2,1,0:T(8,128)S(1)}) custom-call(f32[4,64,256]{2,1,0:T(8,128)S(1)} %get-tuple-element.43.refs_0_.edges, f32[6,2,64,256]{3,2,1,0:T(8,128)S(1)} %bitcast.3, ...), custom_call_target="tpu_custom_call" | custom-call | tf_op jit(solution)/shard_map/pallas_call | solution.py:300
  31.0 0.0 collective-permute-done.5.refs_6_
  31.0 0.0 collective-permute-done.6.refs_7_
  31.0 1.3 %collective-permute-start.9 = (f32[6,2,64,256]{3,2,1,0:T(8,128)S(1)}, f32[6,2,64,256]{3,2,1,0:T(8,128)S(1)}, u32[]{:S(2)}, u32[]{:S(2)}) collective-permute-start(f32[6,2,64,256]{3,2,1,0:T(8,128)S(1)} %shard_map.77.before_end), channel_id=1, source_target_pairs={{0,16},{1,17},{2,18},{3,19},{4,20},{5,21},{6,22},{7,23},{8,24},{9,... | collective-permute-start | bytes 2359304 | tf_op jit(solution)/shard_map/ppermute | solution.py:394
  32.3 1.9 %collective-permute-start.12 = (f32[6,64,256]{2,1,0:T(8,128)S(1)}, f32[6,64,256]{2,1,0:T(8,128)S(1)}, u32[]{:S(2)}, u32[]{:S(2)}) collective-permute-start(f32[6,64,256]{2,1,0:T(8,128)S(1)} %get-tuple-element.67), channel_id=1, source_target_pairs={{16,17},{17,18},{18,19},{19,20},{20,21},{21,22},{22,23},{23,24},{2... | collective-permute-start | bytes 1179656 | tf_op jit(solution)/shard_map/ppermute | solution.py:320
  34.3 4.7 %collective-permute-start.13 = (f32[6,64,256]{2,1,0:T(8,128)S(1)}, f32[6,64,256]{2,1,0:T(8,128)S(1)}, u32[]{:S(2)}, u32[]{:S(2)}) collective-permute-start(f32[6,64,256]{2,1,0:T(8,128)S(1)} %get-tuple-element.68), channel_id=1, source_target_pairs={{17,16},{18,17},{19,18},{20,19},{21,20},{22,21},{23,22},{24,23},{2... | collective-permute-start | bytes 1179656 | tf_op jit(solution)/shard_map/ppermute | solution.py:320
  39.0 2.0 %collective-permute-done.9.before = f32[6,2,64,256]{3,2,1,0:T(8,128)S(1)} collective-permute-done((f32[6,2,64,256]{3,2,1,0:T(8,128)S(1)}, f32[6,2,64,256]{3,2,1,0:T(8,128)S(1)}, u32[]{:S(2)}, u32[]{:S(2)}) %collective-permute-start.9) | collective-permute-done | bytes 786464 | tf_op jit(solution)/shard_map/ppermute | solution.py:394
  41.0 0.8 %shard_map.78 = (f32[6,2,64,256]{3,2,1,0:T(8,128)S(1)}, f32[3,2,64,256]{3,2,1,0:T(8,128)S(1)}, f32[6,64,256]{2,1,0:T(8,128)S(1)}, f32[6,64,256]{2,1,0:T(8,128)S(1)}, f32[2,6,64,256]{3,2,1,0:T(8,128)S(1)}) custom-call(f32[6,2,64,256]{3,2,1,0:T(8,128)S(1)} %collective-permute-done.9.before, f32[6,2,64,256]{3,2,1,0:T(8,128)S(1)} %bitcast.4, ...), custom_call_target="tpu_custom_call" | custom-call | tf_op jit(solution)/shard_map/pallas_call | solution.py:300
  41.8 3.3 %collective-permute-start.10 = (f32[6,64,256]{2,1,0:T(8,128)S(1)}, f32[6,64,256]{2,1,0:T(8,128)S(1)}, u32[]{:S(2)}, u32[]{:S(2)}) collective-permute-start(f32[6,64,256]{2,1,0:T(8,128)S(1)} %get-tuple-element.63), channel_id=1, source_target_pairs={{16,17},{17,18},{18,19},{19,20},{20,21},{21,22},{22,23},{23,24},{2... | collective-permute-start | bytes 1179656 | tf_op jit(solution)/shard_map/ppermute | solution.py:320
  45.1 3.4 %collective-permute-start.11 = (f32[6,64,256]{2,1,0:T(8,128)S(1)}, f32[6,64,256]{2,1,0:T(8,128)S(1)}, u32[]{:S(2)}, u32[]{:S(2)}) collective-permute-start(f32[6,64,256]{2,1,0:T(8,128)S(1)} %get-tuple-element.64), channel_id=1, source_target_pairs={{17,16},{18,17},{19,18},{20,19},{21,20},{22,21},{23,22},{24,23},{2... | collective-permute-start | bytes 1179656 | tf_op jit(solution)/shard_map/ppermute | solution.py:320
  48.5 0.0 collective-permute-done.12.refs_6_
  48.5 0.0 collective-permute-done.13.refs_7_
  48.5 1.8 %shard_map.79.fine_end = f32[6,2,64,256]{3,2,1,0:T(8,128)S(1)} custom-call(f32[4,64,256]{2,1,0:T(8,128)S(1)} %get-tuple-element.43.refs_0_.edges, f32[6,2,64,256]{3,2,1,0:T(8,128)S(1)} %get-tuple-element.65.refs_1_, f32[2,2,64,256]{3,2,1,0:T(8,128)S(1)} %get-tuple-element.44.refs_2_.moduli, f32[3,2,64,256]{3,2,1,0:T(8,128)S(1)} %get-tuple-element.45.refs_3_, ...), custom_call_target="tpu_custom_call" | custom-call | tf_op jit(solution)/shard_map/pallas_call | solution.py:300
  50.4 1.4 %collective-permute-done.10.low = f32[6,64,256]{2,1,0:T(8,128)S(1)} collective-permute-done((f32[6,64,256]{2,1,0:T(8,128)S(1)}, f32[6,64,256]{2,1,0:T(8,128)S(1)}, u32[]{:S(2)}, u32[]{:S(2)}) %collective-permute-start.10) | collective-permute-done | bytes 393248 | tf_op jit(solution)/shard_map/ppermute | solution.py:320
  51.7 5.6 %collective-permute-done.11.high = f32[6,64,256]{2,1,0:T(8,128)S(1)} collective-permute-done((f32[6,64,256]{2,1,0:T(8,128)S(1)}, f32[6,64,256]{2,1,0:T(8,128)S(1)}, u32[]{:S(2)}, u32[]{:S(2)}) %collective-permute-start.11) | collective-permute-done | bytes 393248 | tf_op jit(solution)/shard_map/ppermute | solution.py:320
  57.3 2.4 %shard_map.80 = f32[6,2,64,256]{3,2,1,0:T(8,128)} custom-call(f32[4,64,256]{2,1,0:T(8,128)S(1)} %get-tuple-element.43.refs_0_.edges, f32[6,2,64,256]{3,2,1,0:T(8,128)S(1)} %get-tuple-element.60.state, f32[2,2,64,256]{3,2,1,0:T(8,128)S(1)} %get-tuple-element.44.refs_2_.moduli, f32[3,2,64,256]{3,2,1,0:T(8,128)S(1)} %get-tuple-element.61.part, ...), custom_call_target="tpu_custom_call" | custom-call | tf_op jit(solution)/shard_map/pallas_call | solution.py:300
  (2 shorter events, 0.0 us)
Async XLA Ops:
  0.0 21.6 %copy-start = (f32[1,6,2,64,256]{4,3,2,1,0:T(8,128)S(1)}, f32[1,6,2,64,256]{4,3,2,1,0:T(8,128)}, u32[]{:S(2)}) copy-start(f32[1,6,2,64,256]{4,3,2,1,0:T(8,128)} %state_hbm.1) | copy-start | bytes 2359300
  2.3 19.3 %collective-permute-start.3 = (f32[6,64,256]{2,1,0:T(8,128)S(1)}, f32[6,64,256]{2,1,0:T(8,128)S(1)}, u32[]{:S(2)}, u32[]{:S(2)}) collective-permute-start(f32[6,64,256]{2,1,0:T(8,128)S(1)} %get-tuple-element.41.up), channel_id=1, source_target_pairs={{0,1},{1,2},{2,3},{3,4},{4,5},{5,6},{6,7},{7,8},{8,9},{9,10},{10,1... | collective-permute-start | bytes 1179656 | tf_op jit(solution)/shard_map/ppermute | solution.py:320
  2.9 18.7 %collective-permute-start.4 = (f32[6,64,256]{2,1,0:T(8,128)S(1)}, f32[6,64,256]{2,1,0:T(8,128)S(1)}, u32[]{:S(2)}, u32[]{:S(2)}) collective-permute-start(f32[6,64,256]{2,1,0:T(8,128)S(1)} %get-tuple-element.42.down), channel_id=1, source_target_pairs={{1,0},{2,1},{3,2},{4,3},{5,4},{6,5},{7,6},{8,7},{9,8},{10,9},{11,1... | collective-permute-start | bytes 1179656 | tf_op jit(solution)/shard_map/ppermute | solution.py:320
  3.6 6.9 %collective-permute-start = (f32[64,256]{1,0:T(8,128)S(1)}, f32[64,256]{1,0:T(8,128)S(1)}, u32[]{:S(2)}, u32[]{:S(2)}) collective-permute-start(f32[64,256]{1,0:T(8,128)S(1)} %get-tuple-element.38), channel_id=1, source_target_pairs={{16,17},{17,18},{18,19},{19,20},{20,21},{21,22},{22,23},{23,24},{2... | collective-permute-start | bytes 196616 | tf_op jit(solution)/shard_map/ppermute | solution.py:320
  6.8 8.4 %collective-permute-start.1 = (f32[64,256]{1,0:T(8,128)S(1)}, f32[64,256]{1,0:T(8,128)S(1)}, u32[]{:S(2)}, u32[]{:S(2)}) collective-permute-start(f32[64,256]{1,0:T(8,128)S(1)} %get-tuple-element.39), channel_id=1, source_target_pairs={{17,16},{18,17},{19,18},{20,19},{21,20},{22,21},{23,22},{24,23},{2... | collective-permute-start | bytes 196616 | tf_op jit(solution)/shard_map/ppermute | solution.py:320
  15.3 6.3 %collective-permute-start.2 = (f32[4,64,256]{2,1,0:T(8,128)S(1)}, f32[4,64,256]{2,1,0:T(8,128)S(1)}, u32[]{:S(2)}, u32[]{:S(2)}) collective-permute-start(f32[4,64,256]{2,1,0:T(8,128)S(1)} %get-tuple-element.43.refs_0_.edges), channel_id=1, source_target_pairs={{0,16},{16,0},{1,17},{17,1},{2,18},{18,2},{3,19},{19,3},{4,20},{20... | collective-permute-start | bytes 786440 | tf_op jit(solution)/shard_map/ppermute | solution.py:368
  15.4 9.4 %collective-permute-start.7 = (f32[6,64,256]{2,1,0:T(8,128)S(1)}, f32[6,64,256]{2,1,0:T(8,128)S(1)}, u32[]{:S(2)}, u32[]{:S(2)}) collective-permute-start(f32[6,64,256]{2,1,0:T(8,128)S(1)} %get-tuple-element.53), channel_id=1, source_target_pairs={{16,17},{17,18},{18,19},{19,20},{20,21},{21,22},{22,23},{23,24},{2... | collective-permute-start | bytes 1179656 | tf_op jit(solution)/shard_map/ppermute | solution.py:320
  17.9 10.7 %collective-permute-start.8 = (f32[6,64,256]{2,1,0:T(8,128)S(1)}, f32[6,64,256]{2,1,0:T(8,128)S(1)}, u32[]{:S(2)}, u32[]{:S(2)}) collective-permute-start(f32[6,64,256]{2,1,0:T(8,128)S(1)} %get-tuple-element.54), channel_id=1, source_target_pairs={{17,16},{18,17},{19,18},{20,19},{21,20},{22,21},{23,22},{24,23},{2... | collective-permute-start | bytes 1179656 | tf_op jit(solution)/shard_map/ppermute | solution.py:320
  21.6 9.4 %collective-permute-start.5 = (f32[6,64,256]{2,1,0:T(8,128)S(1)}, f32[6,64,256]{2,1,0:T(8,128)S(1)}, u32[]{:S(2)}, u32[]{:S(2)}) collective-permute-start(f32[6,64,256]{2,1,0:T(8,128)S(1)} %get-tuple-element.51), channel_id=1, source_target_pairs={{0,1},{1,2},{2,3},{3,4},{4,5},{5,6},{6,7},{7,8},{8,9},{9,10},{10,1... | collective-permute-start | bytes 1179656 | tf_op jit(solution)/shard_map/ppermute | solution.py:320
  22.3 8.7 %collective-permute-start.6 = (f32[6,64,256]{2,1,0:T(8,128)S(1)}, f32[6,64,256]{2,1,0:T(8,128)S(1)}, u32[]{:S(2)}, u32[]{:S(2)}) collective-permute-start(f32[6,64,256]{2,1,0:T(8,128)S(1)} %get-tuple-element.52), channel_id=1, source_target_pairs={{1,0},{2,1},{3,2},{4,3},{5,4},{6,5},{7,6},{8,7},{9,8},{10,9},{11,1... | collective-permute-start | bytes 1179656 | tf_op jit(solution)/shard_map/ppermute | solution.py:320
  31.0 9.9 %collective-permute-start.9 = (f32[6,2,64,256]{3,2,1,0:T(8,128)S(1)}, f32[6,2,64,256]{3,2,1,0:T(8,128)S(1)}, u32[]{:S(2)}, u32[]{:S(2)}) collective-permute-start(f32[6,2,64,256]{3,2,1,0:T(8,128)S(1)} %shard_map.77.before_end), channel_id=1, source_target_pairs={{0,16},{1,17},{2,18},{3,19},{4,20},{5,21},{6,22},{7,23},{8,24},{9,... | collective-permute-start | bytes 2359304 | tf_op jit(solution)/shard_map/ppermute | solution.py:394
  32.3 16.2 %collective-permute-start.12 = (f32[6,64,256]{2,1,0:T(8,128)S(1)}, f32[6,64,256]{2,1,0:T(8,128)S(1)}, u32[]{:S(2)}, u32[]{:S(2)}) collective-permute-start(f32[6,64,256]{2,1,0:T(8,128)S(1)} %get-tuple-element.67), channel_id=1, source_target_pairs={{16,17},{17,18},{18,19},{19,20},{20,21},{21,22},{22,23},{23,24},{2... | collective-permute-start | bytes 1179656 | tf_op jit(solution)/shard_map/ppermute | solution.py:320
  34.3 14.2 %collective-permute-start.13 = (f32[6,64,256]{2,1,0:T(8,128)S(1)}, f32[6,64,256]{2,1,0:T(8,128)S(1)}, u32[]{:S(2)}, u32[]{:S(2)}) collective-permute-start(f32[6,64,256]{2,1,0:T(8,128)S(1)} %get-tuple-element.68), channel_id=1, source_target_pairs={{17,16},{18,17},{19,18},{20,19},{21,20},{22,21},{23,22},{24,23},{2... | collective-permute-start | bytes 1179656 | tf_op jit(solution)/shard_map/ppermute | solution.py:320
  41.8 9.9 %collective-permute-start.10 = (f32[6,64,256]{2,1,0:T(8,128)S(1)}, f32[6,64,256]{2,1,0:T(8,128)S(1)}, u32[]{:S(2)}, u32[]{:S(2)}) collective-permute-start(f32[6,64,256]{2,1,0:T(8,128)S(1)} %get-tuple-element.63), channel_id=1, source_target_pairs={{16,17},{17,18},{18,19},{19,20},{20,21},{21,22},{22,23},{23,24},{2... | collective-permute-start | bytes 1179656 | tf_op jit(solution)/shard_map/ppermute | solution.py:320
  45.1 12.2 %collective-permute-start.11 = (f32[6,64,256]{2,1,0:T(8,128)S(1)}, f32[6,64,256]{2,1,0:T(8,128)S(1)}, u32[]{:S(2)}, u32[]{:S(2)}) collective-permute-start(f32[6,64,256]{2,1,0:T(8,128)S(1)} %get-tuple-element.64), channel_id=1, source_target_pairs={{17,16},{18,17},{19,18},{20,19},{21,20},{22,21},{23,22},{24,23},{2... | collective-permute-start | bytes 1179656 | tf_op jit(solution)/shard_map/ppermute | solution.py:320

commit v9 on v8

--- a/solution.py
+++ b/solution.py
@@ -176,34 +176,53 @@
         zone_rows[kinds + k] = jnp.full((1, columns), lame_table[k], jnp.float32)
 
 
-def two_steps(step, u0, part, rim, low, high, moduli, edges, load):
+def side_sums(step, got, here, shear, bulk, edge_shear, edge_bulk, sign):
+    there = Inplane([got[c] for c in range(3)])
+    even, odd = towards(sums_of(there), sign)
+    velocity = [step * (shear * even[c] + bulk * odd[c]) for c in range(3)]
+    even, odd = towards(here, -sign)
+    square = step * step
+    outer = [
+        got[3 + c] + square * (edge_shear * even[c] + edge_bulk * odd[c]) for c in range(3)
+    ]
+    return velocity, towards(sums_of(Inplane(outer)), sign)
+
+
+def slab_side(step, side, u0, rim, got, moduli, edges):
+    z, sign = ((0, -1.0), (moduli.shape[1] - 1, 1.0))[side]
+    here = tuple(rim[side, c] for c in range(6)) + (u0[2, z],)
+    return side_sums(
+        step, got, here, moduli[0, z], moduli[1, z], edges[2 * side], edges[2 * side + 1], sign
+    )
+
+
+def share_kernel(step, side, edges, u0, moduli, rim, got, share):
+    @pl.when(lax.axis_index("win") != 0)
+    def _():
+        velocity, (even, odd) = slab_side(step, side, u0, rim, got, moduli, edges)
+        for c in range(3):
+            share[c], share[3 + c], share[6 + c] = velocity[c], even[c], odd[c]
+
+
+def two_steps(step, u0, part, rim, low, high, moduli, edges, load, shared=None):
     count = moduli.shape[1]
-    square = step * step
-    sides = ((low, 0, 0, -1.0), (high, 1, count - 1, 1.0))
     velocities = [[part[c, z] for c in range(3)] for z in range(count)]
-    outer = []
-    for side, (got, edge, z, sign) in enumerate(sides):
-        there = Inplane([got[c] for c in range(3)])
-        even, odd = towards(sums_of(there), sign)
-        for c in range(3):
-            velocities[z][c] = velocities[z][c] + step * (
-                moduli[0, z] * even[c] + moduli[1, z] * odd[c]
-            )
-        here = tuple(rim[side, c] for c in range(6)) + (u0[2, z],)
-        even, odd = towards(here, -sign)
-        outer.append(
-            [
-                got[3 + c] + square * (edges[2 * side] * even[c] + edges[2 * side + 1] * odd[c])
-                for c in range(3)
-            ]
-        )
+    sides = []
+    for side, got in enumerate((low, high)):
+        if side == shared:
+            velocity, even, odd = ([got[first + c] for c in range(3)] for first in (0, 3, 6))
+            sides.append((velocity, (even, odd)))
+        else:
+            sides.append(slab_side(step, side, u0, rim, got, moduli, edges))
+    edge_planes = (0, count - 1)
+    for z, (velocity, _) in zip(edge_planes, sides):
+        velocities[z] = [a + b for a, b in zip(velocities[z], velocity)]
     planes = [
         Inplane([u0[c, z] + step * velocities[z][c] for c in range(3)]) for z in range(count)
     ]
     sums, _ = own_sums(planes)
-    for side, (got, edge, z, sign) in enumerate(sides):
-        part_of = towards(sums_of(Inplane(outer[side])), sign)
-        sums[z] = tuple([a + b for a, b in zip(x, y)] for x, y in zip(sums[z], part_of))
+    for z, (_, side) in zip(edge_planes, sides):
+        sums[z] = tuple([a + b for a, b in zip(x, y)] for x, y in zip(sums[z], side))
     return [
         moved(
             sums[z], planes[z].u, velocities[z], moduli[0, z], moduli[1, z],
@@ -280,7 +299,7 @@
     @pl.when(lax.axis_index("win") != 0)
     def _():
         ends = two_steps(
-            DT_COARSE, state, part, rim, low, high, moduli, edges, lambda c, z: 0.0
+            DT_COARSE, state, part, rim, low, high, moduli, edges, lambda c, z: 0.0, 0
         )
         for z, (v, u) in enumerate(ends):
             for c in range(3):
@@ -402,9 +421,13 @@
                 FINE // 2 - 1, 1, edges[1], ends[1], *fixed, parts[1], rim_of[1],
                 later_low, later_high,
             )[0]
+        share = called(
+            functools.partial(share_kernel, DT_COARSE, 0), [(9, *plane)],
+            edges[1], difference, moduli, rim, low,
+        )[0]
         new_end = called(
             coarse_kernel, [state],
-            edges[1], difference, moduli, part, rim, low, high, ends[0], fine_end,
+            edges[1], difference, moduli, part, rim, share, high, ends[0], fine_end,
             out_specs=[HBM],
             scratch=[pltpu.VMEM(state, jnp.float32), pltpu.SemaphoreType.DMA((count,))],
         )[0]

time: 60.2 us -> 59.9 us (level)
    pallas_call x8 -> x9, Pallas kernels: 9.82 us -> 9.92 us  [called(): pl.pallas_call(kernel, out_shape=[jax.ShapeDtypeStruct(shape, jnp.float32...]
where the time goes in v9:
time: 59.9 us; the launch traced here: 59.5 us
  starting transfers between devices  29.8 us (50%)
  waiting for transfers between devices  19.4 us (32%)
  Pallas kernels  9.92 us (17%)
    ppermute x12, starting transfers between devices, passed(): return lax.ppermute(block, ('win', 'slab'), route)  28.4 us
    ppermute x12, waiting for transfers between devices, passed(): return lax.ppermute(block, ('win', 'slab'), route)  17.4 us
    pallas_call x9, Pallas kernels, called(): pl.pallas_call(kernel, out_shape=[jax.ShapeDtypeStruct(shape, jnp.float32...  9.92 us
    ppermute x1, waiting for transfers between devices, shards(): lax.ppermute(new_end, 'win', [(n, n + 1) for n in range(windows - 1)])  1.96 us
    ppermute x1, starting transfers between devices, shards(): lax.ppermute(new_end, 'win', [(n, n + 1) for n in range(windows - 1)])  1.29 us
  transfers between devices with their start and end apart: 14, of which 7 were waited for; matrix products, arithmetic and copies ran while one was open for 0% of the time, Pallas kernels for 9%

profile of v9, /device:TPU:13, one launch (start us, length us, event | category | flops | bytes accessed | tf_op | source)
XLA Modules:
  0.0 59.5 jit_solution(2998694895466265052)
XLA Ops:
  0.0 0.0 copy-start
  0.0 2.2 %shard_map.73 = (f32[2,2,64,256]{3,2,1,0:T(8,128)S(1)}, f32[3,2,64,256]{3,2,1,0:T(8,128)S(1)}, f32[3,2,64,256]{3,2,1,0:T(8,128)S(1)}, f32[6,64,256]{2,1,0:T(8,12...) custom-call(f32[1,6,2,64,256]{4,3,2,1,0:T(8,128)} %state_hbm.1, ...), custom_call_target="tpu_custom_call" | custom-call | tf_op jit(solution)/shard_map/pallas_call | solution.py:319
  2.3 0.7 %collective-permute-start.3 = (f32[6,64,256]{2,1,0:T(8,128)S(1)}, f32[6,64,256]{2,1,0:T(8,128)S(1)}, u32[]{:S(2)}, u32[]{:S(2)}) collective-permute-start(f32[6,64,256]{2,1,0:T(8,128)S(1)} %get-tuple-element.41.up), channel_id=1, source_target_pairs={{0,1},{1,2},{2,3},{3,4},{4,5},{5,6},{6,7},{7,8},{8,9},{9,10},{10,1... | collective-permute-start | bytes 1179656 | tf_op jit(solution)/shard_map/ppermute | solution.py:339
  2.9 0.7 %collective-permute-start.4 = (f32[6,64,256]{2,1,0:T(8,128)S(1)}, f32[6,64,256]{2,1,0:T(8,128)S(1)}, u32[]{:S(2)}, u32[]{:S(2)}) collective-permute-start(f32[6,64,256]{2,1,0:T(8,128)S(1)} %get-tuple-element.42.down), channel_id=1, source_target_pairs={{1,0},{2,1},{3,2},{4,3},{5,4},{6,5},{7,6},{8,7},{9,8},{10,9},{11,1... | collective-permute-start | bytes 1179656 | tf_op jit(solution)/shard_map/ppermute | solution.py:339
  3.6 3.1 %collective-permute-start = (f32[64,256]{1,0:T(8,128)S(1)}, f32[64,256]{1,0:T(8,128)S(1)}, u32[]{:S(2)}, u32[]{:S(2)}) collective-permute-start(f32[64,256]{1,0:T(8,128)S(1)} %get-tuple-element.38), channel_id=1, source_target_pairs={{16,17},{17,18},{18,19},{19,20},{20,21},{21,22},{22,23},{23,24},{2... | collective-permute-start | bytes 196616 | tf_op jit(solution)/shard_map/ppermute | solution.py:339
  6.8 3.1 %collective-permute-start.1 = (f32[64,256]{1,0:T(8,128)S(1)}, f32[64,256]{1,0:T(8,128)S(1)}, u32[]{:S(2)}, u32[]{:S(2)}) collective-permute-start(f32[64,256]{1,0:T(8,128)S(1)} %get-tuple-element.39), channel_id=1, source_target_pairs={{17,16},{18,17},{19,18},{20,19},{21,20},{22,21},{23,22},{24,23},{2... | collective-permute-start | bytes 196616 | tf_op jit(solution)/shard_map/ppermute | solution.py:339
  9.8 0.7 %collective-permute-done.zone_low = f32[64,256]{1,0:T(8,128)S(1)} collective-permute-done((f32[64,256]{1,0:T(8,128)S(1)}, f32[64,256]{1,0:T(8,128)S(1)}, u32[]{:S(2)}, u32[]{:S(2)}) %collective-permute-start) | collective-permute-done | bytes 65568 | tf_op jit(solution)/shard_map/ppermute | solution.py:339
  10.5 4.6 %collective-permute-done.1.zone_high = f32[64,256]{1,0:T(8,128)S(1)} collective-permute-done((f32[64,256]{1,0:T(8,128)S(1)}, f32[64,256]{1,0:T(8,128)S(1)}, u32[]{:S(2)}, u32[]{:S(2)}) %collective-permute-start.1) | collective-permute-done | bytes 65568 | tf_op jit(solution)/shard_map/ppermute | solution.py:339
  15.2 0.1 shard_map.74
  15.3 0.1 collective-permute-start.2
  15.4 2.5 %collective-permute-start.7 = (f32[6,64,256]{2,1,0:T(8,128)S(1)}, f32[6,64,256]{2,1,0:T(8,128)S(1)}, u32[]{:S(2)}, u32[]{:S(2)}) collective-permute-start(f32[6,64,256]{2,1,0:T(8,128)S(1)} %get-tuple-element.53), channel_id=1, source_target_pairs={{16,17},{17,18},{18,19},{19,20},{20,21},{21,22},{22,23},{23,24},{2... | collective-permute-start | bytes 1179656 | tf_op jit(solution)/shard_map/ppermute | solution.py:339
  17.9 3.7 %collective-permute-start.8 = (f32[6,64,256]{2,1,0:T(8,128)S(1)}, f32[6,64,256]{2,1,0:T(8,128)S(1)}, u32[]{:S(2)}, u32[]{:S(2)}) collective-permute-start(f32[6,64,256]{2,1,0:T(8,128)S(1)} %get-tuple-element.54), channel_id=1, source_target_pairs={{17,16},{18,17},{19,18},{20,19},{21,20},{22,21},{23,22},{24,23},{2... | collective-permute-start | bytes 1179656 | tf_op jit(solution)/shard_map/ppermute | solution.py:339
  21.6 0.0 collective-permute-done.2.refs_0_
  21.6 0.0 collective-permute-done.3.refs_6_
  21.6 0.0 collective-permute-done.4.refs_7_
  21.6 0.0 copy-done
  21.6 0.7 %collective-permute-start.5 = (f32[6,64,256]{2,1,0:T(8,128)S(1)}, f32[6,64,256]{2,1,0:T(8,128)S(1)}, u32[]{:S(2)}, u32[]{:S(2)}) collective-permute-start(f32[6,64,256]{2,1,0:T(8,128)S(1)} %get-tuple-element.51), channel_id=1, source_target_pairs={{0,1},{1,2},{2,3},{3,4},{4,5},{5,6},{6,7},{7,8},{8,9},{9,10},{10,1... | collective-permute-start | bytes 1179656 | tf_op jit(solution)/shard_map/ppermute | solution.py:339
  22.3 0.7 %collective-permute-start.6 = (f32[6,64,256]{2,1,0:T(8,128)S(1)}, f32[6,64,256]{2,1,0:T(8,128)S(1)}, u32[]{:S(2)}, u32[]{:S(2)}) collective-permute-start(f32[6,64,256]{2,1,0:T(8,128)S(1)} %get-tuple-element.52), channel_id=1, source_target_pairs={{1,0},{2,1},{3,2},{4,3},{5,4},{6,5},{7,6},{8,7},{9,8},{10,9},{11,1... | collective-permute-start | bytes 1179656 | tf_op jit(solution)/shard_map/ppermute | solution.py:339
  23.0 1.8 %collective-permute-done.7.refs_6_ = f32[6,64,256]{2,1,0:T(8,128)S(1)} collective-permute-done((f32[6,64,256]{2,1,0:T(8,128)S(1)}, f32[6,64,256]{2,1,0:T(8,128)S(1)}, u32[]{:S(2)}, u32[]{:S(2)}) %collective-permute-start.7) | collective-permute-done | bytes 393248 | tf_op jit(solution)/shard_map/ppermute | solution.py:339
  24.8 3.8 %collective-permute-done.8.refs_7_ = f32[6,64,256]{2,1,0:T(8,128)S(1)} collective-permute-done((f32[6,64,256]{2,1,0:T(8,128)S(1)}, f32[6,64,256]{2,1,0:T(8,128)S(1)}, u32[]{:S(2)}, u32[]{:S(2)}) %collective-permute-start.8) | collective-permute-done | bytes 393248 | tf_op jit(solution)/shard_map/ppermute | solution.py:339
  28.6 2.4 %shard_map.76 = (f32[6,2,64,256]{3,2,1,0:T(8,128)S(1)}, f32[3,2,64,256]{3,2,1,0:T(8,128)S(1)}, f32[6,64,256]{2,1,0:T(8,128)S(1)}, f32[6,64,256]{2,1,0:T(8,128)S(1)}, f32[2,6,64,256]{3,2,1,0:T(8,128)S(1)}) custom-call(f32[4,64,256]{2,1,0:T(8,128)S(1)} %get-tuple-element.43.refs_0_.edges, f32[6,2,64,256]{3,2,1,0:T(8,128)S(1)} %bitcast.3, ...), custom_call_target="tpu_custom_call" | custom-call | tf_op jit(solution)/shard_map/pallas_call | solution.py:319
  31.0 0.0 collective-permute-done.5.refs_6_
  31.0 0.0 collective-permute-done.6.refs_7_
  31.0 1.3 %collective-permute-start.9 = (f32[6,2,64,256]{3,2,1,0:T(8,128)S(1)}, f32[6,2,64,256]{3,2,1,0:T(8,128)S(1)}, u32[]{:S(2)}, u32[]{:S(2)}) collective-permute-start(f32[6,2,64,256]{3,2,1,0:T(8,128)S(1)} %shard_map.77.before_end), channel_id=1, source_target_pairs={{0,16},{1,17},{2,18},{3,19},{4,20},{5,21},{6,22},{7,23},{8,24},{9,... | collective-permute-start | bytes 2359304 | tf_op jit(solution)/shard_map/ppermute | solution.py:413
  32.3 1.9 %collective-permute-start.12 = (f32[6,64,256]{2,1,0:T(8,128)S(1)}, f32[6,64,256]{2,1,0:T(8,128)S(1)}, u32[]{:S(2)}, u32[]{:S(2)}) collective-permute-start(f32[6,64,256]{2,1,0:T(8,128)S(1)} %get-tuple-element.67), channel_id=1, source_target_pairs={{16,17},{17,18},{18,19},{19,20},{20,21},{21,22},{22,23},{23,24},{2... | collective-permute-start | bytes 1179656 | tf_op jit(solution)/shard_map/ppermute | solution.py:339
  34.3 4.7 %collective-permute-start.13 = (f32[6,64,256]{2,1,0:T(8,128)S(1)}, f32[6,64,256]{2,1,0:T(8,128)S(1)}, u32[]{:S(2)}, u32[]{:S(2)}) collective-permute-start(f32[6,64,256]{2,1,0:T(8,128)S(1)} %get-tuple-element.68), channel_id=1, source_target_pairs={{17,16},{18,17},{19,18},{20,19},{21,20},{22,21},{23,22},{24,23},{2... | collective-permute-start | bytes 1179656 | tf_op jit(solution)/shard_map/ppermute | solution.py:339
  39.0 2.0 %collective-permute-done.9.before = f32[6,2,64,256]{3,2,1,0:T(8,128)S(1)} collective-permute-done((f32[6,2,64,256]{3,2,1,0:T(8,128)S(1)}, f32[6,2,64,256]{3,2,1,0:T(8,128)S(1)}, u32[]{:S(2)}, u32[]{:S(2)}) %collective-permute-start.9) | collective-permute-done | bytes 786464 | tf_op jit(solution)/shard_map/ppermute | solution.py:413
  40.9 0.8 %shard_map.78 = (f32[6,2,64,256]{3,2,1,0:T(8,128)S(1)}, f32[3,2,64,256]{3,2,1,0:T(8,128)S(1)}, f32[6,64,256]{2,1,0:T(8,128)S(1)}, f32[6,64,256]{2,1,0:T(8,128)S(1)}, f32[2,6,64,256]{3,2,1,0:T(8,128)S(1)}) custom-call(f32[6,2,64,256]{3,2,1,0:T(8,128)S(1)} %collective-permute-done.9.before, f32[6,2,64,256]{3,2,1,0:T(8,128)S(1)} %bitcast.4, ...), custom_call_target="tpu_custom_call" | custom-call | tf_op jit(solution)/shard_map/pallas_call | solution.py:319
  41.8 3.3 %collective-permute-start.10 = (f32[6,64,256]{2,1,0:T(8,128)S(1)}, f32[6,64,256]{2,1,0:T(8,128)S(1)}, u32[]{:S(2)}, u32[]{:S(2)}) collective-permute-start(f32[6,64,256]{2,1,0:T(8,128)S(1)} %get-tuple-element.63), channel_id=1, source_target_pairs={{16,17},{17,18},{18,19},{19,20},{20,21},{21,22},{22,23},{23,24},{2... | collective-permute-start | bytes 1179656 | tf_op jit(solution)/shard_map/ppermute | solution.py:339
  45.0 3.4 %collective-permute-start.11 = (f32[6,64,256]{2,1,0:T(8,128)S(1)}, f32[6,64,256]{2,1,0:T(8,128)S(1)}, u32[]{:S(2)}, u32[]{:S(2)}) collective-permute-start(f32[6,64,256]{2,1,0:T(8,128)S(1)} %get-tuple-element.64), channel_id=1, source_target_pairs={{17,16},{18,17},{19,18},{20,19},{21,20},{22,21},{23,22},{24,23},{2... | collective-permute-start | bytes 1179656 | tf_op jit(solution)/shard_map/ppermute | solution.py:339
  48.5 0.0 collective-permute-done.12.refs_6_
  48.5 0.0 collective-permute-done.13.refs_7_
  48.5 1.8 %shard_map.80.fine_end = f32[6,2,64,256]{3,2,1,0:T(8,128)S(1)} custom-call(f32[4,64,256]{2,1,0:T(8,128)S(1)} %get-tuple-element.43.refs_0_.edges, f32[6,2,64,256]{3,2,1,0:T(8,128)S(1)} %get-tuple-element.65.refs_1_, f32[2,2,64,256]{3,2,1,0:T(8,128)S(1)} %get-tuple-element.44.refs_2_.moduli, f32[3,2,64,256]{3,2,1,0:T(8,128)S(1)} %get-tuple-element.45.refs_3_, ...), custom_call_target="tpu_custom_call" | custom-call | tf_op jit(solution)/shard_map/pallas_call | solution.py:319
  50.3 1.4 %collective-permute-done.10.got = f32[6,64,256]{2,1,0:T(8,128)S(1)} collective-permute-done((f32[6,64,256]{2,1,0:T(8,128)S(1)}, f32[6,64,256]{2,1,0:T(8,128)S(1)}, u32[]{:S(2)}, u32[]{:S(2)}) %collective-permute-start.10) | collective-permute-done | bytes 393248 | tf_op jit(solution)/shard_map/ppermute | solution.py:339
  51.7 0.4 shard_map.79.low
  52.1 5.1 %collective-permute-done.11.high = f32[6,64,256]{2,1,0:T(8,128)S(1)} collective-permute-done((f32[6,64,256]{2,1,0:T(8,128)S(1)}, f32[6,64,256]{2,1,0:T(8,128)S(1)}, u32[]{:S(2)}, u32[]{:S(2)}) %collective-permute-start.11) | collective-permute-done | bytes 393248 | tf_op jit(solution)/shard_map/ppermute | solution.py:339
  57.2 2.1 %shard_map.81 = f32[6,2,64,256]{3,2,1,0:T(8,128)} custom-call(f32[4,64,256]{2,1,0:T(8,128)S(1)} %get-tuple-element.43.refs_0_.edges, f32[6,2,64,256]{3,2,1,0:T(8,128)S(1)} %get-tuple-element.60.u0.state, f32[2,2,64,256]{3,2,1,0:T(8,128)S(1)} %get-tuple-element.44.refs_2_.moduli, f32[3,2,64,256]{3,2,1,0:T(8,128)S(1)} %get-tuple-element.61.part, ...), custom_call_target="tpu_custom_call" | custom-call | tf_op jit(solution)/shard_map/pallas_call | solution.py:319
  (2 shorter events, 0.0 us)
Async XLA Ops:
  0.0 21.6 %copy-start = (f32[1,6,2,64,256]{4,3,2,1,0:T(8,128)S(1)}, f32[1,6,2,64,256]{4,3,2,1,0:T(8,128)}, u32[]{:S(2)}) copy-start(f32[1,6,2,64,256]{4,3,2,1,0:T(8,128)} %state_hbm.1) | copy-start | bytes 2359300
  2.3 19.3 %collective-permute-start.3 = (f32[6,64,256]{2,1,0:T(8,128)S(1)}, f32[6,64,256]{2,1,0:T(8,128)S(1)}, u32[]{:S(2)}, u32[]{:S(2)}) collective-permute-start(f32[6,64,256]{2,1,0:T(8,128)S(1)} %get-tuple-element.41.up), channel_id=1, source_target_pairs={{0,1},{1,2},{2,3},{3,4},{4,5},{5,6},{6,7},{7,8},{8,9},{9,10},{10,1... | collective-permute-start | bytes 1179656 | tf_op jit(solution)/shard_map/ppermute | solution.py:339
  2.9 18.7 %collective-permute-start.4 = (f32[6,64,256]{2,1,0:T(8,128)S(1)}, f32[6,64,256]{2,1,0:T(8,128)S(1)}, u32[]{:S(2)}, u32[]{:S(2)}) collective-permute-start(f32[6,64,256]{2,1,0:T(8,128)S(1)} %get-tuple-element.42.down), channel_id=1, source_target_pairs={{1,0},{2,1},{3,2},{4,3},{5,4},{6,5},{7,6},{8,7},{9,8},{10,9},{11,1... | collective-permute-start | bytes 1179656 | tf_op jit(solution)/shard_map/ppermute | solution.py:339
  3.6 6.9 %collective-permute-start = (f32[64,256]{1,0:T(8,128)S(1)}, f32[64,256]{1,0:T(8,128)S(1)}, u32[]{:S(2)}, u32[]{:S(2)}) collective-permute-start(f32[64,256]{1,0:T(8,128)S(1)} %get-tuple-element.38), channel_id=1, source_target_pairs={{16,17},{17,18},{18,19},{19,20},{20,21},{21,22},{22,23},{23,24},{2... | collective-permute-start | bytes 196616 | tf_op jit(solution)/shard_map/ppermute | solution.py:339
  6.8 8.4 %collective-permute-start.1 = (f32[64,256]{1,0:T(8,128)S(1)}, f32[64,256]{1,0:T(8,128)S(1)}, u32[]{:S(2)}, u32[]{:S(2)}) collective-permute-start(f32[64,256]{1,0:T(8,128)S(1)} %get-tuple-element.39), channel_id=1, source_target_pairs={{17,16},{18,17},{19,18},{20,19},{21,20},{22,21},{23,22},{24,23},{2... | collective-permute-start | bytes 196616 | tf_op jit(solution)/shard_map/ppermute | solution.py:339
  15.3 6.3 %collective-permute-start.2 = (f32[4,64,256]{2,1,0:T(8,128)S(1)}, f32[4,64,256]{2,1,0:T(8,128)S(1)}, u32[]{:S(2)}, u32[]{:S(2)}) collective-permute-start(f32[4,64,256]{2,1,0:T(8,128)S(1)} %get-tuple-element.43.refs_0_.edges), channel_id=1, source_target_pairs={{0,16},{16,0},{1,17},{17,1},{2,18},{18,2},{3,19},{19,3},{4,20},{20... | collective-permute-start | bytes 786440 | tf_op jit(solution)/shard_map/ppermute | solution.py:387
  15.4 9.4 %collective-permute-start.7 = (f32[6,64,256]{2,1,0:T(8,128)S(1)}, f32[6,64,256]{2,1,0:T(8,128)S(1)}, u32[]{:S(2)}, u32[]{:S(2)}) collective-permute-start(f32[6,64,256]{2,1,0:T(8,128)S(1)} %get-tuple-element.53), channel_id=1, source_target_pairs={{16,17},{17,18},{18,19},{19,20},{20,21},{21,22},{22,23},{23,24},{2... | collective-permute-start | bytes 1179656 | tf_op jit(solution)/shard_map/ppermute | solution.py:339
  17.9 10.7 %collective-permute-start.8 = (f32[6,64,256]{2,1,0:T(8,128)S(1)}, f32[6,64,256]{2,1,0:T(8,128)S(1)}, u32[]{:S(2)}, u32[]{:S(2)}) collective-permute-start(f32[6,64,256]{2,1,0:T(8,128)S(1)} %get-tuple-element.54), channel_id=1, source_target_pairs={{17,16},{18,17},{19,18},{20,19},{21,20},{22,21},{23,22},{24,23},{2... | collective-permute-start | bytes 1179656 | tf_op jit(solution)/shard_map/ppermute | solution.py:339
  21.6 9.3 %collective-permute-start.5 = (f32[6,64,256]{2,1,0:T(8,128)S(1)}, f32[6,64,256]{2,1,0:T(8,128)S(1)}, u32[]{:S(2)}, u32[]{:S(2)}) collective-permute-start(f32[6,64,256]{2,1,0:T(8,128)S(1)} %get-tuple-element.51), channel_id=1, source_target_pairs={{0,1},{1,2},{2,3},{3,4},{4,5},{5,6},{6,7},{7,8},{8,9},{9,10},{10,1... | collective-permute-start | bytes 1179656 | tf_op jit(solution)/shard_map/ppermute | solution.py:339
  22.3 8.7 %collective-permute-start.6 = (f32[6,64,256]{2,1,0:T(8,128)S(1)}, f32[6,64,256]{2,1,0:T(8,128)S(1)}, u32[]{:S(2)}, u32[]{:S(2)}) collective-permute-start(f32[6,64,256]{2,1,0:T(8,128)S(1)} %get-tuple-element.52), channel_id=1, source_target_pairs={{1,0},{2,1},{3,2},{4,3},{5,4},{6,5},{7,6},{8,7},{9,8},{10,9},{11,1... | collective-permute-start | bytes 1179656 | tf_op jit(solution)/shard_map/ppermute | solution.py:339
  31.0 9.9 %collective-permute-start.9 = (f32[6,2,64,256]{3,2,1,0:T(8,128)S(1)}, f32[6,2,64,256]{3,2,1,0:T(8,128)S(1)}, u32[]{:S(2)}, u32[]{:S(2)}) collective-permute-start(f32[6,2,64,256]{3,2,1,0:T(8,128)S(1)} %shard_map.77.before_end), channel_id=1, source_target_pairs={{0,16},{1,17},{2,18},{3,19},{4,20},{5,21},{6,22},{7,23},{8,24},{9,... | collective-permute-start | bytes 2359304 | tf_op jit(solution)/shard_map/ppermute | solution.py:413
  32.3 16.1 %collective-permute-start.12 = (f32[6,64,256]{2,1,0:T(8,128)S(1)}, f32[6,64,256]{2,1,0:T(8,128)S(1)}, u32[]{:S(2)}, u32[]{:S(2)}) collective-permute-start(f32[6,64,256]{2,1,0:T(8,128)S(1)} %get-tuple-element.67), channel_id=1, source_target_pairs={{16,17},{17,18},{18,19},{19,20},{20,21},{21,22},{22,23},{23,24},{2... | collective-permute-start | bytes 1179656 | tf_op jit(solution)/shard_map/ppermute | solution.py:339
  34.3 14.2 %collective-permute-start.13 = (f32[6,64,256]{2,1,0:T(8,128)S(1)}, f32[6,64,256]{2,1,0:T(8,128)S(1)}, u32[]{:S(2)}, u32[]{:S(2)}) collective-permute-start(f32[6,64,256]{2,1,0:T(8,128)S(1)} %get-tuple-element.68), channel_id=1, source_target_pairs={{17,16},{18,17},{19,18},{20,19},{21,20},{22,21},{23,22},{24,23},{2... | collective-permute-start | bytes 1179656 | tf_op jit(solution)/shard_map/ppermute | solution.py:339
  41.8 9.9 %collective-permute-start.10 = (f32[6,64,256]{2,1,0:T(8,128)S(1)}, f32[6,64,256]{2,1,0:T(8,128)S(1)}, u32[]{:S(2)}, u32[]{:S(2)}) collective-permute-start(f32[6,64,256]{2,1,0:T(8,128)S(1)} %get-tuple-element.63), channel_id=1, source_target_pairs={{16,17},{17,18},{18,19},{19,20},{20,21},{21,22},{22,23},{23,24},{2... | collective-permute-start | bytes 1179656 | tf_op jit(solution)/shard_map/ppermute | solution.py:339
  45.0 12.2 %collective-permute-start.11 = (f32[6,64,256]{2,1,0:T(8,128)S(1)}, f32[6,64,256]{2,1,0:T(8,128)S(1)}, u32[]{:S(2)}, u32[]{:S(2)}) collective-permute-start(f32[6,64,256]{2,1,0:T(8,128)S(1)} %get-tuple-element.64), channel_id=1, source_target_pairs={{17,16},{18,17},{19,18},{20,19},{21,20},{22,21},{23,22},{24,23},{2... | collective-permute-start | bytes 1179656 | tf_op jit(solution)/shard_map/ppermute | solution.py:339
